TPU v7x, 32 devices: a whole 2x2x4 slice. The times are simulated.
32 devices in a mesh: height: 4 (over z), chan: 4 (over x, core), dp: 2 (over y).
Axes of the slice: x: 2, y: 2, z: 4, core: 2. Of those that a mesh axis runs over, the one named last changes fastest.
Arguments:
- inputs: bfloat16 [96, 8, 7, 2048], P('dp', 'height'), may hold values from -9 to 9, as said below
- cotangent: bfloat16 [96, 8, 7, 2048], P('dp', 'height', None, 'chan'), may hold values from -6 to 6
- reduce_master: float32 [2048, 1024], P(('height', 'dp'), 'chan'), may hold values from -0.125 to 0.125
- reduce_first: float32 [2048, 1024], P(('height', 'dp'), 'chan'), may hold values from -274.34286 to 274.34286
- reduce_second: float32 [2048, 1024], P(('height', 'dp'), 'chan'), may hold values from 2352 to 18816
- reduce_average: float32 [2048, 1024], P(('height', 'dp'), 'chan'), may hold values from -0.125 to 0.125
- group_master: float32 [288, 1024], P(('height', 'dp'), 'chan'), may hold values from -0.375 to 0.375
- group_first: float32 [288, 1024], P(('height', 'dp'), 'chan'), may hold values from -137.17143 to 137.17143
- group_second: float32 [288, 1024], P(('height', 'dp'), 'chan'), may hold values from 588 to 4704
- group_average: float32 [288, 1024], P(('height', 'dp'), 'chan'), may hold values from -0.375 to 0.375
- expand_master: float32 [1024, 2048], P('chan', ('height', 'dp')), may hold values from -0.1875 to 0.1875
- expand_first: float32 [1024, 2048], P('chan', ('height', 'dp')), may hold values from -137.17143 to 137.17143
- expand_second: float32 [1024, 2048], P('chan', ('height', 'dp')), may hold values from 588 to 4704
- expand_average: float32 [1024, 2048], P('chan', ('height', 'dp')), may hold values from -0.1875 to 0.1875
- inner_master: float32 [4, 1024], P(None, 'chan'), may hold values from -0.9 to 1.5, as said below
- inner_first: float32 [4, 1024], P(None, 'chan'), may hold values from -274.34286 to 274.34286
- inner_second: float32 [4, 1024], P(None, 'chan'), may hold values from 2352 to 18816
- inner_average: float32 [4, 1024], P(None, 'chan'), may hold values from -0.9 to 1.5, as said below
- outer_master: float32 [2, 2048], P(None, 'chan'), may hold values from -0.9 to 1.5, as said below
- outer_first: float32 [2, 2048], P(None, 'chan'), may hold values from -274.34286 to 274.34286
- outer_second: float32 [2, 2048], P(None, 'chan'), may hold values from 2352 to 18816
- outer_average: float32 [2, 2048], P(None, 'chan'), may hold values from -0.9 to 1.5, as said below
Outputs:
- block_out: bfloat16 [96, 8, 7, 2048], P('dp', 'height', None, 'chan')
- input_grad: float32 [96, 8, 7, 2048], P('dp', 'height', None, 'chan')
- reduce_grad: float32 [2048, 1024], P(('height', 'dp'), 'chan')
- reduce_first_new: float32 [2048, 1024], P(('height', 'dp'), 'chan')
- reduce_second_new: float32 [2048, 1024], P(('height', 'dp'), 'chan')
- reduce_master_new: float32 [2048, 1024], P(('height', 'dp'), 'chan')
- reduce_copy: bfloat16 [2048, 1024], P(('height', 'dp'), 'chan')
- reduce_average_new: float32 [2048, 1024], P(('height', 'dp'), 'chan')
- group_grad: float32 [288, 1024], P(('height', 'dp'), 'chan')
- group_first_new: float32 [288, 1024], P(('height', 'dp'), 'chan')
- group_second_new: float32 [288, 1024], P(('height', 'dp'), 'chan')
- group_master_new: float32 [288, 1024], P(('height', 'dp'), 'chan')
- group_copy: bfloat16 [288, 1024], P(('height', 'dp'), 'chan')
- group_average_new: float32 [288, 1024], P(('height', 'dp'), 'chan')
- expand_grad: float32 [1024, 2048], P('chan', ('height', 'dp'))
- expand_first_new: float32 [1024, 2048], P('chan', ('height', 'dp'))
- expand_second_new: float32 [1024, 2048], P('chan', ('height', 'dp'))
- expand_master_new: float32 [1024, 2048], P('chan', ('height', 'dp'))
- expand_copy: bfloat16 [1024, 2048], P('chan', ('height', 'dp'))
- expand_average_new: float32 [1024, 2048], P('chan', ('height', 'dp'))
- inner_grad: float32 [4, 1024], P(None, 'chan')
- inner_first_new: float32 [4, 1024], P(None, 'chan')
- inner_second_new: float32 [4, 1024], P(None, 'chan')
- inner_master_new: float32 [4, 1024], P(None, 'chan')
- inner_average_new: float32 [4, 1024], P(None, 'chan')
- outer_grad: float32 [2, 2048], P(None, 'chan')
- outer_first_new: float32 [2, 2048], P(None, 'chan')
- outer_second_new: float32 [2, 2048], P(None, 'chan')
- outer_master_new: float32 [2, 2048], P(None, 'chan')
- outer_average_new: float32 [2, 2048], P(None, 'chan')
Inputs may be any that keep to these rules, and one draw needn't show every extreme that they name: `inputs`: row 7 of every image is zero. `inner_master`: rows 0 and 2 are gains, rows 1 and 3 shifts. `inner_average`: rows 0 and 2 are averaged gains, rows 1 and 3 shifts. `outer_master`: row 0 is the gain, row 1 the shift. `outer_average`: row 0 is the averaged gain, row 1 the shift.
All inputs are finite; a program needn't handle non-finite values.
Results may differ from a plain program's by a relative error of at most 0.02.
Values may be sent and summed in bfloat16 or wider, within the bound.
A program may use at most 128 MiB of HBM per device.

v0:
```python
import jax
import jax.numpy as jnp
from jax import lax
from jax.sharding import PartitionSpec as P

GROUP = 32
HEIGHT = 7
WIDTH = 7
STEP = 10


NORM_EPS = 1e-05
CONV_RATE = 0.02
NORM_RATE = 0.3


def with_halo(block, sides, width):
    for axis, dim in sides:
        count = lax.axis_size(axis)
        forward = [(i, i + 1) for i in range(count - 1)]
        backward = [(target, source) for source, target in forward]
        low = lax.ppermute(
            lax.slice_in_dim(block, block.shape[dim] - width, None, axis=dim), axis, forward
        )
        high = lax.ppermute(lax.slice_in_dim(block, 0, width, axis=dim), axis, backward)
        block = jnp.concatenate([low, block, high], axis=dim)
    return block


def silu_slope(values):
    sigmoid = jax.nn.sigmoid(values)
    return sigmoid * (1.0 + values * (1.0 - sigmoid))


def moments(values, valid_rows):
    return (
        jnp.sum(values * valid_rows, axis=(0, 1, 2)),
        jnp.sum(values * values * valid_rows, axis=(0, 1, 2)),
    )


def normalize(values, totals, squares, pixels):
    average = totals / pixels
    inverse = lax.rsqrt(squares / pixels - average * average + NORM_EPS)
    return ((values - average) * inverse, inverse)


def norm_back(upstream, normed, inverse, gain, shift_sum, gain_sum, pixels, valid_rows):
    return (
        gain * inverse * (upstream - shift_sum / pixels - normed * gain_sum / pixels) * valid_rows
    )


def window_taps(padded, height_out, width_out, groups):
    batch_size = padded.shape[0]
    pieces = [
        padded[:, tap_row : tap_row + height_out, tap_col : tap_col + width_out, :]
        for tap_row in range(3)
        for tap_col in range(3)
    ]
    stacked = jnp.stack(pieces, axis=3).reshape(batch_size, height_out, width_out, 9, groups, -1)
    return jnp.transpose(stacked, (0, 1, 2, 4, 3, 5)).reshape(
        batch_size, height_out, width_out, groups, -1
    )


def pad_columns(values):
    return jnp.pad(values, ((0, 0), (0, 0), (1, 1), (0, 0)))


def adamw_step(master, gradient, moment_one, moment_two, average, rate):
    first_new = 0.5 * moment_one + 0.5 * gradient
    second_new = 0.5 * moment_two + 0.5 * gradient * gradient
    correct = 1.0 - 0.5**STEP
    direction = first_new / correct / (jnp.sqrt(second_new / correct) + 1e-08)
    master_new = master - rate * (direction + 0.05 * master)
    average_new = 0.75 * average + 0.25 * master_new
    return (first_new, second_new, master_new, average_new)


def local(
    inputs,
    cotangent,
    reduce_master,
    reduce_first,
    reduce_second,
    reduce_average,
    group_master,
    group_first,
    group_second,
    group_average,
    expand_master,
    expand_first,
    expand_second,
    expand_average,
    inner_master,
    inner_first,
    inner_second,
    inner_average,
    outer_master,
    outer_first,
    outer_second,
    outer_average,
):
    batch_size = inputs.shape[0]
    local_rows = inputs.shape[1]
    local_cols = inputs.shape[2]
    pixels = batch_size * lax.axis_size("dp") * HEIGHT * WIDTH * 1.0
    row_number = lax.axis_index("height") * local_rows + jnp.arange(local_rows)
    valid_rows = (row_number < HEIGHT).astype(jnp.float32)[None, :, None, None]
    w_reduce, w_group, w_expand = (
        lax.all_gather(reduce_master.astype(jnp.bfloat16), ("height", "dp"), axis=0, tiled=True),
        lax.all_gather(group_master.astype(jnp.bfloat16), ("height", "dp"), axis=0, tiled=True),
        lax.all_gather(expand_master.astype(jnp.bfloat16), ("height", "dp"), axis=1, tiled=True),
    )
    local_mid = w_reduce.shape[1]
    local_out = outer_master.shape[1]
    groups = local_mid // GROUP
    first = jnp.einsum("nhwc,cd->nhwd", inputs, w_reduce, preferred_element_type=jnp.float32)
    sum_one, square_one = moments(first, valid_rows)
    sum_one, square_one = lax.psum((sum_one, square_one), ("height", "dp"))
    normed_one, inverse_one = normalize(first, sum_one, square_one, pixels)
    z_one = normed_one * inner_master[0] + inner_master[1]
    act_one = (jax.nn.silu(z_one) * valid_rows).astype(jnp.bfloat16)
    padded_one = pad_columns(with_halo(act_one, (("height", 1),), 1))
    taps_one = window_taps(padded_one, local_rows, local_cols, groups)
    kernel = w_group.reshape(9 * GROUP, groups, GROUP)
    second = jnp.einsum(
        "nhwgk,kgo->nhwgo", taps_one, kernel, preferred_element_type=jnp.float32
    ).reshape(batch_size, local_rows, local_cols, local_mid)
    sum_two, square_two = moments(second, valid_rows)
    sum_two, square_two = lax.psum((sum_two, square_two), ("height", "dp"))
    normed_two, inverse_two = normalize(second, sum_two, square_two, pixels)
    z_two = normed_two * inner_master[2] + inner_master[3]
    act_two = (jax.nn.silu(z_two) * valid_rows).astype(jnp.bfloat16)
    partial_out = jnp.einsum("nhwd,dc->nhwc", act_two, w_expand, preferred_element_type=jnp.float32)
    third = lax.psum_scatter(partial_out, "chan", scatter_dimension=3, tiled=True)
    sum_three, square_three = moments(third, valid_rows)
    sum_three, square_three = lax.psum((sum_three, square_three), ("height", "dp"))
    normed_three, inverse_three = normalize(third, sum_three, square_three, pixels)
    chan_start = lax.axis_index("chan") * local_out
    residual = lax.dynamic_slice_in_dim(inputs, chan_start, local_out, 3).astype(jnp.float32)
    pre = normed_three * outer_master[0] + outer_master[1] + residual
    block_out = (jax.nn.silu(pre) * valid_rows).astype(jnp.bfloat16)
    d_pre = cotangent.astype(jnp.float32) * valid_rows * silu_slope(pre)
    shift_three, gain_three = lax.psum(
        (
            jnp.sum(d_pre * valid_rows, axis=(0, 1, 2)),
            jnp.sum(d_pre * normed_three * valid_rows, axis=(0, 1, 2)),
        ),
        ("height", "dp"),
    )
    back_three = norm_back(
        d_pre,
        normed_three,
        inverse_three,
        outer_master[0],
        shift_three,
        gain_three,
        pixels,
        valid_rows,
    ).astype(jnp.bfloat16)
    piece = lax.all_gather(back_three, "chan", axis=3, tiled=True)
    act_grad = jnp.einsum("nhwc,dc->nhwd", piece, w_expand, preferred_element_type=jnp.float32)
    block = jnp.einsum("nhwd,nhwc->dc", act_two, piece, preferred_element_type=jnp.float32)
    dz_two = act_grad * silu_slope(z_two) * valid_rows
    shift_two, gain_two = lax.psum(
        (
            jnp.sum(dz_two * valid_rows, axis=(0, 1, 2)),
            jnp.sum(dz_two * normed_two * valid_rows, axis=(0, 1, 2)),
        ),
        ("height", "dp"),
    )
    back_two = norm_back(
        dz_two, normed_two, inverse_two, inner_master[2], shift_two, gain_two, pixels, valid_rows
    ).astype(jnp.bfloat16)
    padded_two = pad_columns(with_halo(back_two, (("height", 1),), 1))
    taps_two = window_taps(padded_two, local_rows, local_cols, groups)
    flipped = jnp.transpose(w_group.reshape(9, GROUP, groups, GROUP)[::-1], (0, 3, 2, 1)).reshape(
        9 * GROUP, groups, GROUP
    )
    back_act_one = jnp.einsum(
        "nhwgk,kgj->nhwgj", taps_two, flipped, preferred_element_type=jnp.float32
    ).reshape(batch_size, local_rows, local_cols, local_mid)
    group_local = jnp.einsum(
        "nhwgk,nhwgo->kgo",
        taps_one,
        back_two.reshape(batch_size, local_rows, local_cols, groups, GROUP),
        preferred_element_type=jnp.float32,
    ).reshape(9 * GROUP, local_mid)
    dz_one = back_act_one * silu_slope(z_one) * valid_rows
    shift_one, gain_one = lax.psum(
        (
            jnp.sum(dz_one * valid_rows, axis=(0, 1, 2)),
            jnp.sum(dz_one * normed_one * valid_rows, axis=(0, 1, 2)),
        ),
        ("height", "dp"),
    )
    back_one = norm_back(
        dz_one, normed_one, inverse_one, inner_master[0], shift_one, gain_one, pixels, valid_rows
    ).astype(jnp.bfloat16)
    reduce_local = jnp.einsum("nhwc,nhwd->cd", inputs, back_one, preferred_element_type=jnp.float32)
    input_part = jnp.einsum("nhwd,cd->nhwc", back_one, w_reduce, preferred_element_type=jnp.float32)
    input_grad = (
        lax.psum_scatter(
            input_part.astype(jnp.bfloat16), "chan", scatter_dimension=3, tiled=True
        ).astype(jnp.float32)
        + d_pre
    )
    reduce_total, group_total, expand_total = (
        lax.psum(reduce_local.astype(jnp.bfloat16), ("height", "dp")).astype(jnp.float32),
        lax.psum(group_local.astype(jnp.bfloat16), ("height", "dp")).astype(jnp.float32),
        lax.psum(block.astype(jnp.bfloat16), ("height", "dp")).astype(jnp.float32),
    )
    owner = lax.axis_index(("height", "dp"))
    reduce_grad = lax.dynamic_slice_in_dim(
        reduce_total, owner * reduce_master.shape[0], reduce_master.shape[0], 0
    )
    group_grad = lax.dynamic_slice_in_dim(
        group_total, owner * group_master.shape[0], group_master.shape[0], 0
    )
    expand_grad = lax.dynamic_slice_in_dim(
        expand_total, owner * expand_master.shape[1], expand_master.shape[1], 1
    )
    inner_grad = jnp.stack([gain_one, shift_one, gain_two, shift_two])
    outer_grad = jnp.stack([gain_three, shift_three])
    red = adamw_step(
        reduce_master, reduce_grad, reduce_first, reduce_second, reduce_average, CONV_RATE
    )
    grp = adamw_step(group_master, group_grad, group_first, group_second, group_average, CONV_RATE)
    exp_new = adamw_step(
        expand_master, expand_grad, expand_first, expand_second, expand_average, CONV_RATE
    )
    inn = adamw_step(inner_master, inner_grad, inner_first, inner_second, inner_average, NORM_RATE)
    out_new = adamw_step(
        outer_master, outer_grad, outer_first, outer_second, outer_average, NORM_RATE
    )
    return (
        block_out,
        input_grad,
        reduce_grad,
        red[0],
        red[1],
        red[2],
        red[2].astype(jnp.bfloat16),
        red[3],
        group_grad,
        grp[0],
        grp[1],
        grp[2],
        grp[2].astype(jnp.bfloat16),
        grp[3],
        expand_grad,
        exp_new[0],
        exp_new[1],
        exp_new[2],
        exp_new[2].astype(jnp.bfloat16),
        exp_new[3],
        inner_grad,
        inn[0],
        inn[1],
        inn[2],
        inn[3],
        outer_grad,
        out_new[0],
        out_new[1],
        out_new[2],
        out_new[3],
    )


def solution(mesh):
    placed = (
        P("dp", "height", None, None),
        P("dp", "height", None, "chan"),
        P(("height", "dp"), "chan"),
        P(("height", "dp"), "chan"),
        P(("height", "dp"), "chan"),
        P(("height", "dp"), "chan"),
        P(("height", "dp"), "chan"),
        P(("height", "dp"), "chan"),
        P(("height", "dp"), "chan"),
        P(("height", "dp"), "chan"),
        P("chan", ("height", "dp")),
        P("chan", ("height", "dp")),
        P("chan", ("height", "dp")),
        P("chan", ("height", "dp")),
        P(None, "chan"),
        P(None, "chan"),
        P(None, "chan"),
        P(None, "chan"),
        P(None, "chan"),
        P(None, "chan"),
        P(None, "chan"),
        P(None, "chan"),
    )
    return jax.shard_map(
        local,
        mesh=mesh,
        in_specs=placed,
        out_specs=(
            P("dp", "height", None, "chan"),
            P("dp", "height", None, "chan"),
            P(("height", "dp"), "chan"),
            P(("height", "dp"), "chan"),
            P(("height", "dp"), "chan"),
            P(("height", "dp"), "chan"),
            P(("height", "dp"), "chan"),
            P(("height", "dp"), "chan"),
            P(("height", "dp"), "chan"),
            P(("height", "dp"), "chan"),
            P(("height", "dp"), "chan"),
            P(("height", "dp"), "chan"),
            P(("height", "dp"), "chan"),
            P(("height", "dp"), "chan"),
            P("chan", ("height", "dp")),
            P("chan", ("height", "dp")),
            P("chan", ("height", "dp")),
            P("chan", ("height", "dp")),
            P("chan", ("height", "dp")),
            P("chan", ("height", "dp")),
            P(None, "chan"),
            P(None, "chan"),
            P(None, "chan"),
            P(None, "chan"),
            P(None, "chan"),
            P(None, "chan"),
            P(None, "chan"),
            P(None, "chan"),
            P(None, "chan"),
            P(None, "chan"),
        ),
        check_vma=False,
    )
```

profile of v0, /device:TPU:2, one launch (start us, length us, event | category | flops | bytes accessed | tf_op | source)
XLA Modules:
  0.0 599.8 jit_solution(2615158743272444486)
XLA Ops:
  12.1 40.1 %all-gather.5.cloned.1.call-done = bf16[2048,256]{1,0:T(8,128)(2,1)} async-done(((bf16[256,256]{1,0:T(8,128)(2,1)}), bf16[2048,256]{1,0:T(8,128)(2,1)}) %all-gather.5.cloned.1.call-update) | async-done | bytes 1048592 | tf_op jit(solution)/shard_map/all_gather | solution.py:112
  52.1 3.7 multiply_reduce_fusion.11
  55.9 19.5 %all-reduce.7 = (f32[256]{0:T(256)S(1)}, f32[256]{0:T(256)S(1)}) all-reduce(f32[256]{0:T(256)S(1)} %get-tuple-element.131, f32[256]{0:T(256)S(1)} %get-tuple-element.130), channel_id=1, replica_groups=mesh['height'=4,'chan'=4,'dp'=2] {'height','dp'}, use_global_device_ids=true, to_apply=%region_3.0 | all-reduce | flops 512 | bytes 4096 | tf_op jit(solution)/shard_map/psum | solution.py:121
  78.3 4.6 collective-permute-start
  82.9 30.9 %all-gather = bf16[8,36,256]{2,1,0:T(8,128)(2,1)S(1)} all-gather(bf16[1,36,256]{2,1,0:T(8,128)(2,1)S(1)} %convert_bitcast_fusion), channel_id=1, replica_groups=mesh['height'=4,'chan'=4,'dp'=2] {'height','dp'}, dimensions={0}, use_global_device_ids=true | all-gather | bytes 165888 | tf_op jit(solution)/shard_map/all_gather | solution.py:113
  127.4 2.7 stack.87
  136.7 2.7 constant_dynamic-update-slice_fusion.6
  149.2 15.0 %copy.190 = bf16[48,2,7,8,9,32]{0,5,4,2,1,3:T(8,128)(2,1)} copy(bf16[48,2,7,8,9,32]{5,3,0,2,1,4:T(8,128)(2,1)} %bitcast.166) | data formatting | bytes 6193152 | tf_op jit(solution)/shard_map/reshape | solution.py:62
  164.2 6.1 %multiply_reduce_fusion.1 = (f32[8,32]{1,0:T(8,128)S(1)}, f32[8,32]{1,0:T(8,128)S(1)}, f32[48,2,7,8,32]{0,4,2,1,3:T(8,128)}) fusion(f32[2]{0:T(128)S(1)} %copy-done.37, bf16[48,2,7,8,288]{0,4,2,1,3:T(8,128)(2,1)} %bitcast.162, bf16[288,8,32,1,1]{2,1,0,4,3:T(8,128)(2,1)S(1)} %bitcast.168), kind=kOutput, calls=%fused_computation.9 | convolution fusion | flops 99950080 | bytes 3934216 | tf_op jit(solution)/shard_map/nhwgk,kgo->nhwgo/dot_general | solution.py:128
  173.5 19.7 %all-reduce.6 = (f32[256]{0:T(256)S(1)}, f32[256]{0:T(256)S(1)}) all-reduce(f32[256]{0:T(256)S(1)} %reduce_sum.117, f32[256]{0:T(256)S(1)} %reduce_sum.115), channel_id=1, replica_groups=mesh['height'=4,'chan'=4,'dp'=2] {'height','dp'}, use_global_device_ids=true, to_apply=%region_7.8 | all-reduce | flops 512 | bytes 4096 | tf_op jit(solution)/shard_map/psum | solution.py:132
  193.3 4.6 fusion.17
  199.7 2.7 copy.130
  202.4 44.9 %reduce-scatter.3.cloned.1.call-done = f32[48,2,7,512]{3,0,2,1:T(8,128)} async-done(((f32[48,2,7,2048]{3,0,2,1:T(8,128)}), f32[48,2,7,512]{3,0,2,1:T(8,128)}) %reduce-scatter.3.cloned.1.call-update) | async-done | bytes 1376272 | tf_op jit(solution)/shard_map/reduce_scatter | solution.py:137
  249.1 21.6 %all-reduce.5 = (f32[512]{0:T(512)S(1)}, f32[512]{0:T(512)S(1)}) all-reduce(f32[512]{0:T(512)S(1)} %get-tuple-element.125, f32[512]{0:T(512)S(1)} %get-tuple-element.124), channel_id=1, replica_groups=mesh['height'=4,'chan'=4,'dp'=2] {'height','dp'}, use_global_device_ids=true, to_apply=%region_12.13 | all-reduce | flops 1024 | bytes 8192 | tf_op jit(solution)/shard_map/psum | solution.py:139
  270.7 3.3 multiply_reduce_fusion.3
  274.0 17.1 %all-reduce.4 = (f32[512]{0:T(512)S(1)}, f32[512]{0:T(512)S(1)}) all-reduce(f32[512]{0:T(512)S(1)} %get-tuple-element.123, f32[512]{0:T(512)S(1)} %get-tuple-element.122), channel_id=1, replica_groups=mesh['height'=4,'chan'=4,'dp'=2] {'height','dp'}, use_global_device_ids=true, to_apply=%region_16.17 | all-reduce | flops 1024 | bytes 8192 | tf_op jit(solution)/shard_map/psum | solution.py:146
  295.1 21.3 %all-gather.9.cloned.1.call-done = bf16[48,2,7,2048]{3,0,2,1:T(8,128)(2,1)} async-done(((bf16[48,2,7,512]{3,0,2,1:T(8,128)(2,1)}), bf16[48,2,7,2048]{3,0,2,1:T(8,128)(2,1)}) %all-gather.9.cloned.1.call-update) | async-done | bytes 2752528 | tf_op jit(solution)/shard_map/all_gather | solution.py:163
  316.4 3.2 multiply_reduce_fusion.9
  319.6 21.7 %all-reduce.3 = (f32[256]{0:T(256)S(1)}, f32[256]{0:T(256)S(1)}) all-reduce(f32[256]{0:T(256)S(1)} %get-tuple-element.129, f32[256]{0:T(256)S(1)} %get-tuple-element.128), channel_id=1, replica_groups=mesh['height'=4,'chan'=4,'dp'=2] {'height','dp'}, use_global_device_ids=true, to_apply=%region_20.21 | all-reduce | flops 512 | bytes 4096 | tf_op jit(solution)/shard_map/psum | solution.py:167
  345.2 5.5 collective-permute-start.2
  350.7 6.8 %fusion.10 = bf16[8,32,288]{2,1,0:T(8,128)(2,1)} fusion(bf16[48,2,7,8,288]{0,4,2,1,3:T(8,128)(2,1)} %bitcast.163, bf16[48,2,7,8,32]{4,3,0,2,1:T(8,128)(2,1)} %reshape.160), kind=kOutput, calls=%fused_computation.29 | convolution fusion | flops 99164160 | bytes 3588096 | tf_op jit(solution)/shard_map/nhwgk,nhwgo->kgo/dot_general | solution.py:185
  369.9 3.0 stack.95
  372.9 2.7 stack.96
  375.6 2.6 stack.97
  379.9 2.7 stack.100
  385.9 2.7 constant_dynamic-update-slice_fusion.16
  400.3 15.1 %copy.191 = bf16[48,2,7,8,9,32]{0,5,4,2,1,3:T(8,128)(2,1)} copy(bf16[48,2,7,8,9,32]{5,3,0,2,1,4:T(8,128)(2,1)} %bitcast.165) | data formatting | bytes 6193152 | tf_op jit(solution)/shard_map/reshape | solution.py:62
  415.4 5.1 convolution_bitcast_fusion.2
  425.5 17.1 %all-reduce.2 = (f32[256]{0:T(256)S(1)}, f32[256]{0:T(256)S(1)}) all-reduce(f32[256]{0:T(256)S(1)} %get-tuple-element.127, f32[256]{0:T(256)S(1)} %get-tuple-element.126), channel_id=1, replica_groups=mesh['height'=4,'chan'=4,'dp'=2] {'height','dp'}, use_global_device_ids=true, to_apply=%region_24.25 | all-reduce | flops 512 | bytes 4096 | tf_op jit(solution)/shard_map/psum | solution.py:192
  442.9 4.7 fusion.2
  462.3 91.3 %all-reduce.11.cloned.1.call-done = (bf16[2048,256]{0,1:T(8,128)(2,1)}, bf16[288,256]{1,0:T(8,128)(2,1)}, bf16[256,2048]{0,1:T(8,128)(2,1)}) async-done(((bf16[2048,256]{0,1:T(8,128)(2,1)}, bf16[288,256]{1,0:T(8,128)(2,1)}, bf16[256,2048]{0,1:T(8,128)(2,1)}), (bf16[2048,256]{0,1:T(8,128)(2,1)}, bf16[288,256]{1,0:T(8,128)(2,1)}, bf16[256,2048]{0,1:T(8,128)(2,1)})) %all-reduce.11.cloned.1.call-update) | async-done | bytes 2244624 | tf_op jit(solution)/shard_map/psum | solution.py:211
  572.3 17.0 %reduce-scatter.5.cloned.1.call-done = bf16[48,2,7,512]{3,0,2,1:T(8,128)(2,1)} async-done(((bf16[48,2,7,2048]{3,0,2,1:T(8,128)(2,1)}), bf16[48,2,7,512]{3,0,2,1:T(8,128)(2,1)}) %reduce-scatter.5.cloned.1.call-update) | async-done | bytes 688144 | tf_op jit(solution)/shard_map/reduce_scatter | solution.py:205
  (236 shorter events, 123.2 us)
Async XLA Ops:
  7.2 44.9 %all-gather.5.cloned.1.call-start = ((), (), s32[]{:S(2)}) async-start(), calls=%async_computation.2 | async-start | bytes 1179648 | tf_op jit(solution)/shard_map/all_gather | solution.py:112
  8.9 184.3 %all-gather.7.cloned.1.call-start = ((), (), s32[]{:S(2)}) async-start(), calls=%async_computation.3 | async-start | bytes 1179648 | tf_op jit(solution)/shard_map/all_gather | solution.py:114
  10.6 236.7 %reduce-scatter.3.cloned.1.call-start = ((), (), s32[]{:S(2)}) async-start(), calls=%async_computation.4 | async-start | bytes 6881280 | tf_op jit(solution)/shard_map/reduce_scatter | solution.py:137
  10.7 65.3 %copy-start.36 = (f32[2]{0:T(128)}, f32[2]{0:T(128)S(1)}, u32[]{:S(2)}) copy-start(f32[2]{0:T(128)S(1)} %compare_convert_fusion) | copy-start | bytes 28
  12.1 63.9 %copy-start.38 = (f32[1,256]{1,0:T(1,128)}, f32[1,256]{1,0:T(1,128)S(1)}, u32[]{:S(2)}) copy-start(f32[1,256]{1,0:T(1,128)S(1)} %get-tuple-element.197) | copy-start | bytes 3076
  12.1 63.9 %copy-start.47 = (f32[1,256]{1,0:T(1,128)}, f32[1,256]{1,0:T(1,128)S(1)}, u32[]{:S(2)}) copy-start(f32[1,256]{1,0:T(1,128)S(1)} %get-tuple-element.196) | copy-start | bytes 3076
  55.9 59.4 %copy-start.1 = (f32[48,2,7,256]{3,0,2,1:T(8,128)}, f32[48,2,7,256]{3,0,2,1:T(8,128)S(1)}, u32[]{:S(2)}) copy-start(f32[48,2,7,256]{3,0,2,1:T(8,128)S(1)} %get-tuple-element.208) | copy-start | bytes 2064388
  55.9 27.0 %copy-start.34 = (f32[36,256]{1,0:T(8,128)S(1)}, f32[36,256]{1,0:T(8,128)}, u32[]{:S(2)}) copy-start(f32[36,256]{1,0:T(8,128)} %param.28) | copy-start | bytes 110596
  76.0 6.8 %copy-start.43 = (f32[256]{0:T(256)}, f32[256]{0:T(256)S(1)}, u32[]{:S(2)}) copy-start(f32[256]{0:T(256)S(1)} %get-tuple-element.202) | copy-start | bytes 3076
  76.0 6.8 %copy-start.45 = (f32[256]{0:T(256)}, f32[256]{0:T(256)S(1)}, u32[]{:S(2)}) copy-start(f32[256]{0:T(256)S(1)} %get-tuple-element.206) | copy-start | bytes 3076
  77.0 38.3 %collective-permute-start.1 = (bf16[48,1,7,256]{3,0,2,1:T(8,128)(2,1)}, bf16[48,1,7,256]{3,0,2,1:T(8,128)(2,1)S(1)}, u32[]{:S(2)}, u32[]{:S(2)}) collective-permute-start(bf16[48,1,7,256]{3,0,2,1:T(8,128)(2,1)} %get-tuple-element.192), channel_id=1, source_target_pairs={{8,0},{16,8},{24,16},{9,1},{17,9},{25,17},{10,2},{18,10},{26,18},{... | collective-permute-start | bytes 516104 | tf_op jit(solution)/shard_map/ppermute | solution.py:25
  78.3 37.1 %collective-permute-start = (bf16[48,1,7,256]{3,0,2,1:T(8,128)(2,1)S(1)}, bf16[48,1,7,256]{3,0,2,1:T(8,128)(2,1)S(1)}, u32[]{:S(2)}, u32[]{:S(2)}) collective-permute-start(bf16[48,1,7,256]{3,0,2,1:T(8,128)(2,1)S(1)} %get-tuple-element.191), channel_id=1, source_target_pairs={{0,8},{8,16},{16,24},{1,9},{9,17},{17,25},{2,10},{10,18},{18,26},{... | collective-permute-start | bytes 516104 | tf_op jit(solution)/shard_map/ppermute | solution.py:22
  149.2 15.0 %copy-start.37 = (f32[2]{0:T(128)S(1)}, f32[2]{0:T(128)}, u32[]{:S(2)}) copy-start(f32[2]{0:T(128)} %copy-done.36) | copy-start | bytes 28
  172.5 20.7 %copy-start.40 = (f32[1,256]{1,0:T(1,128)S(1)}, f32[1,256]{1,0:T(1,128)}, u32[]{:S(2)}) copy-start(f32[1,256]{1,0:T(1,128)} %get-tuple-element.195) | copy-start | bytes 3076
  172.5 20.7 %copy-start.49 = (f32[1,256]{1,0:T(1,128)S(1)}, f32[1,256]{1,0:T(1,128)}, u32[]{:S(2)}) copy-start(f32[1,256]{1,0:T(1,128)} %get-tuple-element.198) | copy-start | bytes 3076
  197.9 118.4 %all-gather.9.cloned.1.call-start = ((), (), s32[]{:S(2)}) async-start(), calls=%async_computation.5 | async-start | bytes 3440640 | tf_op jit(solution)/shard_map/all_gather | solution.py:163
  247.3 23.4 %copy-start = (f32[48,2,7,512]{3,0,2,1:T(8,128)S(1)}, f32[48,2,7,512]{3,0,2,1:T(8,128)}, u32[]{:S(2)}) copy-start(f32[48,2,7,512]{3,0,2,1:T(8,128)} %reduce-scatter.3.cloned.1.call-done) | copy-start | bytes 4128772
  292.4 261.2 %all-reduce.11.cloned.1.call-start = ((), (), s32[]{:S(2)}) async-start(), calls=%async_computation.7 | async-start | bytes 4489216 | tf_op jit(solution)/shard_map/psum | solution.py:211
  343.9 17.7 %collective-permute-start.3 = (bf16[48,1,7,256]{3,0,2,1:T(8,128)(2,1)}, bf16[48,1,7,256]{3,0,2,1:T(8,128)(2,1)}, u32[]{:S(2)}, u32[]{:S(2)}) collective-permute-start(bf16[48,1,7,256]{3,0,2,1:T(8,128)(2,1)} %get-tuple-element.188), channel_id=1, source_target_pairs={{8,0},{16,8},{24,16},{9,1},{17,9},{25,17},{10,2},{18,10},{26,18},{... | collective-permute-start | bytes 516104 | tf_op jit(solution)/shard_map/ppermute | solution.py:25
  345.2 12.3 %copy-start.57 = (bf16[48,2,7,2048]{3,0,2,1:T(8,128)(2,1)S(1)}, bf16[48,2,7,2048]{3,0,2,1:T(8,128)(2,1)}, u32[]{:S(2)}) copy-start(bf16[48,2,7,2048]{3,0,2,1:T(8,128)(2,1)} %all-gather.9.cloned.1.call-done) | copy-start | bytes 8257540
  345.2 16.4 %collective-permute-start.2 = (bf16[48,1,7,256]{3,0,2,1:T(8,128)(2,1)}, bf16[48,1,7,256]{3,0,2,1:T(8,128)(2,1)}, u32[]{:S(2)}, u32[]{:S(2)}) collective-permute-start(bf16[48,1,7,256]{3,0,2,1:T(8,128)(2,1)} %get-tuple-element.187), channel_id=1, source_target_pairs={{0,8},{8,16},{16,24},{1,9},{9,17},{17,25},{2,10},{10,18},{18,26},{... | collective-permute-start | bytes 516104 | tf_op jit(solution)/shard_map/ppermute | solution.py:22
  425.0 17.6 %copy-start.56 = (f32[256]{0:T(256)S(1)}, f32[256]{0:T(256)}, u32[]{:S(2)}) copy-start(f32[256]{0:T(256)} %get-tuple-element.201) | copy-start | bytes 3076
  447.6 141.7 %reduce-scatter.5.cloned.1.call-start = ((), (), s32[]{:S(2)}) async-start(), calls=%async_computation.6 | async-start | bytes 3440640 | tf_op jit(solution)/shard_map/reduce_scatter | solution.py:205
  452.4 7.0 %copy-start.14 = (bf16[48,2,7,512]{3,0,2,1:T(8,128)(2,1)S(1)}, bf16[48,2,7,512]{3,0,2,1:T(8,128)(2,1)}, u32[]{:S(2)}) copy-start(bf16[48,2,7,512]{3,0,2,1:T(8,128)(2,1)} %get-tuple-element.172) | copy-start | bytes 2064388
  454.2 6.7 %copy-start.52 = (f32[2,512]{1,0:T(2,128)S(1)}, f32[2,512]{1,0:T(2,128)}, u32[]{:S(2)}) copy-start(f32[2,512]{1,0:T(2,128)} %param.41) | copy-start | bytes 12292
  454.2 7.4 %copy-start.42 = (f32[4,256]{1,0:T(4,128)S(1)}, f32[4,256]{1,0:T(4,128)}, u32[]{:S(2)}) copy-start(f32[4,256]{1,0:T(4,128)} %param.36) | copy-start | bytes 12292
  454.2 7.4 %copy-start.53 = (f32[4,256]{1,0:T(4,128)S(1)}, f32[4,256]{1,0:T(4,128)}, u32[]{:S(2)}) copy-start(f32[4,256]{1,0:T(4,128)} %param.39) | copy-start | bytes 12292
  454.3 7.3 %copy-start.54 = (f32[4,256]{1,0:T(4,128)S(1)}, f32[4,256]{1,0:T(4,128)}, u32[]{:S(2)}) copy-start(f32[4,256]{1,0:T(4,128)} %param.38) | copy-start | bytes 12292
  454.3 7.3 %copy-start.55 = (f32[4,256]{1,0:T(4,128)S(1)}, f32[4,256]{1,0:T(4,128)}, u32[]{:S(2)}) copy-start(f32[4,256]{1,0:T(4,128)} %param.37) | copy-start | bytes 12292
  558.4 6.8 %copy-start.23 = (f32[256,256]{0,1:T(8,128)S(1)}, f32[256,256]{0,1:T(8,128)}, u32[]{:S(2)}) copy-start(f32[256,256]{0,1:T(8,128)} %get-tuple-element.166) | copy-start | bytes 786436
  561.0 8.1 %copy-start.22 = (f32[256,256]{0,1:T(8,128)S(1)}, f32[256,256]{0,1:T(8,128)}, u32[]{:S(2)}) copy-start(f32[256,256]{0,1:T(8,128)} %get-tuple-element.160) | copy-start | bytes 786436
  567.6 23.0 %copy-start.35 = (f32[36,256]{1,0:T(8,128)}, f32[36,256]{1,0:T(8,128)S(1)}, u32[]{:S(2)}) copy-start(f32[36,256]{1,0:T(8,128)S(1)} %get-tuple-element.162) | copy-start | bytes 110596
  (36 other events, 95.8 us)
Sparse Core Ops, SparseCore 0:
  10.7 41.3 all-gather.4
  54.8 39.3 all-gather.6
  198.0 49.1 reduce-scatter.2
  292.5 23.8 all-gather.8
  447.8 105.7 all-reduce.10
  556.0 33.2 reduce-scatter.4
where the time goes:
time: 608 us; the launch traced here: 600 us
  waiting for transfers between devices  215 us (35%)
  blocking collectives  148 us (24%)
  local copies, waits for them, and re-layouts  145 us (24%)
  matrix products  39.2 us (6%)
  other arithmetic  24.8 us (4%)
  between operations  14.9 us (2%)
  starting transfers between devices  13.2 us (2%)
    psum x1, waiting for transfers between devices, local(): lax.psum(reduce_local.astype(jnp.bfloat16), ('height', 'dp'))  91.3 us
    unnamed x155, local copies, waits for them, and re-layouts  61.7 us
    reduce_scatter x1, waiting for transfers between devices, local(): lax.psum_scatter(partial_out, 'chan', scatter_dimension=3, tiled=True)  44.9 us
    all_gather x1, waiting for transfers between devices, local(): lax.all_gather(reduce_master.astype(jnp.bfloat16), ('height', 'dp'), axis...  40.1 us
    another operation x20, local copies, waits for them, and re-layouts, window_taps(): jnp.stack(pieces, axis=3)  35.3 us
    all_gather x1, blocking collectives, local(): lax.all_gather(group_master.astype(jnp.bfloat16), ('height', 'dp'), axis=...  30.9 us
    reshape x2, local copies, waits for them, and re-layouts, window_taps(): jnp.transpose(stacked, (0, 1, 2, 4, 3, 5))  30.1 us
    psum x1, blocking collectives, local(): lax.psum((jnp.sum(dz_two * valid_rows, axis=(0, 1, 2)), jnp.sum(dz_two *...  21.7 us
  transfers between devices with their start and end apart: 10, of which 5 were waited for; matrix products, arithmetic and copies ran while one was open for 18% of the time, Pallas kernels for 0%

commit v1 on v0

v1 whole, which is shorter than its diff:
```python
import functools

import jax
import jax.numpy as jnp
from jax import lax
from jax.experimental import pallas as pl
from jax.experimental.pallas import tpu as pltpu
from jax.sharding import PartitionSpec as P

GROUP = 32
HEIGHT = 7
STEP = 10
NORM_EPS = 1e-05
CONV_RATE = 0.02
NORM_RATE = 0.3

BF = jnp.bfloat16
F32 = jnp.float32
MESH = pl.DeviceIdType.MESH
SEMAPHORES = 192
SLOT = 48


def dot(a, b):
    return jnp.dot(a, b, preferred_element_type=F32)


def dot_nt(a, b):
    return lax.dot_general(a, b, (((1,), (1,)), ((), ())), preferred_element_type=F32)


def block_kernel(names, dims, *refs):
    r = dict(zip(names, refs, strict=True))
    H, D, N, W, MID, OUT, CIN = (dims[k] for k in ("H", "D", "N", "W", "MID", "OUT", "CIN"))
    own_gather = dims["own_gather"]
    R = W * N
    PITCH = (W + 2) * N
    HD = H * D
    pixels = float(N * D * HEIGHT * W)
    x_ref, ct_ref, inner_ref, outer_ref = r["x"], r["ct"], r["inner"], r["outer"]

    z = lax.axis_index("height")
    c = lax.axis_index("chan")
    y = lax.axis_index("dp")
    xp = lax.div(c, 2)
    k = lax.rem(c, 2)
    cx = lax.rem(c + 2, 4)
    cc = c + 1 - 2 * k
    owner = z * D + y

    def dev(dz=0, chan=None, dy=0):
        return {
            "height": lax.rem(z + dz, H),
            "chan": c if chan is None else chan,
            "dp": lax.rem(y + dy, D),
        }

    offsets = [(dz, dy) for dz in range(H) for dy in range(D)]
    family = [dev(dz, None, dy) for dz, dy in offsets if dz or dy]
    twin_family = [dev(dz, cx, dy) for dz, dy in offsets]
    core_peer = dev(0, cc, 0)
    x_peer = dev(0, cx, 0)

    def rows(h):
        return pl.ds(pl.multiple_of(h * R, 16), R)

    def tile(h, w):
        return pl.ds(pl.multiple_of(h * R + w * N, 16), N)

    def slab(hh, ww, count):
        return pl.ds(pl.multiple_of((hh * (W + 2) + ww) * N, 16), count)

    def quarter(j, core):
        return pl.ds(pl.multiple_of((2 * j + core) * OUT, 128), OUT)

    def valid(h):
        return jnp.where(z * 2 + h < HEIGHT, 1.0, 0.0).astype(F32)

    sends = []
    used = [0]

    def make(src, dst, target):
        i = used[0]
        used[0] += 1
        return pltpu.make_async_remote_copy(
            src_ref=src,
            dst_ref=dst,
            send_sem=r["ssem"].at[i],
            recv_sem=r["rsem"].at[i],
            device_id=target,
            device_id_type=MESH,
        )

    def send(src, dst, target):
        copy = make(src, dst, target)
        copy.start()
        sends.append(copy)
        return copy

    a1, b2 = r["a1"], r["b2"]
    a1[...] = jnp.zeros(a1.shape, BF)
    b2[...] = jnp.zeros(b2.shape, BF)
    lane_group = lax.shift_right_logical(lax.broadcasted_iota(jnp.int32, (MID, MID), 1), 5)
    row_group = lax.shift_right_logical(lax.broadcasted_iota(jnp.int32, (MID, MID), 0), 5)
    block_diagonal = lane_group == row_group
    if own_gather:
        wr, we, wg = r["wr"], r["we"], r["wg"]
        RB, EB = r["rm"].shape[0], r["em"].shape[1]
        GB = r["gm"].shape[0]

        def reduce_block(o):
            return wr.at[pl.ds(pl.multiple_of(o * RB, 16), RB), :]

        def expand_block(o):
            return we.at[:, pl.ds(pl.multiple_of(o * EB, 128), EB)]

        def group_block(o):
            return wg.at[o]

        reduce_block(owner)[...] = r["rm"][...].astype(BF)
        expand_block(owner)[...] = r["em"][...].astype(BF)
        wg[owner] = jnp.concatenate(
            [r["gm"][...], jnp.zeros((SLOT - GB, MID), F32)], axis=0
        ).astype(BF)
    else:
        wr, we = r["wr_full"], r["we_full"]

    barrier = pltpu.get_barrier_semaphore()
    everyone = family + twin_family + [core_peer]
    for target in everyone:
        pl.semaphore_signal(barrier, inc=1, device_id=target, device_id_type=MESH)
    pl.semaphore_wait(barrier, len(everyone))

    class Gather:
        def __init__(self, block):
            self.block = block
            self.here = block(owner)

        def start(self):
            self.along_z = [
                (dz, send(self.here, self.here, dev(dz, None, 0))) for dz in range(1, H)
            ]

        def start_y(self):
            self.along_y = [send(self.here, self.here, dev(0, None, dy)) for dy in range(1, D)]

        def forward(self):
            for dz, copy in self.along_z:
                copy.wait_recv()
                block = self.block(lax.rem(z - dz + H, H) * D + y)
                for dy in range(1, D):
                    self.along_y.append(send(block, block, dev(0, None, dy)))

        def finish(self):
            for copy in self.along_y:
                copy.wait_recv()

    if own_gather:
        g_reduce, g_group, g_expand = Gather(reduce_block), Gather(group_block), Gather(expand_block)
        g_reduce.start()
        g_reduce.start_y()
        g_group.start()
        g_group.start_y()
    ct2, out2 = r["ct2"], r["out2"]
    ct_in = send(ct_ref.at[rows(1 - xp)], ct2.at[xp], x_peer)
    ct2[xp] = ct_ref[rows(xp), :]
    out2[xp] = outer_ref[...]
    outer_in = send(out2.at[xp], out2.at[xp], x_peer)
    wep = r["wep"]
    twin_in = []
    if not own_gather:
        twin_in.append(send(we, wep, x_peer))

    def statistics(buf, position, targets, value):
        buf[position] = value
        return [send(buf.at[position], buf.at[position], t) for t in targets]

    def total(buf, copies):
        for copy in copies:
            copy.wait_recv()
        return jnp.sum(buf[...], axis=0)

    first = r["first"]

    def product(blocks, start):
        def body(h, carry):
            left = jnp.concatenate(
                [x_ref[rows(h), pl.ds(pl.multiple_of(o * RB, 128), RB)] for o in blocks], axis=1
            )
            right = jnp.concatenate([reduce_block(o)[...] for o in blocks], axis=0)
            part = dot(left, right)
            first[rows(h), :] = part if start else first[rows(h), :] + part
            return carry

        lax.fori_loop(0, 2, body, 0)

    if own_gather:
        g_reduce.forward()
        g_expand.start()
        g_expand.start_y()
        twin_in.append(send(g_expand.here, wep.at[:, pl.ds(pl.multiple_of(owner * EB, 128), EB)], x_peer))
        g_group.forward()
        product([zz * D + y for zz in range(H)], True)
        g_reduce.finish()
        for dy in range(1, D):
            product([zz * D + lax.rem(y + dy, D) for zz in range(H)], False)
    else:
        def body(h, carry):
            first[rows(h), :] = dot(x_ref[rows(h), :], wr[...])
            return carry

        lax.fori_loop(0, 2, body, 0)

    def moments(ref):
        def body(h, carry):
            v = ref[rows(h), :]
            return (
                carry[0] + jnp.sum(v, axis=0, keepdims=True) * valid(h),
                carry[1] + jnp.sum(v * v, axis=0, keepdims=True) * valid(h),
            )

        zero = jnp.zeros((1, ref.shape[1]), F32)
        return jnp.concatenate(lax.fori_loop(0, 2, body, (zero, zero)), axis=0)

    def average_and_inverse(sums):
        mean = sums[0:1] / pixels
        return mean, lax.rsqrt(sums[1:2] / pixels - mean * mean + NORM_EPS)

    stat1 = statistics(r["st1"], owner, family, moments(first))

    wall, wallt, gf = r["wall"], r["wallt"], r["gf"]
    if own_gather:
        g_group.finish()
        for o in range(HD):
            gf[o * GB : (o + 1) * GB, :] = wg[o].astype(F32)[0:GB]
    else:
        gf[...] = r["wg_full"][...].astype(F32)

    def spread(t, carry):
        piece = gf[pl.ds(pl.multiple_of(t * GROUP, 8), GROUP), :]
        full = jnp.where(block_diagonal, jnp.concatenate([piece] * (MID // GROUP), axis=0), 0.0)
        wall[pl.ds(pl.multiple_of(t * MID, 16), MID), :] = full.astype(BF)
        wallt[pl.ds(pl.multiple_of((8 - t) * MID, 16), MID), :] = full.T.astype(BF)
        return carry

    lax.fori_loop(0, 9, spread, 0)
    if own_gather:
        g_expand.forward()
        for dz in range(1, H):
            o = lax.rem(z - dz + H, H) * D + y
            there = pl.ds(pl.multiple_of(o * EB, 128), EB)
            twin_in.append(send(expand_block(o), wep.at[:, there], x_peer))

    mean1, inv1 = average_and_inverse(total(r["st1"], stat1))
    gain1, shift1 = inner_ref[0:1, :], inner_ref[1:2, :]
    slope1 = r["slope1"]

    def activate(h):
        ok = valid(h)

        def body(w, carry):
            v = (first[tile(h, w), :] - mean1) * inv1
            v = v * gain1 + shift1
            q = jax.nn.sigmoid(v)
            a1[slab(h + 1, w + 1, N), :] = (v * q * ok).astype(BF)
            slope1[tile(h, w), :] = q * (1.0 + v * (1.0 - q)) * ok
            return carry

        lax.fori_loop(0, W, body, 0)

    class Halo:
        def __init__(self, ref):
            self.up = make(ref.at[slab(1, 1, R)], ref.at[slab(3, 1, R)], dev(H - 1, None, 0))
            self.down = make(ref.at[slab(2, 1, R)], ref.at[slab(0, 1, R)], dev(1, None, 0))

        def start_up(self):
            pl.when(z > 0)(self.up.start)

        def start_down(self):
            pl.when(z < H - 1)(self.down.start)

        def arrived(self):
            pl.when(z > 0)(self.down.wait_recv)
            pl.when(z < H - 1)(self.up.wait_recv)

        def sent(self):
            pl.when(z > 0)(self.up.wait_send)
            pl.when(z < H - 1)(self.down.wait_send)

    halo1, halo2 = Halo(a1), Halo(b2)
    activate(0)
    halo1.start_up()
    activate(1)
    halo1.start_down()

    def convolve(ref, weights, out, edge):
        def body(h, carry):
            if edge:
                hh, base, count = 3 * h, 6 * h, 1
            else:
                hh, base, count = 1, 3 * (1 - h), 2
            left = jnp.concatenate(
                [ref[slab(hh + i, kc, R), :] for i in range(count) for kc in range(3)], axis=1
            )
            part = dot(left, weights[pl.ds(pl.multiple_of(base * MID, 16), 3 * count * MID), :])
            out[rows(h), :] = out[rows(h), :] + part if edge else part
            return carry

        lax.fori_loop(0, 2, body, 0)

    second = r["second"]
    convolve(a1, wall, second, False)
    halo1.arrived()
    convolve(a1, wall, second, True)
    stat2 = statistics(r["st2"], owner, family, moments(second))
    if own_gather:
        g_expand.finish()
        for dy in range(1, D):
            for zz in range(H):
                o = zz * D + lax.rem(y + dy, D)
                there = pl.ds(pl.multiple_of(o * EB, 128), EB)
                twin_in.append(send(expand_block(o), wep.at[:, there], x_peer))
    mean2, inv2 = average_and_inverse(total(r["st2"], stat2))
    gain2, shift2 = inner_ref[2:3, :], inner_ref[3:4, :]
    a2, slope2 = r["a2"], r["slope2"]

    def activate_two(h):
        ok = valid(h)

        def body(w, carry):
            n = (second[tile(h, w), :] - mean2) * inv2
            second[tile(h, w), :] = n
            v = n * gain2 + shift2
            q = jax.nn.sigmoid(v)
            a2[tile(h, w), :] = (v * q * ok).astype(BF)
            slope2[tile(h, w), :] = q * (1.0 + v * (1.0 - q)) * ok
            return carry

        lax.fori_loop(0, W, body, 0)

    activate_two(1 - xp)
    ax_in = send(a2.at[rows(1 - xp)], r["ax"], x_peer)
    activate_two(xp)

    for copy in twin_in:
        copy.wait_recv()
    ax_in.wait_recv()
    third, tsend, trecv = r["third"], r["tsend"], r["trecv"]
    left = jnp.concatenate([a2[rows(xp), :], r["ax"][...]], axis=1)

    def expand(j, core):
        right = jnp.concatenate([we[:, quarter(j, core)], wep[:, quarter(j, core)]], axis=0)
        return dot(left, right)

    core_in = []
    for j in range(2):
        tsend[j] = expand(j, 1 - k).astype(BF)
        core_in.append(send(tsend.at[j], trecv.at[j], core_peer))
    for j in range(2):
        third[j] = expand(j, k)
    okx = valid(xp)
    sums = []
    for j in range(2):
        core_in[j].wait_recv()

        def body(w, carry):
            at = pl.ds(pl.multiple_of(w * N, 16), N)
            v = third[j, at, :] + trecv[j, at, :].astype(F32)
            third[j, at, :] = v
            return carry[0] + jnp.sum(v, axis=0, keepdims=True), carry[1] + jnp.sum(
                v * v, axis=0, keepdims=True
            )

        zero = jnp.zeros((1, OUT), F32)
        sums.append(lax.fori_loop(0, W, body, (zero, zero)))
    position = xp * HD + owner
    both = family + twin_family
    stat3 = statistics(
        r["st3"],
        position,
        both,
        jnp.concatenate(
            [jnp.concatenate([s[i] for s in sums], axis=1) * okx for i in range(2)], axis=0
        ),
    )
    ct_in.wait_recv()
    outer_in.wait_recv()
    mean3, inv3 = average_and_inverse(total(r["st3"], stat3))
    dpre, boj = r["dpre"], r["boj"]
    sums = []
    for j in range(2):
        lanes = slice(j * OUT, (j + 1) * OUT)
        m, iv = mean3[:, lanes], inv3[:, lanes]
        g, s = out2[j, 0:1, :], out2[j, 1:2, :]

        def body(w, carry):
            at = pl.ds(pl.multiple_of(w * N, 16), N)
            n = (third[j, at, :] - m) * iv
            third[j, at, :] = n
            v = n * g + s + x_ref[tile(xp, w), quarter(j, k)].astype(F32)
            q = jax.nn.sigmoid(v)
            boj[j, at, :] = (v * q * okx).astype(BF)
            d = ct2[j, at, :].astype(F32) * okx * (q * (1.0 + v * (1.0 - q)))
            dpre[j, at, :] = d
            return carry[0] + jnp.sum(d, axis=0, keepdims=True), carry[1] + jnp.sum(
                d * n, axis=0, keepdims=True
            )

        zero = jnp.zeros((1, OUT), F32)
        sums.append(lax.fori_loop(0, W, body, (zero, zero)))
    stat3b = statistics(
        r["st3b"],
        position,
        both,
        jnp.concatenate(
            [jnp.concatenate([s[i] for s in sums], axis=1) for i in range(2)], axis=0
        ),
    )
    a2t = r["a2t"]
    a2t[...] = a2[...].T
    total3 = total(r["st3b"], stat3b)
    r["tot3"][...] = total3
    piece = r["piece"]
    core_in = []
    for j in range(2):
        lanes = slice(j * OUT, (j + 1) * OUT)
        factor = out2[j, 0:1, :] * inv3[:, lanes] * okx
        sh = total3[0:1, lanes] / pixels
        ga = total3[1:2, lanes] / pixels

        def body(w, carry):
            at = pl.ds(pl.multiple_of(w * N, 16), N)
            v = factor * (dpre[j, at, :] - sh - third[j, at, :] * ga)
            piece[tile(xp, w), quarter(j, k)] = v.astype(BF)
            return carry

        lax.fori_loop(0, W, body, 0)
        part = piece.at[rows(xp), quarter(j, k)]
        core_in.append(send(part, part, core_peer))
    for copy in core_in:
        copy.wait_recv()
    agrad = r["agrad"]
    r["agsend"][...] = dot_nt(piece[rows(xp), :], wep[...]).astype(BF)
    ag_in = send(r["agsend"], r["agrecv"], x_peer)
    piece_in = []
    for j in range(2):
        part = piece.at[rows(xp), quarter(j, k)]
        piece_in.append(send(part, part, x_peer))
    agrad[rows(xp), :] = dot_nt(piece[rows(xp), :], we[...])

    def slope_two(h, received, carry):
        def body(w, carry):
            if received:
                up = r["agrecv"][pl.ds(pl.multiple_of(w * N, 16), N), :].astype(F32)
            else:
                up = agrad[tile(h, w), :]
            d = up * slope2[tile(h, w), :]
            agrad[tile(h, w), :] = d
            return carry[0] + jnp.sum(d, axis=0, keepdims=True), carry[1] + jnp.sum(
                d * second[tile(h, w), :], axis=0, keepdims=True
            )

        return lax.fori_loop(0, W, body, carry)

    zero = jnp.zeros((1, MID), F32)
    carry = slope_two(xp, False, (zero, zero))
    ag_in.wait_recv()
    carry = slope_two(1 - xp, True, carry)
    stat2b = statistics(r["st2b"], owner, family, jnp.concatenate(carry, axis=0))
    bo_in = send(boj.at[1 - xp], r["borecv"], x_peer)
    total2 = total(r["st2b"], stat2b)
    b2n = r["b2n"]

    def norm_two(h):
        factor = gain2 * inv2 * valid(h)
        sh, ga = total2[0:1] / pixels, total2[1:2] / pixels

        def body(w, carry):
            v = factor * (agrad[tile(h, w), :] - sh - second[tile(h, w), :] * ga)
            v = v.astype(BF)
            b2[slab(h + 1, w + 1, N), :] = v
            b2n[tile(h, w), :] = v
            return carry

        lax.fori_loop(0, W, body, 0)

    norm_two(0)
    halo2.start_up()
    norm_two(1)
    halo2.start_down()
    back1 = r["second_back"]
    convolve(b2, wallt, back1, False)
    b2t = r["b2t"]
    b2t[...] = b2n[...].T
    halo2.arrived()
    convolve(b2, wallt, back1, True)

    def slope_one(i, carry):
        h, w = lax.div(i, W), lax.rem(i, W)
        d = back1[tile(h, w), :] * slope1[tile(h, w), :]
        n = (first[tile(h, w), :] - mean1) * inv1
        first[tile(h, w), :] = n
        back1[tile(h, w), :] = d
        return carry[0] + jnp.sum(d, axis=0, keepdims=True), carry[1] + jnp.sum(
            d * n, axis=0, keepdims=True
        )

    carry = lax.fori_loop(0, 2 * W, slope_one, (zero, zero))
    stat1b = statistics(r["st1b"], owner, family, jnp.concatenate(carry, axis=0))

    core_in = []
    for j in range(2):
        piece_in[j].wait_recv()
        part = piece.at[rows(1 - xp), quarter(j, k)]
        core_in.append(send(part, part, core_peer))
    ggf = r["ggf"]
    fold = jnp.where(
        jnp.bitwise_and(lax.broadcasted_iota(jnp.int32, (GROUP, MID), 1), GROUP - 1)
        == lax.broadcasted_iota(jnp.int32, (GROUP, MID), 0),
        1.0,
        0.0,
    ).astype(BF)

    def group_grad(t, carry):
        kr, kc = lax.div(t, 3), lax.rem(t, 3)
        left = jnp.concatenate([a1[slab(kr, kc, R), :], a1[slab(kr + 1, kc, R), :]], axis=0)
        turned = jnp.where(block_diagonal, dot(b2t[...], left), 0.0).astype(BF)
        ggf[pl.ds(pl.multiple_of(t * GROUP, 8), GROUP), :] = dot_nt(fold, turned)
        return carry

    lax.fori_loop(0, 9, group_grad, 0)

    class Scatter:
        def __init__(self, name, block):
            self.block = block
            self.ys, self.yr = r[name + "_ys"], r[name + "_yr"]
            self.zs, self.zr = r[name + "_zs"], r[name + "_zr"]

        def start(self):
            self.along_y = []
            for dz in list(range(1, H)) + [0]:
                zi = lax.rem(z + dz, H)
                for dy in range(1, D):
                    n = (dy - 1) * H + dz
                    self.ys[n] = self.block(zi * D + lax.rem(y + dy, D)).astype(BF)
                    self.along_y.append((dz, n, send(self.ys.at[n], self.yr.at[n], dev(0, None, dy))))

        def middle(self):
            self.along_z = []
            for dz in list(range(1, H)) + [0]:
                value = self.block(lax.rem(z + dz, H) * D + y)
                for at, n, copy in self.along_y:
                    if at == dz:
                        copy.wait_recv()
                        value = value + self.yr[n].astype(F32)
                if dz:
                    self.zs[dz - 1] = value.astype(BF)
                    self.along_z.append(send(self.zs.at[dz - 1], self.zr.at[dz - 1], dev(dz, None, 0)))
                else:
                    self.own = value

        def finish(self):
            value = self.own
            for i, copy in enumerate(self.along_z):
                copy.wait_recv()
                value = value + self.zr[i].astype(F32)
            return value

    def wide(left_ref, right_ref, o):
        return dot(left_ref[...], right_ref[:, pl.ds(pl.multiple_of(o * EB, 128), EB)])

    for copy in core_in:
        copy.wait_recv()
    if own_gather:
        def group_part(o):
            return r["ggs"][o].astype(F32)

        for o in range(HD):
            r["ggs"][o] = jnp.concatenate(
                [ggf[o * GB : (o + 1) * GB, :], jnp.zeros((SLOT - GB, MID), F32)], axis=0
            )
        s_group = Scatter("gg", group_part)
        s_expand = Scatter("eg", lambda o: wide(a2t, piece, o))
        s_group.start()
        s_expand.start()
    else:
        r["group_out"][...] = ggf[...].astype(BF)
        r["expand_out"][...] = dot(a2t[...], piece[...]).astype(BF)

    total1 = total(r["st1b"], stat1b)
    b1 = r["b1"]

    def norm_one(i, carry):
        h, w = lax.div(i, W), lax.rem(i, W)
        factor = gain1 * inv1 * valid(h)
        sh, ga = total1[0:1] / pixels, total1[1:2] / pixels
        v = factor * (back1[tile(h, w), :] - sh - first[tile(h, w), :] * ga)
        b1[tile(h, w), :] = v.astype(BF)
        return carry

    lax.fori_loop(0, 2 * W, norm_one, 0)

    ipsend, iprecv, xsend, xrecv = r["ipsend"], r["iprecv"], r["xsend"], r["xrecv"]
    ig = r["ig"]

    def share(j, core, h):
        return dot_nt(b1[rows(h), :], wr[quarter(j, core), :])

    core_in = []
    for n, j in enumerate((1 - xp, xp)):
        for h in range(2):
            ipsend[n, rows(h), :] = share(j, 1 - k, h).astype(BF)
            core_in.append(send(ipsend.at[n, rows(h)], iprecv.at[n, rows(h)], core_peer))
        if n == 0:
            x_in = []
            for h in range(2):
                part = share(j, k, h)
                here = jnp.where(xp == h, 1.0, 0.0).astype(F32)
                core_in[h].wait_recv()
                part = part + iprecv[0, rows(h), :].astype(F32) + here * dpre[j]
                xsend[rows(h), :] = part.astype(BF)
                x_in.append(send(xsend.at[rows(h)], xrecv.at[rows(h)], x_peer))
    b1t = r["b1t"]
    b1t[...] = b1[...].T
    if own_gather:
        s_reduce = Scatter("rg", lambda o: wide(b1t, x_ref, o))
        s_group.middle()
        s_reduce.start()
        s_expand.middle()
    else:
        r["reduce_out"][...] = dot(b1t[...], x_ref[...]).astype(BF)
    for h in range(2):
        part = share(xp, k, h)
        here = jnp.where(xp == h, 1.0, 0.0).astype(F32)
        core_in[2 + h].wait_recv()
        ig[rows(h), :] = part + iprecv[1, rows(h), :].astype(F32) + here * dpre[xp]
    r["inner_grad"][...] = jnp.concatenate(
        [total1[1:2], total1[0:1], total2[1:2], total2[0:1]], axis=0
    )
    mine = r["tot3"][:, pl.ds(pl.multiple_of(xp * OUT, 128), OUT)]
    r["outer_grad"][...] = jnp.concatenate([mine[1:2], mine[0:1]], axis=0)
    bo = r["bo"]
    bo[rows(xp), :] = boj[xp]
    bo_in.wait_recv()
    bo[rows(1 - xp), :] = r["borecv"][...]
    if own_gather:
        s_reduce.middle()
        r["group_out"][...] = s_group.finish()[0:GB]
        r["expand_out"][...] = s_expand.finish()
        r["reduce_out"][...] = s_reduce.finish().T
    for h in range(2):
        x_in[h].wait_recv()
        ig[rows(h), :] = ig[rows(h), :] + xrecv[rows(h), :].astype(F32)
    for copy in sends:
        copy.wait_send()
    halo1.sent()
    halo2.sent()


def adamw_step(master, gradient, moment_one, moment_two, average, rate):
    first_new = 0.5 * moment_one + 0.5 * gradient
    second_new = 0.5 * moment_two + 0.5 * gradient * gradient
    correct = 1.0 - 0.5**STEP
    direction = first_new / correct / (jnp.sqrt(second_new / correct) + 1e-08)
    master_new = master - rate * (direction + 0.05 * master)
    average_new = 0.75 * average + 0.25 * master_new
    return (first_new, second_new, master_new, average_new)


def adamw_kernel(*refs):
    ins, outs = refs[:25], list(refs[25:])
    for n in range(5):
        gradient, master, one, two, average = (ref[...] for ref in ins[5 * n : 5 * n + 5])
        rate = CONV_RATE if n < 3 else NORM_RATE
        first, second, new, mean = adamw_step(master, gradient, one, two, average, rate)
        values = [gradient, first, second, new] + ([new.astype(BF)] if n < 3 else []) + [mean]
        for value in values:
            outs.pop(0)[...] = value


def step_sizes(leaves):
    return [jax.ShapeDtypeStruct(a.shape, a.dtype) for a in leaves]


def local(
    inputs, cotangent,
    reduce_master, reduce_first, reduce_second, reduce_average,
    group_master, group_first, group_second, group_average,
    expand_master, expand_first, expand_second, expand_average,
    inner_master, inner_first, inner_second, inner_average,
    outer_master, outer_first, outer_second, outer_average,
):
    N, rows, W, CIN = inputs.shape
    OUT = cotangent.shape[3]
    MID = inner_master.shape[1]
    H, D = lax.axis_size("height"), lax.axis_size("dp")
    HD = H * D
    R = W * N
    GB = group_master.shape[0]
    RB, EB = reduce_master.shape[0], expand_master.shape[1]
    own_gather = RB % 128 == 0 and EB % 128 == 0
    dims = dict(H=H, D=D, N=N, W=W, MID=MID, OUT=OUT, CIN=CIN, own_gather=own_gather)

    x = inputs.transpose(1, 2, 0, 3).reshape(rows * R, CIN)
    ct = cotangent.transpose(1, 2, 0, 3).reshape(rows * R, OUT)
    ins = dict(x=x, ct=ct, inner=inner_master, outer=outer_master)
    outs = dict(
        bo=((rows * R, OUT), BF),
        ig=((rows * R, OUT), F32),
        inner_grad=(inner_master.shape, F32),
        outer_grad=(outer_master.shape, F32),
    )
    scratch = dict(
        wep=((MID, CIN), BF),
        ct2=((2, R, OUT), BF),
        out2=((2, 2, OUT), F32),
        first=((2 * R, MID), F32),
        second=((2 * R, MID), F32),
        slope1=((2 * R, MID), F32),
        slope2=((2 * R, MID), F32),
        a1=((4 * (W + 2) * N, MID), BF),
        b2=((4 * (W + 2) * N, MID), BF),
        wall=((9 * MID, MID), BF),
        wallt=((9 * MID, MID), BF),
        gf=((9 * GROUP, MID), F32),
        ggf=((9 * GROUP, MID), F32),
        st1=((HD, 2, MID), F32),
        st2=((HD, 2, MID), F32),
        st3=((2 * HD, 2, 2 * OUT), F32),
        st3b=((2 * HD, 2, 2 * OUT), F32),
        st2b=((HD, 2, MID), F32),
        st1b=((HD, 2, MID), F32),
        tot3=((2, 2 * OUT), F32),
        a2=((2 * R, MID), BF),
        a2t=((MID, 2 * R), BF),
        ax=((R, MID), BF),
        third=((2, R, OUT), F32),
        tsend=((2, R, OUT), BF),
        trecv=((2, R, OUT), BF),
        dpre=((2, R, OUT), F32),
        boj=((2, R, OUT), BF),
        borecv=((R, OUT), BF),
        piece=((2 * R, CIN), BF),
        agrad=((2 * R, MID), F32),
        agsend=((R, MID), BF),
        agrecv=((R, MID), BF),
        b2n=((2 * R, MID), BF),
        b2t=((MID, 2 * R), BF),
        second_back=((2 * R, MID), F32),
        b1=((2 * R, MID), BF),
        b1t=((MID, 2 * R), BF),
        ipsend=((2, 2 * R, OUT), BF),
        iprecv=((2, 2 * R, OUT), BF),
        xsend=((2 * R, OUT), BF),
        xrecv=((2 * R, OUT), BF),
    )
    if own_gather:
        ins.update(rm=reduce_master, gm=group_master, em=expand_master)
        outs.update(
            reduce_out=((RB, MID), F32), group_out=((GB, MID), F32), expand_out=((MID, EB), F32)
        )
        scratch.update(
            wr=((CIN, MID), BF), we=((MID, CIN), BF), wg=((HD, SLOT, MID), BF),
            ggs=((HD, SLOT, MID), F32),
        )
        for name, shape in (("rg", (MID, RB)), ("eg", (MID, EB)), ("gg", (SLOT, MID))):
            scratch[name + "_ys"] = scratch[name + "_yr"] = (((D - 1) * H, *shape), BF)
            scratch[name + "_zs"] = scratch[name + "_zr"] = ((H - 1, *shape), BF)
    else:
        both = ("height", "dp")
        ins.update(
            wr_full=lax.all_gather(reduce_master.astype(BF), both, axis=0, tiled=True),
            wg_full=lax.all_gather(group_master.astype(BF), both, axis=0, tiled=True),
            we_full=lax.all_gather(expand_master.astype(BF), both, axis=1, tiled=True),
        )
        outs.update(
            reduce_out=((MID, CIN), BF),
            group_out=((9 * GROUP, MID), BF),
            expand_out=((MID, CIN), BF),
        )
    names = [*ins, *outs, *scratch, "ssem", "rsem"]
    whole = pl.BlockSpec(memory_space=pltpu.VMEM)
    results = pl.pallas_call(
        functools.partial(block_kernel, names, dims),
        out_shape=[jax.ShapeDtypeStruct(*v) for v in outs.values()],
        in_specs=[whole] * len(ins),
        out_specs=[whole] * len(outs),
        scratch_shapes=[pltpu.VMEM(*v) for v in scratch.values()]
        + [pltpu.SemaphoreType.DMA((dims.get("semaphores", SEMAPHORES + 16 * D),))] * 2,
        compiler_params=pltpu.CompilerParams(
            collective_id=0, has_side_effects=True, vmem_limit_bytes=56 << 20
        ),
        name="block",
    )(*ins.values())
    got = dict(zip(outs, results, strict=True))
    block_out = got["bo"].reshape(rows, W, N, OUT).transpose(2, 0, 1, 3)
    input_grad = got["ig"].reshape(rows, W, N, OUT).transpose(2, 0, 1, 3)
    reduce_grad, group_grad, expand_grad = got["reduce_out"], got["group_out"], got["expand_out"]
    if not own_gather:
        both = ("height", "dp")
        reduce_grad = lax.psum_scatter(reduce_grad.T, both, scatter_dimension=0, tiled=True).astype(F32)
        group_grad = lax.psum_scatter(group_grad, both, scatter_dimension=0, tiled=True).astype(F32)
        expand_grad = lax.psum_scatter(expand_grad, both, scatter_dimension=1, tiled=True).astype(F32)
    groups = (
        (reduce_grad, reduce_master, reduce_first, reduce_second, reduce_average),
        (group_grad, group_master, group_first, group_second, group_average),
        (expand_grad, expand_master, expand_first, expand_second, expand_average),
        (got["inner_grad"], inner_master, inner_first, inner_second, inner_average),
        (got["outer_grad"], outer_master, outer_first, outer_second, outer_average),
    )
    shapes = []
    for n, group in enumerate(groups):
        kinds = [F32] * 4 + ([BF] if n < 3 else []) + [F32]
        shapes += [jax.ShapeDtypeStruct(group[0].shape, kind) for kind in kinds]
    flat = [a for group in groups for a in group]
    news = pl.pallas_call(
        adamw_kernel,
        out_shape=shapes,
        in_specs=[whole] * len(flat),
        out_specs=[whole] * len(shapes),
        compiler_params=pltpu.CompilerParams(vmem_limit_bytes=32 << 20),
        name="adamw",
    )(*flat)
    return (block_out, input_grad, *news)


def solution(mesh):
    pixel = P("dp", "height", None, "chan")
    first = P(("height", "dp"), "chan")
    last = P("chan", ("height", "dp"))
    table = P(None, "chan")
    return jax.shard_map(
        local,
        mesh=mesh,
        in_specs=(P("dp", "height", None, None), pixel)
        + (first,) * 8
        + (last,) * 4
        + (table,) * 8,
        out_specs=(pixel, pixel) + (first,) * 12 + (last,) * 6 + (table,) * 10,
        check_vma=False,
    )
```

time: 608 us -> 155 us (0.25)
  waiting for transfers between devices: 215 us -> 0 us
  blocking collectives: 148 us -> 0 us
  Pallas kernels: 0 us -> 139 us
  local copies, waits for them, and re-layouts: 145 us -> 12.9 us
  matrix products: 39.2 us -> 0 us
  other arithmetic: 24.8 us -> 0 us
  between operations: 14.9 us -> 1.21 us
  starting transfers between devices: 13.2 us -> 0 us
    pallas_call x0 -> x2, Pallas kernels: none -> 139 us  [the longest x1 137 us: local(): pl.pallas_call(functools.partial(block_kernel, names, dims), out_shape=[j...]
    psum x6 -> x0, blocking collectives: 117 us -> none  [the longest x1 21.7 us: local(): lax.psum((jnp.sum(dz_two * valid_rows, axis=(0, 1, 2)), jnp.sum(dz_two *...]
    psum x1 -> x0, waiting for transfers between devices: 91.3 us -> none  [local(): lax.psum(reduce_local.astype(jnp.bfloat16), ('height', 'dp'))]
    reduce_scatter x2 -> x0, waiting for transfers between devices: 61.9 us -> none  [the longest x1 44.9 us: local(): lax.psum_scatter(partial_out, 'chan', scatter_dimension=3, tiled=True)]
    unnamed x155 -> x50, local copies, waits for them, and re-layouts: 61.7 us -> 0.15 us
    all_gather x3 -> x0, waiting for transfers between devices: 61.4 us -> none  [the longest x1 40.1 us: local(): lax.all_gather(reduce_master.astype(jnp.bfloat16), ('height', 'dp'), axis...]
    dot_general x9 -> x0, matrix products: 39.2 us -> none  [the longest x1 6.8 us: local(): jnp.einsum('nhwgk,nhwgo->kgo', taps_one, back_two.reshape(batch_size, loc...]
    another operation x20 -> x0, local copies, waits for them, and re-layouts: 35.3 us -> none  [window_taps(): jnp.stack(pieces, axis=3)]
  transfers between devices with their start and end apart: 10 -> 0, of which waited for: 5 -> 0; matrix products, arithmetic and copies ran while one was open for 18% -> 0% of each run, Pallas kernels for 0% -> 0%
where the time goes in v1:
time: 155 us; the launch traced here: 153 us
  Pallas kernels  139 us (90%)
  local copies, waits for them, and re-layouts  12.9 us (8%)
    pallas_call x1, Pallas kernels, local(): pl.pallas_call(functools.partial(block_kernel, names, dims), out_shape=[j...  137 us
    transpose x1, local copies, waits for them, and re-layouts, local(): x = inputs.transpose(1, 2, 0, 3).reshape(rows * R, CIN)  4.5 us
    reshape x1, local copies, waits for them, and re-layouts, local(): input_grad = got['ig'].reshape(rows, W, N, OUT).transpose(2, 0, 1, 3)  3.48 us

profile of v1, /device:TPU:2, one launch (start us, length us, event | category | flops | bytes accessed | tf_op | source)
XLA Modules:
  0.0 152.7 jit_solution(1308338583446206719)
XLA Ops:
  0.7 2.0 %copy.53 = bf16[2,7,48,512]{3,2,1,0:T(8,128)(2,1)} copy(bf16[2,7,48,512]{3,0,1,2:T(2,128)(2,1)} %bitcast.17) | data formatting | bytes 1376256 | tf_op jit(solution)/shard_map/transpose | solution.py:705
  2.7 4.5 %copy.52 = bf16[2,7,48,2048]{3,2,1,0:T(8,128)(2,1)} copy(bf16[2,7,48,2048]{3,0,1,2:T(2,128)(2,1)} %bitcast.13) | data formatting | bytes 5505024 | tf_op jit(solution)/shard_map/transpose | solution.py:704
  7.2 136.5 %block.1 = (bf16[672,512]{1,0:T(8,128)(2,1)}, f32[672,512]{1,0:T(8,128)}, f32[4,256]{1,0:T(4,128)}, f32[2,512]{1,0:T(2,128)}, f32[256,256]{1,0:T(8,128)}, /*index=5*/f32[36,256]{1,0:T(8,128)}, f32[256,256]{1,0:T(8,128)}) custom-call(bf16[672,2048]{1,0:T(8,128)(2,1)} %bitcast.12, bf16[672,512]{1,0:T(8,128)(2,1)} %bitcast.14, f32[4,256]{1,0:T(4,128)} %refs_16_.1, ...), custom_call_target="tpu_custom_call" | custom-call | tf_op jit(solution)/shard_map/block/pallas_call | solution.py:783
  143.7 0.0 copy-start
  143.8 0.0 copy-start.1
  143.8 0.0 copy-start.2
  143.8 0.0 copy-start.3
  143.8 0.0 copy-start.4
  143.8 0.0 copy-start.5
  143.8 0.0 copy-start.6
  143.8 0.0 copy-start.7
  143.8 0.0 copy-start.8
  143.9 0.0 copy-start.10
  143.9 0.0 copy-start.11
  143.9 0.0 copy-start.12
  143.9 0.0 copy-start.13
  143.9 0.0 copy-start.14
  143.9 0.0 copy-start.15
  143.9 0.0 copy-start.16
  143.9 0.0 copy-start.17
  144.0 0.0 copy-start.18
  144.0 0.0 copy-start.19
  144.0 0.0 copy-start.20
  144.0 0.0 copy-start.21
  144.0 0.0 copy-start.22
  144.0 0.0 copy-start.23
  144.0 0.0 copy-start.24
  144.0 2.8 %copy.59 = bf16[2,7,48,512]{3,0,1,2:T(2,128)(2,1)} copy(bf16[2,7,48,512]{3,2,1,0:T(8,128)(2,1)} %bitcast.19) | data formatting | bytes 1376256 | tf_op jit(solution)/shard_map/reshape | solution.py:796
  146.8 3.5 %copy.58 = f32[2,7,48,512]{3,0,1,2:T(2,128)} copy(f32[2,7,48,512]{3,2,1,0:T(8,128)} %bitcast.16) | data formatting | bytes 2752512 | tf_op jit(solution)/shard_map/reshape | solution.py:797
  150.3 0.0 copy-done
  150.3 0.0 copy-done.2
  150.5 2.0 %adamw.1 = (f32[256,256]{1,0:T(8,128)}, f32[256,256]{1,0:T(8,128)}, f32[256,256]{1,0:T(8,128)}, f32[256,256]{1,0:T(8,128)}, bf16[256,256]{1,0:T(8,128)(2,1)}, /*...) custom-call(f32[256,256]{1,0:T(8,128)S(1)} %copy-done.8, ...), custom_call_target="tpu_custom_call" | custom-call | tf_op jit(solution)/shard_map/adamw/pallas_call | solution.py:816
  (24 shorter events, 0.1 us)
Async XLA Ops:
  143.7 6.6 %copy-start = (f32[256,256]{1,0:T(8,128)S(1)}, f32[256,256]{1,0:T(8,128)}, u32[]{:S(2)}) copy-start(f32[256,256]{1,0:T(8,128)} %refs_1_.1) | copy-start | bytes 786436
  143.8 6.6 %copy-start.1 = (f32[256,256]{1,0:T(8,128)S(1)}, f32[256,256]{1,0:T(8,128)}, u32[]{:S(2)}) copy-start(f32[256,256]{1,0:T(8,128)} %refs_11_.1) | copy-start | bytes 786436
  143.8 6.5 %copy-start.2 = (f32[256,256]{1,0:T(8,128)S(1)}, f32[256,256]{1,0:T(8,128)}, u32[]{:S(2)}) copy-start(f32[256,256]{1,0:T(8,128)} %refs_2_.3) | copy-start | bytes 786436
  143.8 6.5 %copy-start.3 = (f32[256,256]{1,0:T(8,128)S(1)}, f32[256,256]{1,0:T(8,128)}, u32[]{:S(2)}) copy-start(f32[256,256]{1,0:T(8,128)} %refs_3_.3) | copy-start | bytes 786436
  143.8 6.5 %copy-start.4 = (f32[256,256]{1,0:T(8,128)S(1)}, f32[256,256]{1,0:T(8,128)}, u32[]{:S(2)}) copy-start(f32[256,256]{1,0:T(8,128)} %refs_4_.3) | copy-start | bytes 786436
  143.8 6.5 %copy-start.5 = (f32[256,256]{1,0:T(8,128)S(1)}, f32[256,256]{1,0:T(8,128)}, u32[]{:S(2)}) copy-start(f32[256,256]{1,0:T(8,128)} %refs_12_.1) | copy-start | bytes 786436
  143.8 6.5 %copy-start.6 = (f32[256,256]{1,0:T(8,128)S(1)}, f32[256,256]{1,0:T(8,128)}, u32[]{:S(2)}) copy-start(f32[256,256]{1,0:T(8,128)} %refs_13_.1) | copy-start | bytes 786436
  143.8 6.5 %copy-start.7 = (f32[256,256]{1,0:T(8,128)S(1)}, f32[256,256]{1,0:T(8,128)}, u32[]{:S(2)}) copy-start(f32[256,256]{1,0:T(8,128)} %refs_14_.1) | copy-start | bytes 786436
  143.8 6.5 %copy-start.8 = (f32[256,256]{1,0:T(8,128)S(1)}, f32[256,256]{1,0:T(8,128)}, u32[]{:S(2)}) copy-start(f32[256,256]{1,0:T(8,128)} %get-tuple-element.67.refs_0_) | copy-start | bytes 786436
  143.9 6.5 %copy-start.9 = (f32[256,256]{1,0:T(8,128)S(1)}, f32[256,256]{1,0:T(8,128)}, u32[]{:S(2)}) copy-start(f32[256,256]{1,0:T(8,128)} %get-tuple-element.69.refs_10_) | copy-start | bytes 786436
  143.9 6.5 %copy-start.10 = (f32[36,256]{1,0:T(8,128)S(1)}, f32[36,256]{1,0:T(8,128)}, u32[]{:S(2)}) copy-start(f32[36,256]{1,0:T(8,128)} %refs_6_.3) | copy-start | bytes 110596
  143.9 6.5 %copy-start.11 = (f32[36,256]{1,0:T(8,128)S(1)}, f32[36,256]{1,0:T(8,128)}, u32[]{:S(2)}) copy-start(f32[36,256]{1,0:T(8,128)} %refs_7_.1) | copy-start | bytes 110596
  143.9 6.5 %copy-start.12 = (f32[36,256]{1,0:T(8,128)S(1)}, f32[36,256]{1,0:T(8,128)}, u32[]{:S(2)}) copy-start(f32[36,256]{1,0:T(8,128)} %refs_8_.1) | copy-start | bytes 110596
  143.9 6.5 %copy-start.13 = (f32[36,256]{1,0:T(8,128)S(1)}, f32[36,256]{1,0:T(8,128)}, u32[]{:S(2)}) copy-start(f32[36,256]{1,0:T(8,128)} %refs_9_.1) | copy-start | bytes 110596
  143.9 6.5 %copy-start.14 = (f32[36,256]{1,0:T(8,128)S(1)}, f32[36,256]{1,0:T(8,128)}, u32[]{:S(2)}) copy-start(f32[36,256]{1,0:T(8,128)} %get-tuple-element.68.refs_5_) | copy-start | bytes 110596
  143.9 6.5 %copy-start.15 = (f32[4,256]{1,0:T(4,128)S(1)}, f32[4,256]{1,0:T(4,128)}, u32[]{:S(2)}) copy-start(f32[4,256]{1,0:T(4,128)} %refs_16_.1) | copy-start | bytes 12292
  143.9 6.5 %copy-start.16 = (f32[2,512]{1,0:T(2,128)S(1)}, f32[2,512]{1,0:T(2,128)}, u32[]{:S(2)}) copy-start(f32[2,512]{1,0:T(2,128)} %refs_21_.1) | copy-start | bytes 12292
  143.9 6.5 %copy-start.17 = (f32[4,256]{1,0:T(4,128)S(1)}, f32[4,256]{1,0:T(4,128)}, u32[]{:S(2)}) copy-start(f32[4,256]{1,0:T(4,128)} %refs_17_.1) | copy-start | bytes 12292
  144.0 6.5 %copy-start.18 = (f32[4,256]{1,0:T(4,128)S(1)}, f32[4,256]{1,0:T(4,128)}, u32[]{:S(2)}) copy-start(f32[4,256]{1,0:T(4,128)} %refs_18_.1) | copy-start | bytes 12292
  144.0 6.5 %copy-start.19 = (f32[4,256]{1,0:T(4,128)S(1)}, f32[4,256]{1,0:T(4,128)}, u32[]{:S(2)}) copy-start(f32[4,256]{1,0:T(4,128)} %refs_19_.1) | copy-start | bytes 12292
  144.0 6.5 %copy-start.20 = (f32[2,512]{1,0:T(2,128)S(1)}, f32[2,512]{1,0:T(2,128)}, u32[]{:S(2)}) copy-start(f32[2,512]{1,0:T(2,128)} %refs_22_.1) | copy-start | bytes 12292
  144.0 6.5 %copy-start.21 = (f32[2,512]{1,0:T(2,128)S(1)}, f32[2,512]{1,0:T(2,128)}, u32[]{:S(2)}) copy-start(f32[2,512]{1,0:T(2,128)} %refs_23_.1) | copy-start | bytes 12292
  144.0 6.5 %copy-start.22 = (f32[2,512]{1,0:T(2,128)S(1)}, f32[2,512]{1,0:T(2,128)}, u32[]{:S(2)}) copy-start(f32[2,512]{1,0:T(2,128)} %refs_24_.1) | copy-start | bytes 12292
  144.0 6.5 %copy-start.23 = (f32[4,256]{1,0:T(4,128)S(1)}, f32[4,256]{1,0:T(4,128)}, u32[]{:S(2)}) copy-start(f32[4,256]{1,0:T(4,128)} %get-tuple-element.70.refs_15_) | copy-start | bytes 12292
  144.0 6.5 %copy-start.24 = (f32[2,512]{1,0:T(2,128)S(1)}, f32[2,512]{1,0:T(2,128)}, u32[]{:S(2)}) copy-start(f32[2,512]{1,0:T(2,128)} %get-tuple-element.71.refs_20_) | copy-start | bytes 12292

commit v2 on v1

--- a/solution.py
+++ b/solution.py
@@ -60,6 +60,7 @@
     twin_family = [dev(dz, cx, dy) for dz, dy in offsets]
     core_peer = dev(0, cc, 0)
     x_peer = dev(0, cx, 0)
+    diagonal = dev(0, cx + 1 - 2 * k, 0)
 
     def rows(h):
         return pl.ds(pl.multiple_of(h * R, 16), R)
@@ -79,14 +80,15 @@
     sends = []
     used = [0]
 
-    def make(src, dst, target):
-        i = used[0]
-        used[0] += 1
+    def make(src, dst, target, at=None):
+        if at is None:
+            at = (used[0], used[0])
+            used[0] += 1
         return pltpu.make_async_remote_copy(
             src_ref=src,
             dst_ref=dst,
-            send_sem=r["ssem"].at[i],
-            recv_sem=r["rsem"].at[i],
+            send_sem=r["ssem"].at[at[0]],
+            recv_sem=r["rsem"].at[at[1]],
             device_id=target,
             device_id_type=MESH,
         )
@@ -126,41 +128,52 @@
         wr, we = r["wr_full"], r["we_full"]
 
     barrier = pltpu.get_barrier_semaphore()
-    everyone = family + twin_family + [core_peer]
+    everyone = family + twin_family + [core_peer, diagonal]
     for target in everyone:
         pl.semaphore_signal(barrier, inc=1, device_id=target, device_id_type=MESH)
     pl.semaphore_wait(barrier, len(everyone))
+
+    near = [z + 1 - 2 * lax.rem(z, 2), jnp.where(z < 2, 2, 1), jnp.where(z < 2, 3, 0)]
 
     class Gather:
         def __init__(self, block):
             self.block = block
             self.here = block(owner)
-
-        def start(self):
-            self.along_z = [
-                (dz, send(self.here, self.here, dev(dz, None, 0))) for dz in range(1, H)
-            ]
-
-        def start_y(self):
-            self.along_y = [send(self.here, self.here, dev(0, None, dy)) for dy in range(1, D)]
-
-        def forward(self):
-            for dz, copy in self.along_z:
+            self.base = used[0]
+            used[0] += H
+            self.along_y = []
+
+        def send_z(self, rank):
+            target = {"height": near[rank], "chan": c, "dp": y}
+            copy = make(self.here, self.here, target, (self.base + rank, self.base + z))
+            copy.start()
+            sends.append(copy)
+
+        def send_y(self):
+            self.pass_on(self.here)
+
+        def pass_on(self, block):
+            self.along_y.append([send(block, block, dev(0, None, dy)) for dy in range(1, D)])
+
+        def forward(self, rank):
+            source = near[rank]
+            block = self.block(source * D + y)
+            make(block, block, dev(), (self.base, self.base + source)).wait_recv()
+            self.pass_on(block)
+            return source
+
+        def finish(self, number):
+            for copy in self.along_y[number]:
                 copy.wait_recv()
-                block = self.block(lax.rem(z - dz + H, H) * D + y)
-                for dy in range(1, D):
-                    self.along_y.append(send(block, block, dev(0, None, dy)))
-
-        def finish(self):
-            for copy in self.along_y:
-                copy.wait_recv()
 
     if own_gather:
         g_reduce, g_group, g_expand = Gather(reduce_block), Gather(group_block), Gather(expand_block)
-        g_reduce.start()
-        g_reduce.start_y()
-        g_group.start()
-        g_group.start_y()
+        for rank in range(3):
+            g_reduce.send_z(rank)
+        g_reduce.send_y()
+        for rank in range(3):
+            g_group.send_z(rank)
+        g_group.send_y()
     ct2, out2 = r["ct2"], r["out2"]
     ct_in = send(ct_ref.at[rows(1 - xp)], ct2.at[xp], x_peer)
     ct2[xp] = ct_ref[rows(xp), :]
@@ -168,7 +181,23 @@
     outer_in = send(out2.at[xp], out2.at[xp], x_peer)
     wep = r["wep"]
     twin_in = []
-    if not own_gather:
+
+    def twin(o):
+        twin_in.append(
+            send(expand_block(o), wep.at[:, pl.ds(pl.multiple_of(o * EB, 128), EB)], x_peer)
+        )
+
+    def twin_y(number, zz):
+        g_expand.finish(number)
+        for dy in range(1, D):
+            twin(zz * D + lax.rem(y + dy, D))
+
+    if own_gather:
+        g_expand.send_z(0)
+        g_expand.send_z(1)
+        g_expand.send_y()
+        twin(owner)
+    else:
         twin_in.append(send(we, wep, x_peer))
 
     def statistics(buf, position, targets, value):
@@ -195,13 +224,13 @@
         lax.fori_loop(0, 2, body, 0)
 
     if own_gather:
-        g_reduce.forward()
-        g_expand.start()
-        g_expand.start_y()
-        twin_in.append(send(g_expand.here, wep.at[:, pl.ds(pl.multiple_of(owner * EB, 128), EB)], x_peer))
-        g_group.forward()
+        for rank in range(3):
+            g_reduce.forward(rank)
         product([zz * D + y for zz in range(H)], True)
-        g_reduce.finish()
+        for rank in range(3):
+            g_group.forward(rank)
+        for number in range(4):
+            g_reduce.finish(number)
         for dy in range(1, D):
             product([zz * D + lax.rem(y + dy, D) for zz in range(H)], False)
     else:
@@ -230,7 +259,13 @@
 
     wall, wallt, gf = r["wall"], r["wallt"], r["gf"]
     if own_gather:
-        g_group.finish()
+        g_expand.send_z(2)
+        sources = [z] + [g_expand.forward(rank) for rank in range(2)]
+        for source in sources[1:]:
+            twin(source * D + y)
+        twin_y(0, z)
+        for number in range(4):
+            g_group.finish(number)
         for o in range(HD):
             gf[o * GB : (o + 1) * GB, :] = wg[o].astype(F32)[0:GB]
     else:
@@ -244,13 +279,6 @@
         return carry
 
     lax.fori_loop(0, 9, spread, 0)
-    if own_gather:
-        g_expand.forward()
-        for dz in range(1, H):
-            o = lax.rem(z - dz + H, H) * D + y
-            there = pl.ds(pl.multiple_of(o * EB, 128), EB)
-            twin_in.append(send(expand_block(o), wep.at[:, there], x_peer))
-
     mean1, inv1 = average_and_inverse(total(r["st1"], stat1))
     gain1, shift1 = inner_ref[0:1, :], inner_ref[1:2, :]
     slope1 = r["slope1"]
@@ -310,16 +338,16 @@
 
     second = r["second"]
     convolve(a1, wall, second, False)
+    if own_gather:
+        sources.append(g_expand.forward(2))
+        twin(sources[3] * D + y)
+        twin_y(1, sources[1])
+        twin_y(2, sources[2])
     halo1.arrived()
     convolve(a1, wall, second, True)
     stat2 = statistics(r["st2"], owner, family, moments(second))
     if own_gather:
-        g_expand.finish()
-        for dy in range(1, D):
-            for zz in range(H):
-                o = zz * D + lax.rem(y + dy, D)
-                there = pl.ds(pl.multiple_of(o * EB, 128), EB)
-                twin_in.append(send(expand_block(o), wep.at[:, there], x_peer))
+        twin_y(3, sources[3])
     mean2, inv2 = average_and_inverse(total(r["st2"], stat2))
     gain2, shift2 = inner_ref[2:3, :], inner_ref[3:4, :]
     a2, slope2 = r["a2"], r["slope2"]
@@ -373,6 +401,7 @@
 
         zero = jnp.zeros((1, OUT), F32)
         sums.append(lax.fori_loop(0, W, body, (zero, zero)))
+    r["tx"][...] = third[1 - xp].astype(BF)
     position = xp * HD + owner
     both = family + twin_family
     stat3 = statistics(
@@ -383,70 +412,190 @@
             [jnp.concatenate([s[i] for s in sums], axis=1) * okx for i in range(2)], axis=0
         ),
     )
+    cut = (W + 1) // 2
+    parts = [pl.ds(0, cut * N), pl.ds(cut * N, (W - cut) * N)]
+    tx_in = [send(r["tx"].at[parts[0]], r["tother"].at[parts[0]], x_peer)]
+    wrq = r["wrq"]
+
+    def mids(chan):
+        return pl.ds(pl.multiple_of(chan * MID, 128), MID)
+
+    wrq[:, mids(c)] = wr[quarter(xp, k), :]
+    wrq_in = [send(wr.at[quarter(xp, 1 - k), :], wrq.at[:, mids(c)], core_peer)]
+    share = OUT // 2
+
+    def send_wrq(n):
+        target, core = ((x_peer, k), (diagonal, 1 - k))[n // 2]
+        at = pl.ds(pl.multiple_of((2 * (1 - xp) + core) * OUT + n % 2 * share, 16), share)
+        there = wrq.at[pl.ds(n % 2 * share, share), mids(c)]
+        wrq_in.append(send(wr.at[at, :], there, target))
+
+    a2t = r["a2t"]
+    a2t[...] = a2[...].T
     ct_in.wait_recv()
     outer_in.wait_recv()
     mean3, inv3 = average_and_inverse(total(r["st3"], stat3))
-    dpre, boj = r["dpre"], r["boj"]
-    sums = []
+    dpre, dother, bo = r["dpre"], r["dother"], r["bo"]
+    mi3 = r["mi3"]
     for j in range(2):
         lanes = slice(j * OUT, (j + 1) * OUT)
-        m, iv = mean3[:, lanes], inv3[:, lanes]
+        mi3[j] = jnp.concatenate([mean3[:, lanes], inv3[:, lanes]], axis=0)
+
+    def outer_norm(j, h, values, grads, write, start=0, stop=W):
+        m, iv = mi3[j, 0:1, :], mi3[j, 1:2, :]
         g, s = out2[j, 0:1, :], out2[j, 1:2, :]
+        ok = valid(h)
 
         def body(w, carry):
             at = pl.ds(pl.multiple_of(w * N, 16), N)
-            n = (third[j, at, :] - m) * iv
-            third[j, at, :] = n
-            v = n * g + s + x_ref[tile(xp, w), quarter(j, k)].astype(F32)
+            n = (values[0](at) - m) * iv
+            values[1](at, n)
+            v = n * g + s + x_ref[tile(h, w), quarter(j, k)].astype(F32)
             q = jax.nn.sigmoid(v)
-            boj[j, at, :] = (v * q * okx).astype(BF)
-            d = ct2[j, at, :].astype(F32) * okx * (q * (1.0 + v * (1.0 - q)))
-            dpre[j, at, :] = d
+            if write:
+                bo[tile(h, w), :] = (v * q * ok).astype(BF)
+            d = grads[0](at, w) * ok * (q * (1.0 + v * (1.0 - q)))
+            grads[1](at, d)
             return carry[0] + jnp.sum(d, axis=0, keepdims=True), carry[1] + jnp.sum(
                 d * n, axis=0, keepdims=True
             )
 
         zero = jnp.zeros((1, OUT), F32)
-        sums.append(lax.fori_loop(0, W, body, (zero, zero)))
-    stat3b = statistics(
-        r["st3b"],
-        position,
-        both,
-        jnp.concatenate(
-            [jnp.concatenate([s[i] for s in sums], axis=1) for i in range(2)], axis=0
-        ),
-    )
-    a2t = r["a2t"]
-    a2t[...] = a2[...].T
-    total3 = total(r["st3b"], stat3b)
+        return lax.fori_loop(start, stop, body, (zero, zero))
+
+    def third_access(j):
+        def get(at):
+            return third[j, at, :]
+
+        def put(at, n):
+            third[j, at, :] = n
+
+        def get_ct(at, w):
+            return ct2[j, at, :].astype(F32)
+
+        def put_d(at, d):
+            dpre[j, at, :] = d
+
+        return (get, put), (get_ct, put_d)
+
+    st3b = r["st3b"]
+    pair = r["pair"]
+    for j, write in ((xp, True), (1 - xp, False)):
+        pair[j] = jnp.concatenate(outer_norm(j, xp, *third_access(j), write), axis=0)
+    stat3b = statistics(st3b, position, both, jnp.concatenate([pair[0], pair[1]], axis=1))
+
+    tx_in.append(send(r["tx"].at[parts[1]], r["tother"].at[parts[1]], x_peer))
+    send_wrq(0)
+    tx_in[0].wait_recv()
+    nother = r["nother"]
+
+    def get_other(at):
+        return r["tother"][at, :].astype(F32)
+
+    def put_other(at, n):
+        nother[at, :] = n
+
+    def get_ct_other(at, w):
+        return ct_ref[tile(1 - xp, w), :].astype(F32)
+
+    def put_d_other(at, d):
+        dother[at, :] = d
+
+    other_row = ((get_other, put_other), (get_ct_other, put_d_other), True)
+    outer_norm(xp, 1 - xp, *other_row, 0, cut)
+    total3 = total(st3b, stat3b)
     r["tot3"][...] = total3
-    piece = r["piece"]
-    core_in = []
     for j in range(2):
         lanes = slice(j * OUT, (j + 1) * OUT)
-        factor = out2[j, 0:1, :] * inv3[:, lanes] * okx
-        sh = total3[0:1, lanes] / pixels
-        ga = total3[1:2, lanes] / pixels
+        pair[j] = total3[:, lanes] / pixels
+    piece = r["piece"]
+
+    def back_three(j, h, upstream, normed):
+        factor = out2[j, 0:1, :] * mi3[j, 1:2, :] * valid(h)
+        sh, ga = pair[j, 0:1, :], pair[j, 1:2, :]
 
         def body(w, carry):
             at = pl.ds(pl.multiple_of(w * N, 16), N)
-            v = factor * (dpre[j, at, :] - sh - third[j, at, :] * ga)
-            piece[tile(xp, w), quarter(j, k)] = v.astype(BF)
+            v = factor * (upstream(at) - sh - normed(at) * ga)
+            piece[tile(h, w), quarter(j, k)] = v.astype(BF)
             return carry
 
         lax.fori_loop(0, W, body, 0)
-        part = piece.at[rows(xp), quarter(j, k)]
-        core_in.append(send(part, part, core_peer))
+        part = piece.at[rows(h), quarter(j, k)]
+        return send(part, part, core_peer)
+
+    core_in = [
+        back_three(j, xp, lambda at, j=j: dpre[j, at, :], lambda at, j=j: third[j, at, :])
+        for j in range(2)
+    ]
     for copy in core_in:
         copy.wait_recv()
     agrad = r["agrad"]
     r["agsend"][...] = dot_nt(piece[rows(xp), :], wep[...]).astype(BF)
     ag_in = send(r["agsend"], r["agrecv"], x_peer)
-    piece_in = []
-    for j in range(2):
-        part = piece.at[rows(xp), quarter(j, k)]
-        piece_in.append(send(part, part, x_peer))
+    part = piece.at[rows(xp), quarter(xp, k)]
+    piece_in = send(part, part, x_peer)
+    for n in range(1, 4):
+        send_wrq(n)
     agrad[rows(xp), :] = dot_nt(piece[rows(xp), :], we[...])
+    tx_in[1].wait_recv()
+    outer_norm(xp, 1 - xp, *other_row, cut, W)
+    core_other = back_three(xp, 1 - xp, lambda at: dother[at, :], lambda at: nother[at, :])
+
+    class Scatter:
+        def __init__(self, name, block):
+            self.block = block
+            self.ys, self.yr = r[name + "_ys"], r[name + "_yr"]
+            self.zs, self.zr = r[name + "_zs"], r[name + "_zr"]
+            self.own = r[name + "_own"]
+            self.along_y, self.along_z = {}, []
+            self.base = used[0]
+            used[0] += H
+
+        def start(self, targets):
+            for slot, zi in targets:
+                self.along_y[slot] = []
+                for dy in range(1, D):
+                    n = (dy - 1) * H + slot
+                    self.ys[n] = self.block(zi * D + lax.rem(y + dy, D)).astype(BF)
+                    self.along_y[slot].append(
+                        (n, send(self.ys.at[n], self.yr.at[n], dev(0, None, dy)))
+                    )
+
+        def middle(self, targets):
+            for slot, zi in targets:
+                value = self.block(zi * D + y)
+                for n, copy in self.along_y[slot]:
+                    copy.wait_recv()
+                    value = value + self.yr[n].astype(F32)
+                other = zi != z
+
+                @pl.when(jnp.logical_not(other))
+                def keep():
+                    self.own[...] = value
+
+                self.zs[slot] = value.astype(BF)
+                target = {"height": zi, "chan": c, "dp": y}
+                at = (self.base + slot, self.base + z)
+                copy = make(self.zs.at[slot], self.zr.at[z], target, at)
+                pl.when(other)(copy.start)
+                self.along_z.append((other, copy))
+
+        def finish(self):
+            value = self.own[...]
+            for dz in range(1, H):
+                s = lax.rem(z + dz, H)
+                at = (self.base, self.base + s)
+                make(self.zs.at[0], self.zr.at[s], dev(dz), at).wait_recv()
+                value = value + self.zr[s].astype(F32)
+            return value
+
+        def sent(self):
+            for other, copy in self.along_z:
+                pl.when(other)(copy.wait_send)
+
+    def wide(left_ref, right_ref, o):
+        return dot(left_ref[...], right_ref[:, pl.ds(pl.multiple_of(o * EB, 128), EB)])
 
     def slope_two(h, received, carry):
         def body(w, carry):
@@ -464,10 +613,18 @@
 
     zero = jnp.zeros((1, MID), F32)
     carry = slope_two(xp, False, (zero, zero))
+    half = H // 2
+    early = [(i, xp * half + i) for i in range(half)]
+    late = [(half + i, (1 - xp) * half + i) for i in range(half)]
+    around = [(0, lax.rem(z + 2, 4)), (1, 3 - z), (2, near[0]), (3, z)]
+    if own_gather:
+        s_expand = Scatter("eg", lambda o: wide(a2t, piece, o))
     ag_in.wait_recv()
     carry = slope_two(1 - xp, True, carry)
     stat2b = statistics(r["st2b"], owner, family, jnp.concatenate(carry, axis=0))
-    bo_in = send(boj.at[1 - xp], r["borecv"], x_peer)
+    if own_gather:
+        core_other.wait_recv()
+        s_expand.start(early)
     total2 = total(r["st2b"], stat2b)
     b2n = r["b2n"]
 
@@ -492,6 +649,26 @@
     convolve(b2, wallt, back1, False)
     b2t = r["b2t"]
     b2t[...] = b2n[...].T
+    ggf = r["ggf"]
+    fold = jnp.where(
+        jnp.bitwise_and(lax.broadcasted_iota(jnp.int32, (GROUP, MID), 1), GROUP - 1)
+        == lax.broadcasted_iota(jnp.int32, (GROUP, MID), 0),
+        1.0,
+        0.0,
+    ).astype(BF)
+
+    def group_grad(t, carry):
+        kr, kc = lax.div(t, 3), lax.rem(t, 3)
+        left = jnp.concatenate([a1[slab(kr, kc, R), :], a1[slab(kr + 1, kc, R), :]], axis=0)
+        turned = jnp.where(block_diagonal, dot(b2t[...], left), 0.0).astype(BF)
+        ggf[pl.ds(pl.multiple_of(t * GROUP, 8), GROUP), :] = dot_nt(fold, turned)
+        return carry
+
+    lax.fori_loop(0, 9, group_grad, 0)
+
+    piece_in.wait_recv()
+    part = piece.at[rows(1 - xp), quarter(1 - xp, k)]
+    core_last = send(part, part, core_peer)
     halo2.arrived()
     convolve(b2, wallt, back1, True)
 
@@ -508,149 +685,98 @@
     carry = lax.fori_loop(0, 2 * W, slope_one, (zero, zero))
     stat1b = statistics(r["st1b"], owner, family, jnp.concatenate(carry, axis=0))
 
-    core_in = []
-    for j in range(2):
-        piece_in[j].wait_recv()
-        part = piece.at[rows(1 - xp), quarter(j, k)]
-        core_in.append(send(part, part, core_peer))
-    ggf = r["ggf"]
-    fold = jnp.where(
-        jnp.bitwise_and(lax.broadcasted_iota(jnp.int32, (GROUP, MID), 1), GROUP - 1)
-        == lax.broadcasted_iota(jnp.int32, (GROUP, MID), 0),
-        1.0,
-        0.0,
-    ).astype(BF)
-
-    def group_grad(t, carry):
-        kr, kc = lax.div(t, 3), lax.rem(t, 3)
-        left = jnp.concatenate([a1[slab(kr, kc, R), :], a1[slab(kr + 1, kc, R), :]], axis=0)
-        turned = jnp.where(block_diagonal, dot(b2t[...], left), 0.0).astype(BF)
-        ggf[pl.ds(pl.multiple_of(t * GROUP, 8), GROUP), :] = dot_nt(fold, turned)
-        return carry
-
-    lax.fori_loop(0, 9, group_grad, 0)
-
-    class Scatter:
-        def __init__(self, name, block):
-            self.block = block
-            self.ys, self.yr = r[name + "_ys"], r[name + "_yr"]
-            self.zs, self.zr = r[name + "_zs"], r[name + "_zr"]
-
-        def start(self):
-            self.along_y = []
-            for dz in list(range(1, H)) + [0]:
-                zi = lax.rem(z + dz, H)
-                for dy in range(1, D):
-                    n = (dy - 1) * H + dz
-                    self.ys[n] = self.block(zi * D + lax.rem(y + dy, D)).astype(BF)
-                    self.along_y.append((dz, n, send(self.ys.at[n], self.yr.at[n], dev(0, None, dy))))
-
-        def middle(self):
-            self.along_z = []
-            for dz in list(range(1, H)) + [0]:
-                value = self.block(lax.rem(z + dz, H) * D + y)
-                for at, n, copy in self.along_y:
-                    if at == dz:
-                        copy.wait_recv()
-                        value = value + self.yr[n].astype(F32)
-                if dz:
-                    self.zs[dz - 1] = value.astype(BF)
-                    self.along_z.append(send(self.zs.at[dz - 1], self.zr.at[dz - 1], dev(dz, None, 0)))
-                else:
-                    self.own = value
-
-        def finish(self):
-            value = self.own
-            for i, copy in enumerate(self.along_z):
-                copy.wait_recv()
-                value = value + self.zr[i].astype(F32)
-            return value
-
-    def wide(left_ref, right_ref, o):
-        return dot(left_ref[...], right_ref[:, pl.ds(pl.multiple_of(o * EB, 128), EB)])
-
-    for copy in core_in:
-        copy.wait_recv()
-    if own_gather:
-        def group_part(o):
-            return r["ggs"][o].astype(F32)
-
+    core_last.wait_recv()
+    if not own_gather:
+        core_other.wait_recv()
+    if own_gather:
+        s_expand.middle(early)
+        s_expand.start(late)
         for o in range(HD):
             r["ggs"][o] = jnp.concatenate(
                 [ggf[o * GB : (o + 1) * GB, :], jnp.zeros((SLOT - GB, MID), F32)], axis=0
             )
-        s_group = Scatter("gg", group_part)
-        s_expand = Scatter("eg", lambda o: wide(a2t, piece, o))
-        s_group.start()
-        s_expand.start()
+        s_group = Scatter("gg", lambda o: r["ggs"][o])
+        s_group.start(around)
     else:
         r["group_out"][...] = ggf[...].astype(BF)
         r["expand_out"][...] = dot(a2t[...], piece[...]).astype(BF)
 
     total1 = total(r["st1b"], stat1b)
-    b1 = r["b1"]
-
-    def norm_one(i, carry):
-        h, w = lax.div(i, W), lax.rem(i, W)
+    b1, ball = r["b1"], r["ball"]
+
+    def norm_one(h):
         factor = gain1 * inv1 * valid(h)
         sh, ga = total1[0:1] / pixels, total1[1:2] / pixels
-        v = factor * (back1[tile(h, w), :] - sh - first[tile(h, w), :] * ga)
-        b1[tile(h, w), :] = v.astype(BF)
-        return carry
-
-    lax.fori_loop(0, 2 * W, norm_one, 0)
-
-    ipsend, iprecv, xsend, xrecv = r["ipsend"], r["iprecv"], r["xsend"], r["xrecv"]
-    ig = r["ig"]
-
-    def share(j, core, h):
-        return dot_nt(b1[rows(h), :], wr[quarter(j, core), :])
-
-    core_in = []
-    for n, j in enumerate((1 - xp, xp)):
-        for h in range(2):
-            ipsend[n, rows(h), :] = share(j, 1 - k, h).astype(BF)
-            core_in.append(send(ipsend.at[n, rows(h)], iprecv.at[n, rows(h)], core_peer))
-        if n == 0:
-            x_in = []
-            for h in range(2):
-                part = share(j, k, h)
-                here = jnp.where(xp == h, 1.0, 0.0).astype(F32)
-                core_in[h].wait_recv()
-                part = part + iprecv[0, rows(h), :].astype(F32) + here * dpre[j]
-                xsend[rows(h), :] = part.astype(BF)
-                x_in.append(send(xsend.at[rows(h)], xrecv.at[rows(h)], x_peer))
+
+        def body(w, carry):
+            v = factor * (back1[tile(h, w), :] - sh - first[tile(h, w), :] * ga)
+            v = v.astype(BF)
+            b1[tile(h, w), :] = v
+            ball[tile(h, w), mids(c)] = v
+            return carry
+
+        lax.fori_loop(0, W, body, 0)
+
+    ball_x, ball_core, ball_far = [], [], []
+    for h in range(2):
+        norm_one(h)
+        part = ball.at[rows(h), mids(c)]
+        ball_x.append(send(part, part, x_peer))
+        ball_core.append(send(part, part, core_peer))
+
+    def forward_ball(h):
+        ball_x[h].wait_recv()
+        part = ball.at[rows(h), mids(cx)]
+        ball_far.append(send(part, part, core_peer))
+
     b1t = r["b1t"]
     b1t[...] = b1[...].T
     if own_gather:
         s_reduce = Scatter("rg", lambda o: wide(b1t, x_ref, o))
-        s_group.middle()
-        s_reduce.start()
-        s_expand.middle()
+        s_reduce.start(around)
+        s_expand.middle(late)
+        s_group.middle(around)
+        s_reduce.middle(around[0:1])
+        forward_ball(0)
+        s_reduce.middle(around[1:2])
+        forward_ball(1)
+        s_reduce.middle(around[2:3])
     else:
+        forward_ball(0)
+        forward_ball(1)
         r["reduce_out"][...] = dot(b1t[...], x_ref[...]).astype(BF)
-    for h in range(2):
-        part = share(xp, k, h)
-        here = jnp.where(xp == h, 1.0, 0.0).astype(F32)
-        core_in[2 + h].wait_recv()
-        ig[rows(h), :] = part + iprecv[1, rows(h), :].astype(F32) + here * dpre[xp]
+    ig = r["ig"]
+
+    def chip_mids(n):
+        return pl.ds(pl.multiple_of(n * 2 * MID, 128), 2 * MID)
+
     r["inner_grad"][...] = jnp.concatenate(
         [total1[1:2], total1[0:1], total2[1:2], total2[0:1]], axis=0
     )
     mine = r["tot3"][:, pl.ds(pl.multiple_of(xp * OUT, 128), OUT)]
     r["outer_grad"][...] = jnp.concatenate([mine[1:2], mine[0:1]], axis=0)
-    bo = r["bo"]
-    bo[rows(xp), :] = boj[xp]
-    bo_in.wait_recv()
-    bo[rows(1 - xp), :] = r["borecv"][...]
-    if own_gather:
-        s_reduce.middle()
+    for copy in wrq_in:
+        copy.wait_recv()
+    ig[rows(xp), :] = dpre[xp]
+    ig[rows(1 - xp), :] = dother[...]
+
+    def input_part(h, n):
+        ig[rows(h), :] = ig[rows(h), :] + dot_nt(ball[rows(h), chip_mids(n)], wrq[:, chip_mids(n)])
+
+    for h in range(2):
+        ball_core[h].wait_recv()
+        input_part(h, xp)
+    if own_gather:
+        s_reduce.middle(around[3:])
+    for h in range(2):
+        ball_far[h].wait_recv()
+        input_part(h, 1 - xp)
+    if own_gather:
         r["group_out"][...] = s_group.finish()[0:GB]
         r["expand_out"][...] = s_expand.finish()
         r["reduce_out"][...] = s_reduce.finish().T
-    for h in range(2):
-        x_in[h].wait_recv()
-        ig[rows(h), :] = ig[rows(h), :] + xrecv[rows(h), :].astype(F32)
+        for scatter in (s_group, s_expand, s_reduce):
+            scatter.sent()
     for copy in sends:
         copy.wait_send()
     halo1.sent()
@@ -735,11 +861,17 @@
         a2t=((MID, 2 * R), BF),
         ax=((R, MID), BF),
         third=((2, R, OUT), F32),
+        tx=((R, OUT), BF),
+        tother=((R, OUT), BF),
+        nother=((R, OUT), F32),
+        dother=((R, OUT), F32),
+        mi3=((2, 2, OUT), F32),
+        pair=((2, 2, OUT), F32),
+        wrq=((OUT, 4 * MID), BF),
+        ball=((2 * R, 4 * MID), BF),
         tsend=((2, R, OUT), BF),
         trecv=((2, R, OUT), BF),
         dpre=((2, R, OUT), F32),
-        boj=((2, R, OUT), BF),
-        borecv=((R, OUT), BF),
         piece=((2 * R, CIN), BF),
         agrad=((2 * R, MID), F32),
         agsend=((R, MID), BF),
@@ -749,10 +881,6 @@
         second_back=((2 * R, MID), F32),
         b1=((2 * R, MID), BF),
         b1t=((MID, 2 * R), BF),
-        ipsend=((2, 2 * R, OUT), BF),
-        iprecv=((2, 2 * R, OUT), BF),
-        xsend=((2 * R, OUT), BF),
-        xrecv=((2 * R, OUT), BF),
     )
     if own_gather:
         ins.update(rm=reduce_master, gm=group_master, em=expand_master)
@@ -765,7 +893,8 @@
         )
         for name, shape in (("rg", (MID, RB)), ("eg", (MID, EB)), ("gg", (SLOT, MID))):
             scratch[name + "_ys"] = scratch[name + "_yr"] = (((D - 1) * H, *shape), BF)
-            scratch[name + "_zs"] = scratch[name + "_zr"] = ((H - 1, *shape), BF)
+            scratch[name + "_zs"] = scratch[name + "_zr"] = ((H, *shape), BF)
+            scratch[name + "_own"] = (shape, F32)
     else:
         both = ("height", "dp")
         ins.update(
@@ -782,16 +911,16 @@
     whole = pl.BlockSpec(memory_space=pltpu.VMEM)
     results = pl.pallas_call(
         functools.partial(block_kernel, names, dims),
-        out_shape=[jax.ShapeDtypeStruct(*v) for v in outs.values()],
+        out_shape=[pltpu.VMEM(*v) for v in outs.values()],
         in_specs=[whole] * len(ins),
         out_specs=[whole] * len(outs),
         scratch_shapes=[pltpu.VMEM(*v) for v in scratch.values()]
         + [pltpu.SemaphoreType.DMA((dims.get("semaphores", SEMAPHORES + 16 * D),))] * 2,
         compiler_params=pltpu.CompilerParams(
-            collective_id=0, has_side_effects=True, vmem_limit_bytes=56 << 20
+            collective_id=0, has_side_effects=True, vmem_limit_bytes=40 << 20
         ),
         name="block",
-    )(*ins.values())
+    )(*(pltpu.with_memory_space_constraint(v, pltpu.VMEM) for v in ins.values()))
     got = dict(zip(outs, results, strict=True))
     block_out = got["bo"].reshape(rows, W, N, OUT).transpose(2, 0, 1, 3)
     input_grad = got["ig"].reshape(rows, W, N, OUT).transpose(2, 0, 1, 3)

time: 155 us -> 135 us (0.87)
  Pallas kernels: 139 us -> 124 us
  local copies, waits for them, and re-layouts: 12.9 us -> 8.01 us
    pallas_call x1, Pallas kernels: 137 us -> 122 us  [local(): pl.pallas_call(functools.partial(block_kernel, names, dims), out_shape=[p...]
where the time goes in v2:
time: 135 us; the launch traced here: 134 us
  Pallas kernels  124 us (92%)
  local copies, waits for them, and re-layouts  8.01 us (6%)
    pallas_call x1, Pallas kernels, local(): pl.pallas_call(functools.partial(block_kernel, names, dims), out_shape=[p...  122 us
    transpose x1, local copies, waits for them, and re-layouts, local(): x = inputs.transpose(1, 2, 0, 3).reshape(rows * R, CIN)  3.01 us

profile of v2, /device:TPU:2, one launch (start us, length us, event | category | flops | bytes accessed | tf_op | source)
XLA Modules:
  0.0 133.6 jit_solution(18145549784568427879)
XLA Ops:
  0.7 1.2 copy.53
  1.9 0.0 copy-start
  1.9 0.0 copy-start.1
  1.9 0.0 copy-start.8
  1.9 0.0 copy-start.12
  1.9 0.0 copy-start.13
  1.9 3.0 %copy.52 = bf16[2,7,48,2048]{3,2,1,0:T(8,128)(2,1)S(1)} copy(bf16[2,7,48,2048]{3,0,1,2:T(2,128)(2,1)} %bitcast.16) | data formatting | bytes 5505024 | tf_op jit(solution)/shard_map/transpose | solution.py:830
  4.9 0.0 copy-done
  4.9 0.0 copy-done.1
  5.0 0.0 copy-done.8
  5.0 0.0 copy-done.12
  5.0 0.0 copy-done.13
  5.0 122.4 %block.1 = (bf16[672,512]{1,0:T(8,128)(2,1)S(1)}, f32[672,512]{1,0:T(8,128)S(1)}, f32[4,256]{1,0:T(4,128)S(1)}, f32[2,512]{1,0:T(2,128)S(1)}, f32[256,256]{1,0:T...) custom-call(bf16[672,2048]{1,0:T(8,128)(2,1)S(1)} %bitcast.12, bf16[672,512]{1,0:T(8,128)(2,1)S(1)} %bitcast.13, ...), custom_call_target="tpu_custom_call" | custom-call | tf_op jit(solution)/shard_map/block/pallas_call | solution.py:912
  127.4 0.0 copy-start.2
  127.4 0.0 copy-start.3
  127.4 0.0 copy-start.4
  127.5 0.0 copy-start.5
  127.5 0.0 copy-start.6
  127.5 0.0 copy-start.7
  127.5 0.0 copy-start.9
  127.5 0.0 copy-start.10
  127.5 0.0 copy-start.11
  127.5 0.0 copy-start.14
  127.5 0.0 copy-start.15
  127.6 0.0 copy-start.16
  127.6 0.0 copy-start.17
  127.6 0.0 copy-start.18
  127.6 0.0 copy-start.19
  127.6 1.6 %copy.59 = bf16[2,7,48,512]{3,0,1,2:T(2,128)(2,1)} copy(bf16[2,7,48,512]{3,2,1,0:T(8,128)(2,1)S(1)} %bitcast.15) | data formatting | bytes 1376256 | tf_op jit(solution)/shard_map/reshape | solution.py:925
  129.2 2.1 %copy.58 = f32[2,7,48,512]{3,0,1,2:T(2,128)} copy(f32[2,7,48,512]{3,2,1,0:T(8,128)S(1)} %bitcast.14) | data formatting | bytes 2752512 | tf_op jit(solution)/shard_map/reshape | solution.py:926
  131.3 0.0 copy-done.2
  131.4 2.0 %adamw.1 = (f32[256,256]{1,0:T(8,128)}, f32[256,256]{1,0:T(8,128)}, f32[256,256]{1,0:T(8,128)}, f32[256,256]{1,0:T(8,128)}, bf16[256,256]{1,0:T(8,128)(2,1)}, /*...) custom-call(f32[256,256]{1,0:T(8,128)S(1)} %get-tuple-element.67.ref, ...), custom_call_target="tpu_custom_call" | custom-call | tf_op jit(solution)/shard_map/adamw/pallas_call | solution.py:945
  (14 shorter events, 0.0 us)
Async XLA Ops:
  1.9 3.1 %copy-start = (f32[256,256]{1,0:T(8,128)S(1)}, f32[256,256]{1,0:T(8,128)}, u32[]{:S(2)}) copy-start(f32[256,256]{1,0:T(8,128)} %refs_1_.1) | copy-start | bytes 786436
  1.9 3.1 %copy-start.1 = (f32[256,256]{1,0:T(8,128)S(1)}, f32[256,256]{1,0:T(8,128)}, u32[]{:S(2)}) copy-start(f32[256,256]{1,0:T(8,128)} %refs_11_.1) | copy-start | bytes 786436
  1.9 3.1 %copy-start.8 = (f32[36,256]{1,0:T(8,128)S(1)}, f32[36,256]{1,0:T(8,128)}, u32[]{:S(2)}) copy-start(f32[36,256]{1,0:T(8,128)} %refs_6_.3) | copy-start | bytes 110596
  1.9 3.1 %copy-start.12 = (f32[4,256]{1,0:T(4,128)S(1)}, f32[4,256]{1,0:T(4,128)}, u32[]{:S(2)}) copy-start(f32[4,256]{1,0:T(4,128)} %refs_16_.1) | copy-start | bytes 12292
  1.9 3.1 %copy-start.13 = (f32[2,512]{1,0:T(2,128)S(1)}, f32[2,512]{1,0:T(2,128)}, u32[]{:S(2)}) copy-start(f32[2,512]{1,0:T(2,128)} %refs_21_.1) | copy-start | bytes 12292
  127.4 3.9 %copy-start.2 = (f32[256,256]{1,0:T(8,128)S(1)}, f32[256,256]{1,0:T(8,128)}, u32[]{:S(2)}) copy-start(f32[256,256]{1,0:T(8,128)} %refs_2_.3) | copy-start | bytes 786436
  127.4 3.9 %copy-start.3 = (f32[256,256]{1,0:T(8,128)S(1)}, f32[256,256]{1,0:T(8,128)}, u32[]{:S(2)}) copy-start(f32[256,256]{1,0:T(8,128)} %refs_3_.3) | copy-start | bytes 786436
  127.4 3.9 %copy-start.4 = (f32[256,256]{1,0:T(8,128)S(1)}, f32[256,256]{1,0:T(8,128)}, u32[]{:S(2)}) copy-start(f32[256,256]{1,0:T(8,128)} %refs_4_.3) | copy-start | bytes 786436
  127.5 3.9 %copy-start.5 = (f32[256,256]{1,0:T(8,128)S(1)}, f32[256,256]{1,0:T(8,128)}, u32[]{:S(2)}) copy-start(f32[256,256]{1,0:T(8,128)} %refs_12_.1) | copy-start | bytes 786436
  127.5 3.8 %copy-start.6 = (f32[256,256]{1,0:T(8,128)S(1)}, f32[256,256]{1,0:T(8,128)}, u32[]{:S(2)}) copy-start(f32[256,256]{1,0:T(8,128)} %refs_13_.1) | copy-start | bytes 786436
  127.5 3.8 %copy-start.7 = (f32[256,256]{1,0:T(8,128)S(1)}, f32[256,256]{1,0:T(8,128)}, u32[]{:S(2)}) copy-start(f32[256,256]{1,0:T(8,128)} %refs_14_.1) | copy-start | bytes 786436
  127.5 3.8 %copy-start.9 = (f32[36,256]{1,0:T(8,128)S(1)}, f32[36,256]{1,0:T(8,128)}, u32[]{:S(2)}) copy-start(f32[36,256]{1,0:T(8,128)} %refs_7_.1) | copy-start | bytes 110596
  127.5 3.8 %copy-start.10 = (f32[36,256]{1,0:T(8,128)S(1)}, f32[36,256]{1,0:T(8,128)}, u32[]{:S(2)}) copy-start(f32[36,256]{1,0:T(8,128)} %refs_8_.1) | copy-start | bytes 110596
  127.5 3.8 %copy-start.11 = (f32[36,256]{1,0:T(8,128)S(1)}, f32[36,256]{1,0:T(8,128)}, u32[]{:S(2)}) copy-start(f32[36,256]{1,0:T(8,128)} %refs_9_.1) | copy-start | bytes 110596
  127.5 3.8 %copy-start.14 = (f32[4,256]{1,0:T(4,128)S(1)}, f32[4,256]{1,0:T(4,128)}, u32[]{:S(2)}) copy-start(f32[4,256]{1,0:T(4,128)} %refs_17_.1) | copy-start | bytes 12292
  127.5 3.8 %copy-start.15 = (f32[4,256]{1,0:T(4,128)S(1)}, f32[4,256]{1,0:T(4,128)}, u32[]{:S(2)}) copy-start(f32[4,256]{1,0:T(4,128)} %refs_18_.1) | copy-start | bytes 12292
  127.6 3.8 %copy-start.16 = (f32[4,256]{1,0:T(4,128)S(1)}, f32[4,256]{1,0:T(4,128)}, u32[]{:S(2)}) copy-start(f32[4,256]{1,0:T(4,128)} %refs_19_.1) | copy-start | bytes 12292
  127.6 3.8 %copy-start.17 = (f32[2,512]{1,0:T(2,128)S(1)}, f32[2,512]{1,0:T(2,128)}, u32[]{:S(2)}) copy-start(f32[2,512]{1,0:T(2,128)} %refs_22_.1) | copy-start | bytes 12292
  127.6 3.8 %copy-start.18 = (f32[2,512]{1,0:T(2,128)S(1)}, f32[2,512]{1,0:T(2,128)}, u32[]{:S(2)}) copy-start(f32[2,512]{1,0:T(2,128)} %refs_23_.1) | copy-start | bytes 12292
  127.6 3.8 %copy-start.19 = (f32[2,512]{1,0:T(2,128)S(1)}, f32[2,512]{1,0:T(2,128)}, u32[]{:S(2)}) copy-start(f32[2,512]{1,0:T(2,128)} %refs_24_.1) | copy-start | bytes 12292

commit v3 on v2

--- a/solution.py
+++ b/solution.py
@@ -37,7 +37,13 @@
     PITCH = (W + 2) * N
     HD = H * D
     pixels = float(N * D * HEIGHT * W)
-    x_ref, ct_ref, inner_ref, outer_ref = r["x"], r["ct"], r["inner"], r["outer"]
+    x_ref, ct_ref, inner_ref, outer_ref = r["x"], r["ct"], r["inner_in"], r["outer_in"]
+    loads = {
+        name: pltpu.make_async_copy(r[name + "_hbm"], r[name + "_in"], r["lsem"].at[i])
+        for i, name in enumerate(dims["loads"])
+    }
+    for name in reversed(dims["loads"]):
+        loads[name].start()
 
     z = lax.axis_index("height")
     c = lax.axis_index("chan")
@@ -99,38 +105,38 @@
         sends.append(copy)
         return copy
 
-    a1, b2 = r["a1"], r["b2"]
-    a1[...] = jnp.zeros(a1.shape, BF)
-    b2[...] = jnp.zeros(b2.shape, BF)
-    lane_group = lax.shift_right_logical(lax.broadcasted_iota(jnp.int32, (MID, MID), 1), 5)
-    row_group = lax.shift_right_logical(lax.broadcasted_iota(jnp.int32, (MID, MID), 0), 5)
-    block_diagonal = lane_group == row_group
-    if own_gather:
-        wr, we, wg = r["wr"], r["we"], r["wg"]
-        RB, EB = r["rm"].shape[0], r["em"].shape[1]
-        GB = r["gm"].shape[0]
-
-        def reduce_block(o):
-            return wr.at[pl.ds(pl.multiple_of(o * RB, 16), RB), :]
-
-        def expand_block(o):
-            return we.at[:, pl.ds(pl.multiple_of(o * EB, 128), EB)]
-
-        def group_block(o):
-            return wg.at[o]
-
-        reduce_block(owner)[...] = r["rm"][...].astype(BF)
-        expand_block(owner)[...] = r["em"][...].astype(BF)
-        wg[owner] = jnp.concatenate(
-            [r["gm"][...], jnp.zeros((SLOT - GB, MID), F32)], axis=0
-        ).astype(BF)
-    else:
-        wr, we = r["wr_full"], r["we_full"]
-
     barrier = pltpu.get_barrier_semaphore()
     everyone = family + twin_family + [core_peer, diagonal]
     for target in everyone:
         pl.semaphore_signal(barrier, inc=1, device_id=target, device_id_type=MESH)
+    a1, b2 = r["a1"], r["b2"]
+    lane_group = lax.shift_right_logical(lax.broadcasted_iota(jnp.int32, (MID, MID), 1), 5)
+    row_group = lax.shift_right_logical(lax.broadcasted_iota(jnp.int32, (MID, MID), 0), 5)
+    block_diagonal = lane_group == row_group
+    if own_gather:
+        wr, we, wg = r["wr"], r["we"], r["wg"]
+        RB, EB = r["rm_in"].shape[0], r["em_in"].shape[1]
+        GB = r["gm_in"].shape[0]
+
+        def reduce_block(o):
+            return wr.at[pl.ds(pl.multiple_of(o * RB, 16), RB), :]
+
+        def expand_block(o):
+            return we.at[:, pl.ds(pl.multiple_of(o * EB, 128), EB)]
+
+        def group_block(o):
+            return wg.at[o]
+
+        for name in ("rm", "em", "gm"):
+            loads[name].wait()
+        reduce_block(owner)[...] = r["rm_in"][...].astype(BF)
+        expand_block(owner)[...] = r["em_in"][...].astype(BF)
+        wg[owner] = jnp.concatenate(
+            [r["gm_in"][...], jnp.zeros((SLOT - GB, MID), F32)], axis=0
+        ).astype(BF)
+    else:
+        wr, we = r["wr_full"], r["we_full"]
+
     pl.semaphore_wait(barrier, len(everyone))
 
     near = [z + 1 - 2 * lax.rem(z, 2), jnp.where(z < 2, 2, 1), jnp.where(z < 2, 3, 0)]
@@ -174,11 +180,6 @@
         for rank in range(3):
             g_group.send_z(rank)
         g_group.send_y()
-    ct2, out2 = r["ct2"], r["out2"]
-    ct_in = send(ct_ref.at[rows(1 - xp)], ct2.at[xp], x_peer)
-    ct2[xp] = ct_ref[rows(xp), :]
-    out2[xp] = outer_ref[...]
-    outer_in = send(out2.at[xp], out2.at[xp], x_peer)
     wep = r["wep"]
     twin_in = []
 
@@ -199,6 +200,29 @@
         twin(owner)
     else:
         twin_in.append(send(we, wep, x_peer))
+
+    def relay(source, target):
+        def body(w, carry):
+            turned = jnp.swapaxes(source[:, w], 0, 1)
+            for h in range(2):
+                target[tile(h, w), :] = turned[h]
+            return carry
+
+        lax.fori_loop(0, W, body, 0)
+
+    loads["inner"].wait()
+    loads["outer"].wait()
+    loads["ct"].wait()
+    relay(r["ct_in"], ct_ref)
+    ct2, out2 = r["ct2"], r["out2"]
+    ct_in = send(ct_ref.at[rows(1 - xp)], ct2.at[xp], x_peer)
+    ct2[xp] = ct_ref[rows(xp), :]
+    out2[xp] = outer_ref[...]
+    outer_in = send(out2.at[xp], out2.at[xp], x_peer)
+    a1[...] = jnp.zeros(a1.shape, BF)
+    b2[...] = jnp.zeros(b2.shape, BF)
+    loads["x"].wait()
+    relay(r["x_in"], x_ref)
 
     def statistics(buf, position, targets, value):
         buf[position] = value
@@ -224,11 +248,16 @@
         lax.fori_loop(0, 2, body, 0)
 
     if own_gather:
-        for rank in range(3):
-            g_reduce.forward(rank)
+        g_reduce.forward(0)
+        twin_y(0, z)
+        g_reduce.forward(1)
+        g_reduce.forward(2)
         product([zz * D + y for zz in range(H)], True)
         for rank in range(3):
             g_group.forward(rank)
+        sources = [z]
+        sources.append(g_expand.forward(0))
+        twin(sources[1] * D + y)
         for number in range(4):
             g_reduce.finish(number)
         for dy in range(1, D):
@@ -260,10 +289,8 @@
     wall, wallt, gf = r["wall"], r["wallt"], r["gf"]
     if own_gather:
         g_expand.send_z(2)
-        sources = [z] + [g_expand.forward(rank) for rank in range(2)]
-        for source in sources[1:]:
-            twin(source * D + y)
-        twin_y(0, z)
+        sources.append(g_expand.forward(1))
+        twin(sources[2] * D + y)
         for number in range(4):
             g_group.finish(number)
         for o in range(HD):
@@ -581,6 +608,43 @@
                 pl.when(other)(copy.start)
                 self.along_z.append((other, copy))
 
+        def fold(self, targets):
+            (slot, zi), (kept, zk) = targets
+            value = self.block(zi * D + y)
+            for n, copy in self.along_y[slot]:
+                copy.wait_recv()
+                value = value + self.yr[n].astype(F32)
+            self.zs[slot] = value.astype(BF)
+            target = {"height": near[0], "chan": c, "dp": y}
+            pair = send(self.zs.at[slot], self.zr.at[slot], target)
+
+            def rest():
+                value = self.block(zk * D + y)
+                for n, copy in self.along_y[kept]:
+                    copy.wait_recv()
+                    value = value + self.yr[n].astype(F32)
+                pair.wait_recv()
+                value = value + self.zr[slot].astype(F32)
+                other = zk != z
+
+                @pl.when(jnp.logical_not(other))
+                def keep():
+                    self.own[...] = value
+
+                self.zs[kept] = value.astype(BF)
+                target = {"height": lax.rem(z + 2, 4), "chan": c, "dp": y}
+                at = (self.base, self.base)
+                copy = make(self.zs.at[kept], self.zr.at[H], target, at)
+                pl.when(other)(copy.start)
+                self.along_z.append((other, copy))
+                self.last = copy
+
+            return rest
+
+        def finish_fold(self):
+            self.last.wait_recv()
+            return self.own[...] + self.zr[H].astype(F32)
+
         def finish(self):
             value = self.own[...]
             for dz in range(1, H):
@@ -614,8 +678,9 @@
     zero = jnp.zeros((1, MID), F32)
     carry = slope_two(xp, False, (zero, zero))
     half = H // 2
-    early = [(i, xp * half + i) for i in range(half)]
-    late = [(half + i, (1 - xp) * half + i) for i in range(half)]
+    parity = lax.rem(z, 2)
+    early = [(i, xp * half + lax.rem(parity + 1 + i, 2)) for i in range(half)]
+    late = [(half + i, (1 - xp) * half + lax.rem(parity + 1 + i, 2)) for i in range(half)]
     around = [(0, lax.rem(z + 2, 4)), (1, 3 - z), (2, near[0]), (3, z)]
     if own_gather:
         s_expand = Scatter("eg", lambda o: wide(a2t, piece, o))
@@ -625,6 +690,12 @@
     if own_gather:
         core_other.wait_recv()
         s_expand.start(early)
+
+    def turn(w, carry):
+        r["turned"][:, w] = jnp.swapaxes(jnp.stack([bo[tile(h, w), :] for h in range(2)]), 0, 1)
+        return carry
+
+    lax.fori_loop(0, W, turn, 0)
     total2 = total(r["st2b"], stat2b)
     b2n = r["b2n"]
 
@@ -666,6 +737,13 @@
 
     lax.fori_loop(0, 9, group_grad, 0)
 
+    if own_gather:
+        for o in range(HD):
+            r["ggs"][o] = jnp.concatenate(
+                [ggf[o * GB : (o + 1) * GB, :], jnp.zeros((SLOT - GB, MID), F32)], axis=0
+            )
+        s_group = Scatter("gg", lambda o: r["ggs"][o])
+        s_group.start(around)
     piece_in.wait_recv()
     part = piece.at[rows(1 - xp), quarter(1 - xp, k)]
     core_last = send(part, part, core_peer)
@@ -689,14 +767,8 @@
     if not own_gather:
         core_other.wait_recv()
     if own_gather:
-        s_expand.middle(early)
+        rest_early = s_expand.fold(early)
         s_expand.start(late)
-        for o in range(HD):
-            r["ggs"][o] = jnp.concatenate(
-                [ggf[o * GB : (o + 1) * GB, :], jnp.zeros((SLOT - GB, MID), F32)], axis=0
-            )
-        s_group = Scatter("gg", lambda o: r["ggs"][o])
-        s_group.start(around)
     else:
         r["group_out"][...] = ggf[...].astype(BF)
         r["expand_out"][...] = dot(a2t[...], piece[...]).astype(BF)
@@ -734,13 +806,15 @@
     if own_gather:
         s_reduce = Scatter("rg", lambda o: wide(b1t, x_ref, o))
         s_reduce.start(around)
-        s_expand.middle(late)
+        rest_early()
+        rest_late = s_expand.fold(late)
         s_group.middle(around)
         s_reduce.middle(around[0:1])
         forward_ball(0)
         s_reduce.middle(around[1:2])
         forward_ball(1)
         s_reduce.middle(around[2:3])
+        rest_late()
     else:
         forward_ball(0)
         forward_ball(1)
@@ -773,7 +847,7 @@
         input_part(h, 1 - xp)
     if own_gather:
         r["group_out"][...] = s_group.finish()[0:GB]
-        r["expand_out"][...] = s_expand.finish()
+        r["expand_out"][...] = s_expand.finish_fold()
         r["reduce_out"][...] = s_reduce.finish().T
         for scatter in (s_group, s_expand, s_reduce):
             scatter.sent()
@@ -793,8 +867,21 @@
     return (first_new, second_new, master_new, average_new)
 
 
-def adamw_kernel(*refs):
-    ins, outs = refs[:25], list(refs[25:])
+def last_kernel(*refs):
+    ig_ref, bo_ref = refs[:2]
+    ins, (bo_out, ig_out), outs = refs[2:27], refs[27:29], list(refs[29:-3])
+    turned, bo_sem, ig_sem = refs[-3:]
+    W = turned.shape[1]
+    bo_copy = pltpu.make_async_copy(bo_ref, bo_out, bo_sem)
+    bo_copy.start()
+
+    def body(w, carry):
+        turned[:, w] = jnp.swapaxes(ig_ref[:, w], 0, 1)
+        return carry
+
+    lax.fori_loop(0, W, body, 0)
+    ig_copy = pltpu.make_async_copy(turned, ig_out, ig_sem)
+    ig_copy.start()
     for n in range(5):
         gradient, master, one, two, average = (ref[...] for ref in ins[5 * n : 5 * n + 5])
         rate = CONV_RATE if n < 3 else NORM_RATE
@@ -802,10 +889,8 @@
         values = [gradient, first, second, new] + ([new.astype(BF)] if n < 3 else []) + [mean]
         for value in values:
             outs.pop(0)[...] = value
-
-
-def step_sizes(leaves):
-    return [jax.ShapeDtypeStruct(a.shape, a.dtype) for a in leaves]
+    bo_copy.wait()
+    ig_copy.wait()
 
 
 def local(
@@ -827,16 +912,19 @@
     own_gather = RB % 128 == 0 and EB % 128 == 0
     dims = dict(H=H, D=D, N=N, W=W, MID=MID, OUT=OUT, CIN=CIN, own_gather=own_gather)
 
-    x = inputs.transpose(1, 2, 0, 3).reshape(rows * R, CIN)
-    ct = cotangent.transpose(1, 2, 0, 3).reshape(rows * R, OUT)
-    ins = dict(x=x, ct=ct, inner=inner_master, outer=outer_master)
+    shards = dict(x=inputs.transpose(0, 2, 1, 3), ct=cotangent.transpose(0, 2, 1, 3))
+    shards.update(inner=inner_master, outer=outer_master)
+    ins = {}
     outs = dict(
-        bo=((rows * R, OUT), BF),
+        turned=((N, W, rows, OUT), BF),
         ig=((rows * R, OUT), F32),
         inner_grad=(inner_master.shape, F32),
         outer_grad=(outer_master.shape, F32),
     )
     scratch = dict(
+        x=((rows * R, CIN), BF),
+        bo=((rows * R, OUT), BF),
+        ct=((rows * R, OUT), BF),
         wep=((MID, CIN), BF),
         ct2=((2, R, OUT), BF),
         out2=((2, 2, OUT), F32),
@@ -883,7 +971,7 @@
         b1t=((MID, 2 * R), BF),
     )
     if own_gather:
-        ins.update(rm=reduce_master, gm=group_master, em=expand_master)
+        shards.update(rm=reduce_master, gm=group_master, em=expand_master)
         outs.update(
             reduce_out=((RB, MID), F32), group_out=((GB, MID), F32), expand_out=((MID, EB), F32)
         )
@@ -893,7 +981,7 @@
         )
         for name, shape in (("rg", (MID, RB)), ("eg", (MID, EB)), ("gg", (SLOT, MID))):
             scratch[name + "_ys"] = scratch[name + "_yr"] = (((D - 1) * H, *shape), BF)
-            scratch[name + "_zs"] = scratch[name + "_zr"] = ((H, *shape), BF)
+            scratch[name + "_zs"] = scratch[name + "_zr"] = ((H + 1, *shape), BF)
             scratch[name + "_own"] = (shape, F32)
     else:
         both = ("height", "dp")
@@ -907,23 +995,27 @@
             group_out=((9 * GROUP, MID), BF),
             expand_out=((MID, CIN), BF),
         )
-    names = [*ins, *outs, *scratch, "ssem", "rsem"]
+    dims["loads"] = list(shards)
+    scratch.update({name + "_in": (a.shape, a.dtype) for name, a in shards.items()})
+    names = [*(name + "_hbm" for name in shards), *ins, *outs, *scratch, "lsem", "ssem", "rsem"]
     whole = pl.BlockSpec(memory_space=pltpu.VMEM)
     results = pl.pallas_call(
         functools.partial(block_kernel, names, dims),
         out_shape=[pltpu.VMEM(*v) for v in outs.values()],
-        in_specs=[whole] * len(ins),
+        in_specs=[pl.BlockSpec(memory_space=pltpu.HBM)] * len(shards) + [whole] * len(ins),
         out_specs=[whole] * len(outs),
         scratch_shapes=[pltpu.VMEM(*v) for v in scratch.values()]
+        + [pltpu.SemaphoreType.DMA((len(shards),))]
         + [pltpu.SemaphoreType.DMA((dims.get("semaphores", SEMAPHORES + 16 * D),))] * 2,
         compiler_params=pltpu.CompilerParams(
-            collective_id=0, has_side_effects=True, vmem_limit_bytes=40 << 20
+            collective_id=0, has_side_effects=True, vmem_limit_bytes=48 << 20
         ),
         name="block",
-    )(*(pltpu.with_memory_space_constraint(v, pltpu.VMEM) for v in ins.values()))
+    )(
+        *(pltpu.with_memory_space_constraint(v, pltpu.HBM) for v in shards.values()),
+        *(pltpu.with_memory_space_constraint(v, pltpu.VMEM) for v in ins.values()),
+    )
     got = dict(zip(outs, results, strict=True))
-    block_out = got["bo"].reshape(rows, W, N, OUT).transpose(2, 0, 1, 3)
-    input_grad = got["ig"].reshape(rows, W, N, OUT).transpose(2, 0, 1, 3)
     reduce_grad, group_grad, expand_grad = got["reduce_out"], got["group_out"], got["expand_out"]
     if not own_gather:
         both = ("height", "dp")
@@ -937,20 +1029,30 @@
         (got["inner_grad"], inner_master, inner_first, inner_second, inner_average),
         (got["outer_grad"], outer_master, outer_first, outer_second, outer_average),
     )
-    shapes = []
+    shapes = [
+        jax.ShapeDtypeStruct((N, W, rows, OUT), BF),
+        jax.ShapeDtypeStruct((N, W, rows, OUT), F32),
+    ]
     for n, group in enumerate(groups):
         kinds = [F32] * 4 + ([BF] if n < 3 else []) + [F32]
         shapes += [jax.ShapeDtypeStruct(group[0].shape, kind) for kind in kinds]
-    flat = [a for group in groups for a in group]
+    flat = [got["ig"].reshape(rows, W, N, OUT), got["turned"]]
+    flat += [a for group in groups for a in group]
     news = pl.pallas_call(
-        adamw_kernel,
+        last_kernel,
         out_shape=shapes,
         in_specs=[whole] * len(flat),
-        out_specs=[whole] * len(shapes),
-        compiler_params=pltpu.CompilerParams(vmem_limit_bytes=32 << 20),
+        out_specs=[pl.BlockSpec(memory_space=pltpu.HBM)] * 2 + [whole] * (len(shapes) - 2),
+        scratch_shapes=[
+            pltpu.VMEM((N, W, rows, OUT), F32),
+            pltpu.SemaphoreType.DMA,
+            pltpu.SemaphoreType.DMA,
+        ],
+        compiler_params=pltpu.CompilerParams(vmem_limit_bytes=40 << 20),
         name="adamw",
     )(*flat)
-    return (block_out, input_grad, *news)
+    pixel_outs = (a.transpose(0, 2, 1, 3) for a in news[:2])
+    return (*pixel_outs, *news[2:])
 
 
 def solution(mesh):

time: 135 us -> 122 us (0.904)
  local copies, waits for them, and re-layouts: 8.01 us -> 0.08 us
  Pallas kernels: 124 us -> 120 us
    pallas_call x1, Pallas kernels: 122 us -> 117 us  [local(): pl.pallas_call(functools.partial(block_kernel, names, dims), out_shape=[p...]
    transpose x2 -> x0, local copies, waits for them, and re-layouts: 4.19 us -> none  [the longest x1 3.01 us: local(): x = inputs.transpose(1, 2, 0, 3).reshape(rows * R, CIN)]
    reshape x2 -> x0, local copies, waits for them, and re-layouts: 3.7 us -> none  [the longest x1 2.14 us: local(): input_grad = got['ig'].reshape(rows, W, N, OUT).transpose(2, 0, 1, 3)]
where the time goes in v3:
time: 122 us; the launch traced here: 121 us
  Pallas kernels  120 us (98%)
    pallas_call x1, Pallas kernels, local(): pl.pallas_call(functools.partial(block_kernel, names, dims), out_shape=[p...  117 us
    pallas_call x1, Pallas kernels, local(): pl.pallas_call(last_kernel, out_shape=shapes, in_specs=[whole] * len(flat...  3.09 us

profile of v3, /device:TPU:2, one launch (start us, length us, event | category | flops | bytes accessed | tf_op | source)
XLA Modules:
  0.0 121.4 jit_solution(10712452083741359796)
XLA Ops:
  0.7 0.0 copy-start
  0.7 0.0 copy-start.1
  0.7 0.0 copy-start.2
  0.7 0.0 copy-start.3
  0.7 0.0 copy-start.4
  0.7 0.0 copy-start.5
  0.7 0.0 copy-start.6
  0.7 0.0 copy-start.7
  0.8 0.0 copy-start.8
  0.8 0.0 copy-start.9
  0.8 0.0 copy-start.10
  0.8 0.0 copy-start.11
  0.8 0.0 copy-start.12
  0.8 0.0 copy-start.13
  0.8 0.0 copy-start.14
  0.8 0.0 copy-start.15
  0.8 0.0 copy-start.16
  0.8 0.0 copy-start.17
  0.9 0.0 copy-start.18
  0.9 0.0 copy-start.19
  0.9 117.0 %block.1 = (bf16[48,7,2,512]{3,2,1,0:T(2,128)(2,1)S(1)}, f32[672,512]{1,0:T(8,128)S(1)}, f32[4,256]{1,0:T(4,128)S(1)}, f32[2,512]{1,0:T(2,128)S(1)}, f32[256,256...) custom-call(bf16[48,7,2,2048]{3,2,1,0:T(2,128)(2,1)} %bitcast.6, bf16[48,7,2,512]{3,2,1,0:T(2,128)(2,1)} %bitcast.7, ...), custom_call_target="tpu_custom_call" | custom-call | tf_op jit(solution)/shard_map/block/pallas_call | solution.py:1002
  117.9 0.0 copy-done
  117.9 0.0 copy-done.1
  117.9 0.0 copy-done.2
  117.9 0.0 copy-done.3
  117.9 0.0 copy-done.4
  118.0 0.0 copy-done.5
  118.0 0.0 copy-done.6
  118.0 0.0 copy-done.7
  118.0 0.0 copy-done.8
  118.0 0.0 copy-done.9
  118.1 3.1 %adamw.1 = (bf16[48,7,2,512]{3,2,1,0:T(2,128)(2,1)}, f32[48,7,2,512]{3,2,1,0:T(2,128)}, f32[256,256]{1,0:T(8,128)}, f32[256,256]{1,0:T(8,128)}, f32[256,256]{1,0...) custom-call(f32[2,7,48,512]{3,2,1,0:T(8,128)S(1)} %bitcast.5, ...), custom_call_target="tpu_custom_call" | custom-call | tf_op jit(solution)/shard_map/adamw/pallas_call | solution.py:1041
  (10 shorter events, 0.0 us)
Async XLA Ops:
  0.7 117.2 %copy-start = (f32[256,256]{1,0:T(8,128)S(1)}, f32[256,256]{1,0:T(8,128)}, u32[]{:S(2)}) copy-start(f32[256,256]{1,0:T(8,128)} %refs_3_.3) | copy-start | bytes 786436
  0.7 117.2 %copy-start.1 = (f32[256,256]{1,0:T(8,128)S(1)}, f32[256,256]{1,0:T(8,128)}, u32[]{:S(2)}) copy-start(f32[256,256]{1,0:T(8,128)} %refs_13_.1) | copy-start | bytes 786436
  0.7 117.2 %copy-start.2 = (f32[256,256]{1,0:T(8,128)S(1)}, f32[256,256]{1,0:T(8,128)}, u32[]{:S(2)}) copy-start(f32[256,256]{1,0:T(8,128)} %refs_4_.3) | copy-start | bytes 786436
  0.7 117.2 %copy-start.3 = (f32[256,256]{1,0:T(8,128)S(1)}, f32[256,256]{1,0:T(8,128)}, u32[]{:S(2)}) copy-start(f32[256,256]{1,0:T(8,128)} %refs_5_.3) | copy-start | bytes 786436
  0.7 117.2 %copy-start.4 = (f32[256,256]{1,0:T(8,128)S(1)}, f32[256,256]{1,0:T(8,128)}, u32[]{:S(2)}) copy-start(f32[256,256]{1,0:T(8,128)} %refs_6_.3) | copy-start | bytes 786436
  0.7 117.2 %copy-start.5 = (f32[256,256]{1,0:T(8,128)S(1)}, f32[256,256]{1,0:T(8,128)}, u32[]{:S(2)}) copy-start(f32[256,256]{1,0:T(8,128)} %refs_14_.1) | copy-start | bytes 786436
  0.7 117.2 %copy-start.6 = (f32[256,256]{1,0:T(8,128)S(1)}, f32[256,256]{1,0:T(8,128)}, u32[]{:S(2)}) copy-start(f32[256,256]{1,0:T(8,128)} %refs_15_.1) | copy-start | bytes 786436
  0.7 117.2 %copy-start.7 = (f32[256,256]{1,0:T(8,128)S(1)}, f32[256,256]{1,0:T(8,128)}, u32[]{:S(2)}) copy-start(f32[256,256]{1,0:T(8,128)} %refs_16_.1) | copy-start | bytes 786436
  0.8 117.2 %copy-start.8 = (f32[36,256]{1,0:T(8,128)S(1)}, f32[36,256]{1,0:T(8,128)}, u32[]{:S(2)}) copy-start(f32[36,256]{1,0:T(8,128)} %refs_8_.1) | copy-start | bytes 110596
  0.8 117.2 %copy-start.9 = (f32[36,256]{1,0:T(8,128)S(1)}, f32[36,256]{1,0:T(8,128)}, u32[]{:S(2)}) copy-start(f32[36,256]{1,0:T(8,128)} %refs_9_.1) | copy-start | bytes 110596
  0.8 117.2 %copy-start.10 = (f32[36,256]{1,0:T(8,128)S(1)}, f32[36,256]{1,0:T(8,128)}, u32[]{:S(2)}) copy-start(f32[36,256]{1,0:T(8,128)} %refs_10_.1) | copy-start | bytes 110596
  0.8 117.2 %copy-start.11 = (f32[36,256]{1,0:T(8,128)S(1)}, f32[36,256]{1,0:T(8,128)}, u32[]{:S(2)}) copy-start(f32[36,256]{1,0:T(8,128)} %refs_11_.1) | copy-start | bytes 110596
  0.8 117.2 %copy-start.12 = (f32[4,256]{1,0:T(4,128)S(1)}, f32[4,256]{1,0:T(4,128)}, u32[]{:S(2)}) copy-start(f32[4,256]{1,0:T(4,128)} %refs_18_.1) | copy-start | bytes 12292
  0.8 117.2 %copy-start.13 = (f32[2,512]{1,0:T(2,128)S(1)}, f32[2,512]{1,0:T(2,128)}, u32[]{:S(2)}) copy-start(f32[2,512]{1,0:T(2,128)} %refs_23_.1) | copy-start | bytes 12292
  0.8 117.2 %copy-start.14 = (f32[4,256]{1,0:T(4,128)S(1)}, f32[4,256]{1,0:T(4,128)}, u32[]{:S(2)}) copy-start(f32[4,256]{1,0:T(4,128)} %refs_19_.1) | copy-start | bytes 12292
  0.8 117.2 %copy-start.15 = (f32[4,256]{1,0:T(4,128)S(1)}, f32[4,256]{1,0:T(4,128)}, u32[]{:S(2)}) copy-start(f32[4,256]{1,0:T(4,128)} %refs_20_.1) | copy-start | bytes 12292
  0.8 117.2 %copy-start.16 = (f32[4,256]{1,0:T(4,128)S(1)}, f32[4,256]{1,0:T(4,128)}, u32[]{:S(2)}) copy-start(f32[4,256]{1,0:T(4,128)} %refs_21_.1) | copy-start | bytes 12292
  0.8 117.2 %copy-start.17 = (f32[2,512]{1,0:T(2,128)S(1)}, f32[2,512]{1,0:T(2,128)}, u32[]{:S(2)}) copy-start(f32[2,512]{1,0:T(2,128)} %refs_24_.1) | copy-start | bytes 12292
  0.9 117.2 %copy-start.18 = (f32[2,512]{1,0:T(2,128)S(1)}, f32[2,512]{1,0:T(2,128)}, u32[]{:S(2)}) copy-start(f32[2,512]{1,0:T(2,128)} %refs_25_.1) | copy-start | bytes 12292
  0.9 117.2 %copy-start.19 = (f32[2,512]{1,0:T(2,128)S(1)}, f32[2,512]{1,0:T(2,128)}, u32[]{:S(2)}) copy-start(f32[2,512]{1,0:T(2,128)} %refs_26_.1) | copy-start | bytes 12292

commit v4 on v3

--- a/solution.py
+++ b/solution.py
@@ -173,10 +173,16 @@
                 copy.wait_recv()
 
     if own_gather:
-        g_reduce, g_group, g_expand = Gather(reduce_block), Gather(group_block), Gather(expand_block)
+        def reduce_part(n):
+            return lambda o: wr.at[pl.ds(pl.multiple_of(o * RB + n * (RB // 2), 16), RB // 2), :]
+
+        g_reduce = [Gather(reduce_part(n)) for n in range(2)]
+        g_group, g_expand = Gather(group_block), Gather(expand_block)
         for rank in range(3):
-            g_reduce.send_z(rank)
-        g_reduce.send_y()
+            for part in g_reduce:
+                part.send_z(rank)
+        for part in g_reduce:
+            part.send_y()
         for rank in range(3):
             g_group.send_z(rank)
         g_group.send_y()
@@ -248,10 +254,12 @@
         lax.fori_loop(0, 2, body, 0)
 
     if own_gather:
-        g_reduce.forward(0)
+        for part in g_reduce:
+            part.forward(0)
         twin_y(0, z)
-        g_reduce.forward(1)
-        g_reduce.forward(2)
+        for rank in (1, 2):
+            for part in g_reduce:
+                part.forward(rank)
         product([zz * D + y for zz in range(H)], True)
         for rank in range(3):
             g_group.forward(rank)
@@ -259,7 +267,8 @@
         sources.append(g_expand.forward(0))
         twin(sources[1] * D + y)
         for number in range(4):
-            g_reduce.finish(number)
+            for part in g_reduce:
+                part.finish(number)
         for dy in range(1, D):
             product([zz * D + lax.rem(y + dy, D) for zz in range(H)], False)
     else:
@@ -570,28 +579,31 @@
     core_other = back_three(xp, 1 - xp, lambda at: dother[at, :], lambda at: nother[at, :])
 
     class Scatter:
-        def __init__(self, name, block):
+        def __init__(self, name, block, parts=1):
             self.block = block
+            self.parts = parts
             self.ys, self.yr = r[name + "_ys"], r[name + "_yr"]
             self.zs, self.zr = r[name + "_zs"], r[name + "_zr"]
             self.own = r[name + "_own"]
             self.along_y, self.along_z = {}, []
+            self.pair, self.cross = {}, {}
             self.base = used[0]
-            used[0] += H
+            used[0] += H * parts
 
         def start(self, targets):
             for slot, zi in targets:
                 self.along_y[slot] = []
                 for dy in range(1, D):
-                    n = (dy - 1) * H + slot
-                    self.ys[n] = self.block(zi * D + lax.rem(y + dy, D)).astype(BF)
+                    n = (dy - 1) * H * self.parts + slot
+                    self.ys[n] = self.block(zi * D + lax.rem(y + dy, D), slot % self.parts).astype(BF)
                     self.along_y[slot].append(
                         (n, send(self.ys.at[n], self.yr.at[n], dev(0, None, dy)))
                     )
 
         def middle(self, targets):
             for slot, zi in targets:
-                value = self.block(zi * D + y)
+                part = slot % self.parts
+                value = self.block(zi * D + y, part)
                 for n, copy in self.along_y[slot]:
                     copy.wait_recv()
                     value = value + self.yr[n].astype(F32)
@@ -599,56 +611,88 @@
 
                 @pl.when(jnp.logical_not(other))
                 def keep():
-                    self.own[...] = value
+                    self.own[part] = value
 
                 self.zs[slot] = value.astype(BF)
                 target = {"height": zi, "chan": c, "dp": y}
-                at = (self.base + slot, self.base + z)
-                copy = make(self.zs.at[slot], self.zr.at[z], target, at)
+                here = z * self.parts + part
+                at = (self.base + slot, self.base + here)
+                copy = make(self.zs.at[slot], self.zr.at[here], target, at)
                 pl.when(other)(copy.start)
                 self.along_z.append((other, copy))
 
-        def fold(self, targets):
-            (slot, zi), (kept, zk) = targets
-            value = self.block(zi * D + y)
+        def fold(self, base, zone):
+            far, kept = zone + 1 - lax.rem(z, 2), zone + lax.rem(z, 2)
+
+            def received(zi):
+                value = self.block(zi * D + y, 0)
+                for dy in range(1, D):
+                    value = value + self.yr[(dy - 1) * H + base + lax.rem(zi - zone + k, 2)].astype(F32)
+                return value
+
+            for slot in (base, base + 1):
+                for n, copy in self.along_y[slot]:
+                    copy.wait_recv()
+            self.zs[base] = received(far).astype(BF)
+            target = {"height": near[0], "chan": c, "dp": y}
+            pair = send(self.zs.at[base], self.zr.at[base], target)
+
+            def rest():
+                value = received(kept)
+                pair.wait_recv()
+                value = value + self.zr[base].astype(F32)
+                other = kept != z
+
+                @pl.when(jnp.logical_not(other))
+                def keep():
+                    self.own[0] = value
+
+                self.zs[base + 1] = value.astype(BF)
+                target = {"height": lax.rem(z + 2, 4), "chan": c, "dp": y}
+                at = (self.base, self.base)
+                copy = make(self.zs.at[base + 1], self.zr.at[H], target, at)
+                pl.when(other)(copy.start)
+                self.along_z.append((other, copy))
+                self.last = copy
+
+            return rest
+
+        def summed_y(self, slot, zi):
+            part = slot % self.parts
+            value = self.block(zi * D + y, part)
             for n, copy in self.along_y[slot]:
                 copy.wait_recv()
                 value = value + self.yr[n].astype(F32)
+            return value
+
+        def to_near(self, slot, zi):
+            self.zs[slot] = self.summed_y(slot, zi).astype(BF)
+            target = {"height": near[0], "chan": c, "dp": y}
+            self.pair[slot] = send(self.zs.at[slot], self.zr.at[slot], target)
+
+        def from_near(self, slot):
+            self.pair[slot].wait_recv()
+            return self.zr[slot].astype(F32)
+
+        def across(self, slot, zi, pair):
+            value = self.summed_y(slot, zi) + self.from_near(pair)
             self.zs[slot] = value.astype(BF)
-            target = {"height": near[0], "chan": c, "dp": y}
-            pair = send(self.zs.at[slot], self.zr.at[slot], target)
-
-            def rest():
-                value = self.block(zk * D + y)
-                for n, copy in self.along_y[kept]:
-                    copy.wait_recv()
-                    value = value + self.yr[n].astype(F32)
-                pair.wait_recv()
-                value = value + self.zr[slot].astype(F32)
-                other = zk != z
-
-                @pl.when(jnp.logical_not(other))
-                def keep():
-                    self.own[...] = value
-
-                self.zs[kept] = value.astype(BF)
-                target = {"height": lax.rem(z + 2, 4), "chan": c, "dp": y}
-                at = (self.base, self.base)
-                copy = make(self.zs.at[kept], self.zr.at[H], target, at)
-                pl.when(other)(copy.start)
-                self.along_z.append((other, copy))
-                self.last = copy
-
-            return rest
+            target = {"height": lax.rem(z + 2, 4), "chan": c, "dp": y}
+            self.cross[slot] = send(self.zs.at[slot], self.zr.at[slot], target)
+
+        def whole_sum(self, slot, zi, pair, cross):
+            value = self.summed_y(slot, zi) + self.from_near(pair)
+            self.cross[cross].wait_recv()
+            return value + self.zr[cross].astype(F32)
 
         def finish_fold(self):
             self.last.wait_recv()
-            return self.own[...] + self.zr[H].astype(F32)
-
-        def finish(self):
-            value = self.own[...]
+            return self.own[0] + self.zr[H].astype(F32)
+
+        def finish(self, part=0):
+            value = self.own[part]
             for dz in range(1, H):
-                s = lax.rem(z + dz, H)
+                s = lax.rem(z + dz, H) * self.parts + part
                 at = (self.base, self.base + s)
                 make(self.zs.at[0], self.zr.at[s], dev(dz), at).wait_recv()
                 value = value + self.zr[s].astype(F32)
@@ -658,8 +702,10 @@
             for other, copy in self.along_z:
                 pl.when(other)(copy.wait_send)
 
-    def wide(left_ref, right_ref, o):
-        return dot(left_ref[...], right_ref[:, pl.ds(pl.multiple_of(o * EB, 128), EB)])
+    def wide(left_ref, right_ref, o, part, parts):
+        share = left_ref.shape[0] // parts
+        left = left_ref[part * share : (part + 1) * share, :]
+        return dot(left, right_ref[:, pl.ds(pl.multiple_of(o * EB, 128), EB)])
 
     def slope_two(h, received, carry):
         def body(w, carry):
@@ -675,27 +721,28 @@
 
         return lax.fori_loop(0, W, body, carry)
 
+    parity = lax.rem(z, 2)
+    zones = (2 * xp, 2 * (1 - xp))
+    early = [(0, zones[0] + k), (1, zones[0] + 1 - k)]
+    late = [(2, zones[1] + k), (3, zones[1] + 1 - k)]
+    around = [(0, lax.rem(z + 2, 4)), (1, 3 - z), (2, near[0]), (3, z)]
+    if own_gather:
+        s_expand = Scatter("eg", lambda o, part: wide(a2t, piece, o, part, 1))
+        core_other.wait_recv()
+        s_expand.start(early)
     zero = jnp.zeros((1, MID), F32)
     carry = slope_two(xp, False, (zero, zero))
-    half = H // 2
-    parity = lax.rem(z, 2)
-    early = [(i, xp * half + lax.rem(parity + 1 + i, 2)) for i in range(half)]
-    late = [(half + i, (1 - xp) * half + lax.rem(parity + 1 + i, 2)) for i in range(half)]
-    around = [(0, lax.rem(z + 2, 4)), (1, 3 - z), (2, near[0]), (3, z)]
-    if own_gather:
-        s_expand = Scatter("eg", lambda o: wide(a2t, piece, o))
     ag_in.wait_recv()
     carry = slope_two(1 - xp, True, carry)
     stat2b = statistics(r["st2b"], owner, family, jnp.concatenate(carry, axis=0))
-    if own_gather:
-        core_other.wait_recv()
-        s_expand.start(early)
 
     def turn(w, carry):
         r["turned"][:, w] = jnp.swapaxes(jnp.stack([bo[tile(h, w), :] for h in range(2)]), 0, 1)
         return carry
 
     lax.fori_loop(0, W, turn, 0)
+    if own_gather:
+        rest_early = s_expand.fold(0, zones[0])
     total2 = total(r["st2b"], stat2b)
     b2n = r["b2n"]
 
@@ -742,11 +789,11 @@
             r["ggs"][o] = jnp.concatenate(
                 [ggf[o * GB : (o + 1) * GB, :], jnp.zeros((SLOT - GB, MID), F32)], axis=0
             )
-        s_group = Scatter("gg", lambda o: r["ggs"][o])
-        s_group.start(around)
     piece_in.wait_recv()
     part = piece.at[rows(1 - xp), quarter(1 - xp, k)]
     core_last = send(part, part, core_peer)
+    if own_gather:
+        s_expand.start(late[:1])
     halo2.arrived()
     convolve(b2, wallt, back1, True)
 
@@ -767,8 +814,9 @@
     if not own_gather:
         core_other.wait_recv()
     if own_gather:
-        rest_early = s_expand.fold(early)
-        s_expand.start(late)
+        s_expand.start(late[1:])
+        s_group = Scatter("gg", lambda o, part: r["ggs"][o])
+        s_group.start(around)
     else:
         r["group_out"][...] = ggf[...].astype(BF)
         r["expand_out"][...] = dot(a2t[...], piece[...]).astype(BF)
@@ -804,17 +852,23 @@
     b1t = r["b1t"]
     b1t[...] = b1[...].T
     if own_gather:
-        s_reduce = Scatter("rg", lambda o: wide(b1t, x_ref, o))
-        s_reduce.start(around)
+        s_reduce = Scatter("rg", lambda o, part: wide(b1t, x_ref, o, part, 2), 2)
+        here, there = z - parity, lax.rem(z - parity + 2, 4)
+        ends = (there + 1 - parity, there + parity, here + 1 - parity, z)
+        halves = [(2 * slot + part, zi) for slot, zi in enumerate(ends) for part in range(2)]
+        s_reduce.start(halves)
         rest_early()
-        rest_late = s_expand.fold(late)
+        rest_late = s_expand.fold(2, zones[1])
         s_group.middle(around)
-        s_reduce.middle(around[0:1])
+        for half in halves[0:2]:
+            s_reduce.to_near(*half)
         forward_ball(0)
-        s_reduce.middle(around[1:2])
+        rest_late()
+        for half in halves[2:4]:
+            s_reduce.across(*half, half[0] - 2)
         forward_ball(1)
-        s_reduce.middle(around[2:3])
-        rest_late()
+        for half in halves[4:6]:
+            s_reduce.to_near(*half)
     else:
         forward_ball(0)
         forward_ball(1)
@@ -840,15 +894,16 @@
     for h in range(2):
         ball_core[h].wait_recv()
         input_part(h, xp)
-    if own_gather:
-        s_reduce.middle(around[3:])
     for h in range(2):
         ball_far[h].wait_recv()
         input_part(h, 1 - xp)
     if own_gather:
         r["group_out"][...] = s_group.finish()[0:GB]
         r["expand_out"][...] = s_expand.finish_fold()
-        r["reduce_out"][...] = s_reduce.finish().T
+        turned = jnp.concatenate(
+            [s_reduce.whole_sum(*half, half[0] - 2, half[0] - 4) for half in halves[6:8]], axis=0
+        )
+        r["reduce_out"][...] = turned.T
         for scatter in (s_group, s_expand, s_reduce):
             scatter.sent()
     for copy in sends:
@@ -979,10 +1034,13 @@
             wr=((CIN, MID), BF), we=((MID, CIN), BF), wg=((HD, SLOT, MID), BF),
             ggs=((HD, SLOT, MID), F32),
         )
-        for name, shape in (("rg", (MID, RB)), ("eg", (MID, EB)), ("gg", (SLOT, MID))):
-            scratch[name + "_ys"] = scratch[name + "_yr"] = (((D - 1) * H, *shape), BF)
-            scratch[name + "_zs"] = scratch[name + "_zr"] = ((H + 1, *shape), BF)
-            scratch[name + "_own"] = (shape, F32)
+        for name, n, shape in (
+            ("rg", 2, (MID // 2, RB)), ("eg", 1, (MID, EB)), ("gg", 1, (SLOT, MID))
+        ):
+            scratch[name + "_ys"] = scratch[name + "_yr"] = (((D - 1) * H * n, *shape), BF)
+            scratch[name + "_zs"] = ((H * n, *shape), BF)
+            scratch[name + "_zr"] = ((H * n + 1, *shape), BF)
+            scratch[name + "_own"] = ((n, *shape), F32)
     else:
         both = ("height", "dp")
         ins.update(

time: 122 us -> 118 us (0.967)
  Pallas kernels: 120 us -> 117 us
    pallas_call x1, Pallas kernels: 117 us -> 114 us  [local(): pl.pallas_call(functools.partial(block_kernel, names, dims), out_shape=[p...]
where the time goes in v4:
time: 118 us
  Pallas kernels  117 us (99%)
    pallas_call x1, Pallas kernels, local(): pl.pallas_call(functools.partial(block_kernel, names, dims), out_shape=[p...  114 us
    pallas_call x1, Pallas kernels, local(): pl.pallas_call(last_kernel, out_shape=shapes, in_specs=[whole] * len(flat...  3.09 us

profile of v4, /device:TPU:2, one launch (start us, length us, event | category | flops | bytes accessed | tf_op | source)
XLA Modules:
  0.0 118.2 jit_solution(8624733137947298885)
XLA Ops:
  0.7 0.0 copy-start
  0.7 0.0 copy-start.1
  0.7 0.0 copy-start.2
  0.7 0.0 copy-start.3
  0.7 0.0 copy-start.4
  0.7 0.0 copy-start.5
  0.7 0.0 copy-start.6
  0.7 0.0 copy-start.7
  0.8 0.0 copy-start.8
  0.8 0.0 copy-start.9
  0.8 0.0 copy-start.10
  0.8 0.0 copy-start.11
  0.8 0.0 copy-start.12
  0.8 0.0 copy-start.13
  0.8 0.0 copy-start.14
  0.8 0.0 copy-start.15
  0.8 0.0 copy-start.16
  0.8 0.0 copy-start.17
  0.9 0.0 copy-start.18
  0.9 0.0 copy-start.19
  0.9 113.9 %block.1 = (bf16[48,7,2,512]{3,2,1,0:T(2,128)(2,1)S(1)}, f32[672,512]{1,0:T(8,128)S(1)}, f32[4,256]{1,0:T(4,128)S(1)}, f32[2,512]{1,0:T(2,128)S(1)}, f32[256,256...) custom-call(bf16[48,7,2,2048]{3,2,1,0:T(2,128)(2,1)} %bitcast.6, bf16[48,7,2,512]{3,2,1,0:T(2,128)(2,1)} %bitcast.7, ...), custom_call_target="tpu_custom_call" | custom-call | tf_op jit(solution)/shard_map/block/pallas_call | solution.py:1060
  114.8 0.0 copy-done
  114.8 0.0 copy-done.1
  114.8 0.0 copy-done.2
  114.8 0.0 copy-done.3
  114.8 0.0 copy-done.4
  114.8 0.0 copy-done.5
  114.8 0.0 copy-done.6
  114.8 0.0 copy-done.7
  114.8 0.0 copy-done.8
  114.8 0.0 copy-done.9
  115.0 3.1 %adamw.1 = (bf16[48,7,2,512]{3,2,1,0:T(2,128)(2,1)}, f32[48,7,2,512]{3,2,1,0:T(2,128)}, f32[256,256]{1,0:T(8,128)}, f32[256,256]{1,0:T(8,128)}, f32[256,256]{1,0...) custom-call(f32[2,7,48,512]{3,2,1,0:T(8,128)S(1)} %bitcast.5, ...), custom_call_target="tpu_custom_call" | custom-call | tf_op jit(solution)/shard_map/adamw/pallas_call | solution.py:1099
  (10 shorter events, 0.0 us)
Async XLA Ops:
  0.7 114.1 %copy-start = (f32[256,256]{1,0:T(8,128)S(1)}, f32[256,256]{1,0:T(8,128)}, u32[]{:S(2)}) copy-start(f32[256,256]{1,0:T(8,128)} %refs_3_.3) | copy-start | bytes 786436
  0.7 114.1 %copy-start.1 = (f32[256,256]{1,0:T(8,128)S(1)}, f32[256,256]{1,0:T(8,128)}, u32[]{:S(2)}) copy-start(f32[256,256]{1,0:T(8,128)} %refs_13_.1) | copy-start | bytes 786436
  0.7 114.1 %copy-start.2 = (f32[256,256]{1,0:T(8,128)S(1)}, f32[256,256]{1,0:T(8,128)}, u32[]{:S(2)}) copy-start(f32[256,256]{1,0:T(8,128)} %refs_4_.3) | copy-start | bytes 786436
  0.7 114.1 %copy-start.3 = (f32[256,256]{1,0:T(8,128)S(1)}, f32[256,256]{1,0:T(8,128)}, u32[]{:S(2)}) copy-start(f32[256,256]{1,0:T(8,128)} %refs_5_.3) | copy-start | bytes 786436
  0.7 114.1 %copy-start.4 = (f32[256,256]{1,0:T(8,128)S(1)}, f32[256,256]{1,0:T(8,128)}, u32[]{:S(2)}) copy-start(f32[256,256]{1,0:T(8,128)} %refs_6_.3) | copy-start | bytes 786436
  0.7 114.1 %copy-start.5 = (f32[256,256]{1,0:T(8,128)S(1)}, f32[256,256]{1,0:T(8,128)}, u32[]{:S(2)}) copy-start(f32[256,256]{1,0:T(8,128)} %refs_14_.1) | copy-start | bytes 786436
  0.7 114.1 %copy-start.6 = (f32[256,256]{1,0:T(8,128)S(1)}, f32[256,256]{1,0:T(8,128)}, u32[]{:S(2)}) copy-start(f32[256,256]{1,0:T(8,128)} %refs_15_.1) | copy-start | bytes 786436
  0.7 114.1 %copy-start.7 = (f32[256,256]{1,0:T(8,128)S(1)}, f32[256,256]{1,0:T(8,128)}, u32[]{:S(2)}) copy-start(f32[256,256]{1,0:T(8,128)} %refs_16_.1) | copy-start | bytes 786436
  0.8 114.1 %copy-start.8 = (f32[36,256]{1,0:T(8,128)S(1)}, f32[36,256]{1,0:T(8,128)}, u32[]{:S(2)}) copy-start(f32[36,256]{1,0:T(8,128)} %refs_8_.1) | copy-start | bytes 110596
  0.8 114.1 %copy-start.9 = (f32[36,256]{1,0:T(8,128)S(1)}, f32[36,256]{1,0:T(8,128)}, u32[]{:S(2)}) copy-start(f32[36,256]{1,0:T(8,128)} %refs_9_.1) | copy-start | bytes 110596
  0.8 114.1 %copy-start.10 = (f32[36,256]{1,0:T(8,128)S(1)}, f32[36,256]{1,0:T(8,128)}, u32[]{:S(2)}) copy-start(f32[36,256]{1,0:T(8,128)} %refs_10_.1) | copy-start | bytes 110596
  0.8 114.1 %copy-start.11 = (f32[36,256]{1,0:T(8,128)S(1)}, f32[36,256]{1,0:T(8,128)}, u32[]{:S(2)}) copy-start(f32[36,256]{1,0:T(8,128)} %refs_11_.1) | copy-start | bytes 110596
  0.8 114.1 %copy-start.12 = (f32[4,256]{1,0:T(4,128)S(1)}, f32[4,256]{1,0:T(4,128)}, u32[]{:S(2)}) copy-start(f32[4,256]{1,0:T(4,128)} %refs_18_.1) | copy-start | bytes 12292
  0.8 114.1 %copy-start.13 = (f32[2,512]{1,0:T(2,128)S(1)}, f32[2,512]{1,0:T(2,128)}, u32[]{:S(2)}) copy-start(f32[2,512]{1,0:T(2,128)} %refs_23_.1) | copy-start | bytes 12292
  0.8 114.1 %copy-start.14 = (f32[4,256]{1,0:T(4,128)S(1)}, f32[4,256]{1,0:T(4,128)}, u32[]{:S(2)}) copy-start(f32[4,256]{1,0:T(4,128)} %refs_19_.1) | copy-start | bytes 12292
  0.8 114.1 %copy-start.15 = (f32[4,256]{1,0:T(4,128)S(1)}, f32[4,256]{1,0:T(4,128)}, u32[]{:S(2)}) copy-start(f32[4,256]{1,0:T(4,128)} %refs_20_.1) | copy-start | bytes 12292
  0.8 114.1 %copy-start.16 = (f32[4,256]{1,0:T(4,128)S(1)}, f32[4,256]{1,0:T(4,128)}, u32[]{:S(2)}) copy-start(f32[4,256]{1,0:T(4,128)} %refs_21_.1) | copy-start | bytes 12292
  0.8 114.1 %copy-start.17 = (f32[2,512]{1,0:T(2,128)S(1)}, f32[2,512]{1,0:T(2,128)}, u32[]{:S(2)}) copy-start(f32[2,512]{1,0:T(2,128)} %refs_24_.1) | copy-start | bytes 12292
  0.9 114.1 %copy-start.18 = (f32[2,512]{1,0:T(2,128)S(1)}, f32[2,512]{1,0:T(2,128)}, u32[]{:S(2)}) copy-start(f32[2,512]{1,0:T(2,128)} %refs_25_.1) | copy-start | bytes 12292
  0.9 114.1 %copy-start.19 = (f32[2,512]{1,0:T(2,128)S(1)}, f32[2,512]{1,0:T(2,128)}, u32[]{:S(2)}) copy-start(f32[2,512]{1,0:T(2,128)} %refs_26_.1) | copy-start | bytes 12292

commit v5 on v4

--- a/solution.py
+++ b/solution.py
@@ -127,13 +127,8 @@
         def group_block(o):
             return wg.at[o]
 
-        for name in ("rm", "em", "gm"):
-            loads[name].wait()
+        loads["rm"].wait()
         reduce_block(owner)[...] = r["rm_in"][...].astype(BF)
-        expand_block(owner)[...] = r["em_in"][...].astype(BF)
-        wg[owner] = jnp.concatenate(
-            [r["gm_in"][...], jnp.zeros((SLOT - GB, MID), F32)], axis=0
-        ).astype(BF)
     else:
         wr, we = r["wr_full"], r["we_full"]
 
@@ -183,6 +178,12 @@
                 part.send_z(rank)
         for part in g_reduce:
             part.send_y()
+        for name in ("gm", "em"):
+            loads[name].wait()
+        wg[owner] = jnp.concatenate(
+            [r["gm_in"][...], jnp.zeros((SLOT - GB, MID), F32)], axis=0
+        ).astype(BF)
+        expand_block(owner)[...] = r["em_in"][...].astype(BF)
         for rank in range(3):
             g_group.send_z(rank)
         g_group.send_y()
@@ -382,8 +383,6 @@
     halo1.arrived()
     convolve(a1, wall, second, True)
     stat2 = statistics(r["st2"], owner, family, moments(second))
-    if own_gather:
-        twin_y(3, sources[3])
     mean2, inv2 = average_and_inverse(total(r["st2"], stat2))
     gain2, shift2 = inner_ref[2:3, :], inner_ref[3:4, :]
     a2, slope2 = r["a2"], r["slope2"]
@@ -405,6 +404,8 @@
     activate_two(1 - xp)
     ax_in = send(a2.at[rows(1 - xp)], r["ax"], x_peer)
     activate_two(xp)
+    if own_gather:
+        twin_y(3, sources[3])
 
     for copy in twin_in:
         copy.wait_recv()
@@ -924,28 +925,31 @@
 
 def last_kernel(*refs):
     ig_ref, bo_ref = refs[:2]
-    ins, (bo_out, ig_out), outs = refs[2:27], refs[27:29], list(refs[29:-3])
-    turned, bo_sem, ig_sem = refs[-3:]
-    W = turned.shape[1]
-    bo_copy = pltpu.make_async_copy(bo_ref, bo_out, bo_sem)
-    bo_copy.start()
-
-    def body(w, carry):
-        turned[:, w] = jnp.swapaxes(ig_ref[:, w], 0, 1)
-        return carry
-
-    lax.fori_loop(0, W, body, 0)
-    ig_copy = pltpu.make_async_copy(turned, ig_out, ig_sem)
-    ig_copy.start()
-    for n in range(5):
+    ins, (bo_out, ig_out), outs = refs[2:27], refs[27:29], refs[29:57]
+    turned, held, sems = refs[57], refs[58:-1], refs[-1]
+    copies = []
+
+    def put(source, target):
+        copies.append(pltpu.make_async_copy(source, target, sems.at[len(copies)]))
+        copies[-1].start()
+
+    put(bo_ref, bo_out)
+    number = 0
+    for n in (0, 2, 1, 3, 4):
         gradient, master, one, two, average = (ref[...] for ref in ins[5 * n : 5 * n + 5])
         rate = CONV_RATE if n < 3 else NORM_RATE
         first, second, new, mean = adamw_step(master, gradient, one, two, average, rate)
-        values = [gradient, first, second, new] + ([new.astype(BF)] if n < 3 else []) + [mean]
-        for value in values:
-            outs.pop(0)[...] = value
-    bo_copy.wait()
-    ig_copy.wait()
+        values = [first, second, new] + ([new.astype(BF)] if n < 3 else []) + [mean]
+        number = 6 * n if n < 3 else 5 * n + 3
+        put(ins[5 * n], outs[number])
+        for at, value in enumerate(values, number + 1):
+            held[at][...] = value
+            put(held[at], outs[at])
+    for w in range(turned.shape[1]):
+        turned[:, w] = jnp.swapaxes(ig_ref[:, w], 0, 1)
+        put(turned.at[:, w], ig_out.at[:, w])
+    for copy in copies:
+        copy.wait()
 
 
 def local(
@@ -1026,7 +1030,7 @@
         b1t=((MID, 2 * R), BF),
     )
     if own_gather:
-        shards.update(rm=reduce_master, gm=group_master, em=expand_master)
+        shards.update(em=expand_master, gm=group_master, rm=reduce_master)
         outs.update(
             reduce_out=((RB, MID), F32), group_out=((GB, MID), F32), expand_out=((MID, EB), F32)
         )
@@ -1100,12 +1104,10 @@
         last_kernel,
         out_shape=shapes,
         in_specs=[whole] * len(flat),
-        out_specs=[pl.BlockSpec(memory_space=pltpu.HBM)] * 2 + [whole] * (len(shapes) - 2),
-        scratch_shapes=[
-            pltpu.VMEM((N, W, rows, OUT), F32),
-            pltpu.SemaphoreType.DMA,
-            pltpu.SemaphoreType.DMA,
-        ],
+        out_specs=[pl.BlockSpec(memory_space=pltpu.HBM)] * len(shapes),
+        scratch_shapes=[pltpu.VMEM((N, W, rows, OUT), F32)]
+        + [pltpu.VMEM(a.shape, a.dtype) for a in shapes[2:]]
+        + [pltpu.SemaphoreType.DMA((len(shapes) + W,))],
         compiler_params=pltpu.CompilerParams(vmem_limit_bytes=40 << 20),
         name="adamw",
     )(*flat)

time: 118 us -> 118 us (level)
  no operation moved by 1% of the time
where the time goes in v5:
time: 118 us
  Pallas kernels  116 us (98%)
    pallas_call x1, Pallas kernels, local(): pl.pallas_call(functools.partial(block_kernel, names, dims), out_shape=[p...  114 us
    pallas_call x1, Pallas kernels, local(): pl.pallas_call(last_kernel, out_shape=shapes, in_specs=[whole] * len(flat...  2.69 us

profile of v5, /device:TPU:2, one launch (start us, length us, event | category | flops | bytes accessed | tf_op | source)
XLA Modules:
  0.0 117.7 jit_solution(18131165823783520448)
XLA Ops:
  0.7 0.0 copy-start
  0.7 0.0 copy-start.1
  0.7 0.0 copy-start.2
  0.7 0.0 copy-start.3
  0.7 0.0 copy-start.4
  0.7 0.0 copy-start.5
  0.7 0.0 copy-start.6
  0.7 0.0 copy-start.7
  0.8 0.0 copy-start.8
  0.8 0.0 copy-start.9
  0.8 0.0 copy-start.10
  0.8 0.0 copy-start.11
  0.8 0.0 copy-start.12
  0.8 0.0 copy-start.13
  0.8 0.0 copy-start.14
  0.8 0.0 copy-start.15
  0.8 0.0 copy-start.16
  0.8 0.0 copy-start.17
  0.9 0.0 copy-start.18
  0.9 0.0 copy-start.19
  0.9 113.8 %block.1 = (bf16[48,7,2,512]{3,2,1,0:T(2,128)(2,1)S(1)}, f32[672,512]{1,0:T(8,128)S(1)}, f32[4,256]{1,0:T(4,128)S(1)}, f32[2,512]{1,0:T(2,128)S(1)}, f32[256,256...) custom-call(bf16[48,7,2,2048]{3,2,1,0:T(2,128)(2,1)} %bitcast.6, bf16[48,7,2,512]{3,2,1,0:T(2,128)(2,1)} %bitcast.7, ...), custom_call_target="tpu_custom_call" | custom-call | tf_op jit(solution)/shard_map/block/pallas_call | solution.py:1064
  114.7 0.0 copy-done
  114.7 0.0 copy-done.1
  114.7 0.0 copy-done.2
  114.7 0.0 copy-done.3
  114.7 0.0 copy-done.4
  114.7 0.0 copy-done.5
  114.7 0.0 copy-done.6
  114.7 0.0 copy-done.7
  114.7 0.0 copy-done.8
  114.7 0.0 copy-done.9
  114.9 2.7 %adamw.1 = (bf16[48,7,2,512]{3,2,1,0:T(2,128)(2,1)}, f32[48,7,2,512]{3,2,1,0:T(2,128)}, f32[256,256]{1,0:T(8,128)}, f32[256,256]{1,0:T(8,128)}, f32[256,256]{1,0...) custom-call(f32[2,7,48,512]{3,2,1,0:T(8,128)S(1)} %bitcast.5, ...), custom_call_target="tpu_custom_call" | custom-call | tf_op jit(solution)/shard_map/adamw/pallas_call | solution.py:1103
  (10 shorter events, 0.0 us)
Async XLA Ops:
  0.7 114.0 %copy-start = (f32[256,256]{1,0:T(8,128)S(1)}, f32[256,256]{1,0:T(8,128)}, u32[]{:S(2)}) copy-start(f32[256,256]{1,0:T(8,128)} %refs_13_.1) | copy-start | bytes 786436
  0.7 114.0 %copy-start.1 = (f32[256,256]{1,0:T(8,128)S(1)}, f32[256,256]{1,0:T(8,128)}, u32[]{:S(2)}) copy-start(f32[256,256]{1,0:T(8,128)} %refs_3_.3) | copy-start | bytes 786436
  0.7 114.0 %copy-start.2 = (f32[256,256]{1,0:T(8,128)S(1)}, f32[256,256]{1,0:T(8,128)}, u32[]{:S(2)}) copy-start(f32[256,256]{1,0:T(8,128)} %refs_4_.3) | copy-start | bytes 786436
  0.7 114.0 %copy-start.3 = (f32[256,256]{1,0:T(8,128)S(1)}, f32[256,256]{1,0:T(8,128)}, u32[]{:S(2)}) copy-start(f32[256,256]{1,0:T(8,128)} %refs_5_.3) | copy-start | bytes 786436
  0.7 114.0 %copy-start.4 = (f32[256,256]{1,0:T(8,128)S(1)}, f32[256,256]{1,0:T(8,128)}, u32[]{:S(2)}) copy-start(f32[256,256]{1,0:T(8,128)} %refs_6_.3) | copy-start | bytes 786436
  0.7 114.0 %copy-start.5 = (f32[256,256]{1,0:T(8,128)S(1)}, f32[256,256]{1,0:T(8,128)}, u32[]{:S(2)}) copy-start(f32[256,256]{1,0:T(8,128)} %refs_14_.1) | copy-start | bytes 786436
  0.7 114.0 %copy-start.6 = (f32[256,256]{1,0:T(8,128)S(1)}, f32[256,256]{1,0:T(8,128)}, u32[]{:S(2)}) copy-start(f32[256,256]{1,0:T(8,128)} %refs_15_.1) | copy-start | bytes 786436
  0.7 114.0 %copy-start.7 = (f32[256,256]{1,0:T(8,128)S(1)}, f32[256,256]{1,0:T(8,128)}, u32[]{:S(2)}) copy-start(f32[256,256]{1,0:T(8,128)} %refs_16_.1) | copy-start | bytes 786436
  0.8 114.0 %copy-start.8 = (f32[36,256]{1,0:T(8,128)S(1)}, f32[36,256]{1,0:T(8,128)}, u32[]{:S(2)}) copy-start(f32[36,256]{1,0:T(8,128)} %refs_8_.1) | copy-start | bytes 110596
  0.8 114.0 %copy-start.9 = (f32[36,256]{1,0:T(8,128)S(1)}, f32[36,256]{1,0:T(8,128)}, u32[]{:S(2)}) copy-start(f32[36,256]{1,0:T(8,128)} %refs_9_.1) | copy-start | bytes 110596
  0.8 114.0 %copy-start.10 = (f32[36,256]{1,0:T(8,128)S(1)}, f32[36,256]{1,0:T(8,128)}, u32[]{:S(2)}) copy-start(f32[36,256]{1,0:T(8,128)} %refs_10_.1) | copy-start | bytes 110596
  0.8 114.0 %copy-start.11 = (f32[36,256]{1,0:T(8,128)S(1)}, f32[36,256]{1,0:T(8,128)}, u32[]{:S(2)}) copy-start(f32[36,256]{1,0:T(8,128)} %refs_11_.1) | copy-start | bytes 110596
  0.8 114.0 %copy-start.12 = (f32[4,256]{1,0:T(4,128)S(1)}, f32[4,256]{1,0:T(4,128)}, u32[]{:S(2)}) copy-start(f32[4,256]{1,0:T(4,128)} %refs_18_.1) | copy-start | bytes 12292
  0.8 114.0 %copy-start.13 = (f32[2,512]{1,0:T(2,128)S(1)}, f32[2,512]{1,0:T(2,128)}, u32[]{:S(2)}) copy-start(f32[2,512]{1,0:T(2,128)} %refs_23_.1) | copy-start | bytes 12292
  0.8 114.0 %copy-start.14 = (f32[4,256]{1,0:T(4,128)S(1)}, f32[4,256]{1,0:T(4,128)}, u32[]{:S(2)}) copy-start(f32[4,256]{1,0:T(4,128)} %refs_19_.1) | copy-start | bytes 12292
  0.8 114.0 %copy-start.15 = (f32[4,256]{1,0:T(4,128)S(1)}, f32[4,256]{1,0:T(4,128)}, u32[]{:S(2)}) copy-start(f32[4,256]{1,0:T(4,128)} %refs_20_.1) | copy-start | bytes 12292
  0.8 114.0 %copy-start.16 = (f32[4,256]{1,0:T(4,128)S(1)}, f32[4,256]{1,0:T(4,128)}, u32[]{:S(2)}) copy-start(f32[4,256]{1,0:T(4,128)} %refs_21_.1) | copy-start | bytes 12292
  0.8 114.0 %copy-start.17 = (f32[2,512]{1,0:T(2,128)S(1)}, f32[2,512]{1,0:T(2,128)}, u32[]{:S(2)}) copy-start(f32[2,512]{1,0:T(2,128)} %refs_24_.1) | copy-start | bytes 12292
  0.9 114.0 %copy-start.18 = (f32[2,512]{1,0:T(2,128)S(1)}, f32[2,512]{1,0:T(2,128)}, u32[]{:S(2)}) copy-start(f32[2,512]{1,0:T(2,128)} %refs_25_.1) | copy-start | bytes 12292
  0.9 114.0 %copy-start.19 = (f32[2,512]{1,0:T(2,128)S(1)}, f32[2,512]{1,0:T(2,128)}, u32[]{:S(2)}) copy-start(f32[2,512]{1,0:T(2,128)} %refs_26_.1) | copy-start | bytes 12292

commit v6 on v5

--- a/solution.py
+++ b/solution.py
@@ -440,7 +440,7 @@
         sums.append(lax.fori_loop(0, W, body, (zero, zero)))
     r["tx"][...] = third[1 - xp].astype(BF)
     position = xp * HD + owner
-    both = family + twin_family
+    both = twin_family + family
     stat3 = statistics(
         r["st3"],
         position,
@@ -850,6 +850,8 @@
         part = ball.at[rows(h), mids(cx)]
         ball_far.append(send(part, part, core_peer))
 
+    if own_gather:
+        rest_early()
     b1t = r["b1t"]
     b1t[...] = b1[...].T
     if own_gather:
@@ -857,9 +859,9 @@
         here, there = z - parity, lax.rem(z - parity + 2, 4)
         ends = (there + 1 - parity, there + parity, here + 1 - parity, z)
         halves = [(2 * slot + part, zi) for slot, zi in enumerate(ends) for part in range(2)]
-        s_reduce.start(halves)
-        rest_early()
+        s_reduce.start(halves[:4])
         rest_late = s_expand.fold(2, zones[1])
+        s_reduce.start(halves[4:])
         s_group.middle(around)
         for half in halves[0:2]:
             s_reduce.to_near(*half)

time: 118 us -> 116 us (0.983)
    pallas_call x1, Pallas kernels: 114 us -> 112 us  [local(): pl.pallas_call(functools.partial(block_kernel, names, dims), out_shape=[p...]
where the time goes in v6:
time: 116 us
  Pallas kernels  115 us (99%)
  between operations  1.16 us (1%)
    pallas_call x1, Pallas kernels, local(): pl.pallas_call(functools.partial(block_kernel, names, dims), out_shape=[p...  112 us
    pallas_call x1, Pallas kernels, local(): pl.pallas_call(last_kernel, out_shape=shapes, in_specs=[whole] * len(flat...  2.69 us

profile of v6, /device:TPU:2, one launch (start us, length us, event | category | flops | bytes accessed | tf_op | source)
XLA Modules:
  0.0 116.0 jit_solution(3045983517695050123)
XLA Ops:
  0.7 0.0 copy-start
  0.7 0.0 copy-start.1
  0.7 0.0 copy-start.2
  0.7 0.0 copy-start.3
  0.7 0.0 copy-start.4
  0.7 0.0 copy-start.5
  0.7 0.0 copy-start.6
  0.7 0.0 copy-start.7
  0.8 0.0 copy-start.8
  0.8 0.0 copy-start.9
  0.8 0.0 copy-start.10
  0.8 0.0 copy-start.11
  0.8 0.0 copy-start.12
  0.8 0.0 copy-start.13
  0.8 0.0 copy-start.14
  0.8 0.0 copy-start.15
  0.8 0.0 copy-start.16
  0.8 0.0 copy-start.17
  0.9 0.0 copy-start.18
  0.9 0.0 copy-start.19
  0.9 112.1 %block.1 = (bf16[48,7,2,512]{3,2,1,0:T(2,128)(2,1)S(1)}, f32[672,512]{1,0:T(8,128)S(1)}, f32[4,256]{1,0:T(4,128)S(1)}, f32[2,512]{1,0:T(2,128)S(1)}, f32[256,256...) custom-call(bf16[48,7,2,2048]{3,2,1,0:T(2,128)(2,1)} %bitcast.6, bf16[48,7,2,512]{3,2,1,0:T(2,128)(2,1)} %bitcast.7, ...), custom_call_target="tpu_custom_call" | custom-call | tf_op jit(solution)/shard_map/block/pallas_call | solution.py:1066
  112.9 0.0 copy-done
  112.9 0.0 copy-done.1
  113.0 0.0 copy-done.2
  113.0 0.0 copy-done.3
  113.0 0.0 copy-done.4
  113.0 0.0 copy-done.5
  113.0 0.0 copy-done.6
  113.0 0.0 copy-done.7
  113.0 0.0 copy-done.8
  113.0 0.0 copy-done.9
  113.1 2.7 %adamw.1 = (bf16[48,7,2,512]{3,2,1,0:T(2,128)(2,1)}, f32[48,7,2,512]{3,2,1,0:T(2,128)}, f32[256,256]{1,0:T(8,128)}, f32[256,256]{1,0:T(8,128)}, f32[256,256]{1,0...) custom-call(f32[2,7,48,512]{3,2,1,0:T(8,128)S(1)} %bitcast.5, ...), custom_call_target="tpu_custom_call" | custom-call | tf_op jit(solution)/shard_map/adamw/pallas_call | solution.py:1105
  (10 shorter events, 0.0 us)
Async XLA Ops:
  0.7 112.3 %copy-start = (f32[256,256]{1,0:T(8,128)S(1)}, f32[256,256]{1,0:T(8,128)}, u32[]{:S(2)}) copy-start(f32[256,256]{1,0:T(8,128)} %refs_13_.1) | copy-start | bytes 786436
  0.7 112.3 %copy-start.1 = (f32[256,256]{1,0:T(8,128)S(1)}, f32[256,256]{1,0:T(8,128)}, u32[]{:S(2)}) copy-start(f32[256,256]{1,0:T(8,128)} %refs_3_.3) | copy-start | bytes 786436
  0.7 112.3 %copy-start.2 = (f32[256,256]{1,0:T(8,128)S(1)}, f32[256,256]{1,0:T(8,128)}, u32[]{:S(2)}) copy-start(f32[256,256]{1,0:T(8,128)} %refs_4_.3) | copy-start | bytes 786436
  0.7 112.3 %copy-start.3 = (f32[256,256]{1,0:T(8,128)S(1)}, f32[256,256]{1,0:T(8,128)}, u32[]{:S(2)}) copy-start(f32[256,256]{1,0:T(8,128)} %refs_5_.3) | copy-start | bytes 786436
  0.7 112.3 %copy-start.4 = (f32[256,256]{1,0:T(8,128)S(1)}, f32[256,256]{1,0:T(8,128)}, u32[]{:S(2)}) copy-start(f32[256,256]{1,0:T(8,128)} %refs_6_.3) | copy-start | bytes 786436
  0.7 112.3 %copy-start.5 = (f32[256,256]{1,0:T(8,128)S(1)}, f32[256,256]{1,0:T(8,128)}, u32[]{:S(2)}) copy-start(f32[256,256]{1,0:T(8,128)} %refs_14_.1) | copy-start | bytes 786436
  0.7 112.3 %copy-start.6 = (f32[256,256]{1,0:T(8,128)S(1)}, f32[256,256]{1,0:T(8,128)}, u32[]{:S(2)}) copy-start(f32[256,256]{1,0:T(8,128)} %refs_15_.1) | copy-start | bytes 786436
  0.7 112.3 %copy-start.7 = (f32[256,256]{1,0:T(8,128)S(1)}, f32[256,256]{1,0:T(8,128)}, u32[]{:S(2)}) copy-start(f32[256,256]{1,0:T(8,128)} %refs_16_.1) | copy-start | bytes 786436
  0.8 112.3 %copy-start.8 = (f32[36,256]{1,0:T(8,128)S(1)}, f32[36,256]{1,0:T(8,128)}, u32[]{:S(2)}) copy-start(f32[36,256]{1,0:T(8,128)} %refs_8_.1) | copy-start | bytes 110596
  0.8 112.3 %copy-start.9 = (f32[36,256]{1,0:T(8,128)S(1)}, f32[36,256]{1,0:T(8,128)}, u32[]{:S(2)}) copy-start(f32[36,256]{1,0:T(8,128)} %refs_9_.1) | copy-start | bytes 110596
  0.8 112.3 %copy-start.10 = (f32[36,256]{1,0:T(8,128)S(1)}, f32[36,256]{1,0:T(8,128)}, u32[]{:S(2)}) copy-start(f32[36,256]{1,0:T(8,128)} %refs_10_.1) | copy-start | bytes 110596
  0.8 112.3 %copy-start.11 = (f32[36,256]{1,0:T(8,128)S(1)}, f32[36,256]{1,0:T(8,128)}, u32[]{:S(2)}) copy-start(f32[36,256]{1,0:T(8,128)} %refs_11_.1) | copy-start | bytes 110596
  0.8 112.3 %copy-start.12 = (f32[4,256]{1,0:T(4,128)S(1)}, f32[4,256]{1,0:T(4,128)}, u32[]{:S(2)}) copy-start(f32[4,256]{1,0:T(4,128)} %refs_18_.1) | copy-start | bytes 12292
  0.8 112.3 %copy-start.13 = (f32[2,512]{1,0:T(2,128)S(1)}, f32[2,512]{1,0:T(2,128)}, u32[]{:S(2)}) copy-start(f32[2,512]{1,0:T(2,128)} %refs_23_.1) | copy-start | bytes 12292
  0.8 112.3 %copy-start.14 = (f32[4,256]{1,0:T(4,128)S(1)}, f32[4,256]{1,0:T(4,128)}, u32[]{:S(2)}) copy-start(f32[4,256]{1,0:T(4,128)} %refs_19_.1) | copy-start | bytes 12292
  0.8 112.3 %copy-start.15 = (f32[4,256]{1,0:T(4,128)S(1)}, f32[4,256]{1,0:T(4,128)}, u32[]{:S(2)}) copy-start(f32[4,256]{1,0:T(4,128)} %refs_20_.1) | copy-start | bytes 12292
  0.8 112.3 %copy-start.16 = (f32[4,256]{1,0:T(4,128)S(1)}, f32[4,256]{1,0:T(4,128)}, u32[]{:S(2)}) copy-start(f32[4,256]{1,0:T(4,128)} %refs_21_.1) | copy-start | bytes 12292
  0.8 112.3 %copy-start.17 = (f32[2,512]{1,0:T(2,128)S(1)}, f32[2,512]{1,0:T(2,128)}, u32[]{:S(2)}) copy-start(f32[2,512]{1,0:T(2,128)} %refs_24_.1) | copy-start | bytes 12292
  0.9 112.3 %copy-start.18 = (f32[2,512]{1,0:T(2,128)S(1)}, f32[2,512]{1,0:T(2,128)}, u32[]{:S(2)}) copy-start(f32[2,512]{1,0:T(2,128)} %refs_25_.1) | copy-start | bytes 12292
  0.9 112.3 %copy-start.19 = (f32[2,512]{1,0:T(2,128)S(1)}, f32[2,512]{1,0:T(2,128)}, u32[]{:S(2)}) copy-start(f32[2,512]{1,0:T(2,128)} %refs_26_.1) | copy-start | bytes 12292

commit v7 on v6

--- a/solution.py
+++ b/solution.py
@@ -572,8 +572,6 @@
     ag_in = send(r["agsend"], r["agrecv"], x_peer)
     part = piece.at[rows(xp), quarter(xp, k)]
     piece_in = send(part, part, x_peer)
-    for n in range(1, 4):
-        send_wrq(n)
     agrad[rows(xp), :] = dot_nt(piece[rows(xp), :], we[...])
     tx_in[1].wait_recv()
     outer_norm(xp, 1 - xp, *other_row, cut, W)
@@ -744,6 +742,8 @@
     lax.fori_loop(0, W, turn, 0)
     if own_gather:
         rest_early = s_expand.fold(0, zones[0])
+    for n in range(1, 4):
+        send_wrq(n)
     total2 = total(r["st2b"], stat2b)
     b2n = r["b2n"]
 

time: 116 us -> 116 us (level)
  no operation moved by 1% of the time
where the time goes in v7:
time: 116 us
  Pallas kernels  115 us (99%)
  between operations  1.16 us (1%)
    pallas_call x1, Pallas kernels, local(): pl.pallas_call(functools.partial(block_kernel, names, dims), out_shape=[p...  112 us
    pallas_call x1, Pallas kernels, local(): pl.pallas_call(last_kernel, out_shape=shapes, in_specs=[whole] * len(flat...  2.69 us

profile of v7, /device:TPU:2, one launch (start us, length us, event | category | flops | bytes accessed | tf_op | source)
XLA Modules:
  0.0 116.0 jit_solution(6915851569074928592)
XLA Ops:
  0.7 0.0 copy-start
  0.7 0.0 copy-start.1
  0.7 0.0 copy-start.2
  0.7 0.0 copy-start.3
  0.7 0.0 copy-start.4
  0.7 0.0 copy-start.5
  0.7 0.0 copy-start.6
  0.7 0.0 copy-start.7
  0.8 0.0 copy-start.8
  0.8 0.0 copy-start.9
  0.8 0.0 copy-start.10
  0.8 0.0 copy-start.11
  0.8 0.0 copy-start.12
  0.8 0.0 copy-start.13
  0.8 0.0 copy-start.14
  0.8 0.0 copy-start.15
  0.8 0.0 copy-start.16
  0.8 0.0 copy-start.17
  0.9 0.0 copy-start.18
  0.9 0.0 copy-start.19
  0.9 112.1 %block.1 = (bf16[48,7,2,512]{3,2,1,0:T(2,128)(2,1)S(1)}, f32[672,512]{1,0:T(8,128)S(1)}, f32[4,256]{1,0:T(4,128)S(1)}, f32[2,512]{1,0:T(2,128)S(1)}, f32[256,256...) custom-call(bf16[48,7,2,2048]{3,2,1,0:T(2,128)(2,1)} %bitcast.6, bf16[48,7,2,512]{3,2,1,0:T(2,128)(2,1)} %bitcast.7, ...), custom_call_target="tpu_custom_call" | custom-call | tf_op jit(solution)/shard_map/block/pallas_call | solution.py:1066
  113.0 0.0 copy-done
  113.0 0.0 copy-done.1
  113.0 0.0 copy-done.2
  113.0 0.0 copy-done.3
  113.0 0.0 copy-done.4
  113.0 0.0 copy-done.5
  113.0 0.0 copy-done.6
  113.0 0.0 copy-done.7
  113.0 0.0 copy-done.8
  113.0 0.0 copy-done.9
  113.2 2.7 %adamw.1 = (bf16[48,7,2,512]{3,2,1,0:T(2,128)(2,1)}, f32[48,7,2,512]{3,2,1,0:T(2,128)}, f32[256,256]{1,0:T(8,128)}, f32[256,256]{1,0:T(8,128)}, f32[256,256]{1,0...) custom-call(f32[2,7,48,512]{3,2,1,0:T(8,128)S(1)} %bitcast.5, ...), custom_call_target="tpu_custom_call" | custom-call | tf_op jit(solution)/shard_map/adamw/pallas_call | solution.py:1105
  (10 shorter events, 0.0 us)
Async XLA Ops:
  0.7 112.3 %copy-start = (f32[256,256]{1,0:T(8,128)S(1)}, f32[256,256]{1,0:T(8,128)}, u32[]{:S(2)}) copy-start(f32[256,256]{1,0:T(8,128)} %refs_13_.1) | copy-start | bytes 786436
  0.7 112.3 %copy-start.1 = (f32[256,256]{1,0:T(8,128)S(1)}, f32[256,256]{1,0:T(8,128)}, u32[]{:S(2)}) copy-start(f32[256,256]{1,0:T(8,128)} %refs_3_.3) | copy-start | bytes 786436
  0.7 112.3 %copy-start.2 = (f32[256,256]{1,0:T(8,128)S(1)}, f32[256,256]{1,0:T(8,128)}, u32[]{:S(2)}) copy-start(f32[256,256]{1,0:T(8,128)} %refs_4_.3) | copy-start | bytes 786436
  0.7 112.3 %copy-start.3 = (f32[256,256]{1,0:T(8,128)S(1)}, f32[256,256]{1,0:T(8,128)}, u32[]{:S(2)}) copy-start(f32[256,256]{1,0:T(8,128)} %refs_5_.3) | copy-start | bytes 786436
  0.7 112.3 %copy-start.4 = (f32[256,256]{1,0:T(8,128)S(1)}, f32[256,256]{1,0:T(8,128)}, u32[]{:S(2)}) copy-start(f32[256,256]{1,0:T(8,128)} %refs_6_.3) | copy-start | bytes 786436
  0.7 112.3 %copy-start.5 = (f32[256,256]{1,0:T(8,128)S(1)}, f32[256,256]{1,0:T(8,128)}, u32[]{:S(2)}) copy-start(f32[256,256]{1,0:T(8,128)} %refs_14_.1) | copy-start | bytes 786436
  0.7 112.3 %copy-start.6 = (f32[256,256]{1,0:T(8,128)S(1)}, f32[256,256]{1,0:T(8,128)}, u32[]{:S(2)}) copy-start(f32[256,256]{1,0:T(8,128)} %refs_15_.1) | copy-start | bytes 786436
  0.7 112.3 %copy-start.7 = (f32[256,256]{1,0:T(8,128)S(1)}, f32[256,256]{1,0:T(8,128)}, u32[]{:S(2)}) copy-start(f32[256,256]{1,0:T(8,128)} %refs_16_.1) | copy-start | bytes 786436
  0.8 112.3 %copy-start.8 = (f32[36,256]{1,0:T(8,128)S(1)}, f32[36,256]{1,0:T(8,128)}, u32[]{:S(2)}) copy-start(f32[36,256]{1,0:T(8,128)} %refs_8_.1) | copy-start | bytes 110596
  0.8 112.3 %copy-start.9 = (f32[36,256]{1,0:T(8,128)S(1)}, f32[36,256]{1,0:T(8,128)}, u32[]{:S(2)}) copy-start(f32[36,256]{1,0:T(8,128)} %refs_9_.1) | copy-start | bytes 110596
  0.8 112.3 %copy-start.10 = (f32[36,256]{1,0:T(8,128)S(1)}, f32[36,256]{1,0:T(8,128)}, u32[]{:S(2)}) copy-start(f32[36,256]{1,0:T(8,128)} %refs_10_.1) | copy-start | bytes 110596
  0.8 112.3 %copy-start.11 = (f32[36,256]{1,0:T(8,128)S(1)}, f32[36,256]{1,0:T(8,128)}, u32[]{:S(2)}) copy-start(f32[36,256]{1,0:T(8,128)} %refs_11_.1) | copy-start | bytes 110596
  0.8 112.3 %copy-start.12 = (f32[4,256]{1,0:T(4,128)S(1)}, f32[4,256]{1,0:T(4,128)}, u32[]{:S(2)}) copy-start(f32[4,256]{1,0:T(4,128)} %refs_18_.1) | copy-start | bytes 12292
  0.8 112.3 %copy-start.13 = (f32[2,512]{1,0:T(2,128)S(1)}, f32[2,512]{1,0:T(2,128)}, u32[]{:S(2)}) copy-start(f32[2,512]{1,0:T(2,128)} %refs_23_.1) | copy-start | bytes 12292
  0.8 112.3 %copy-start.14 = (f32[4,256]{1,0:T(4,128)S(1)}, f32[4,256]{1,0:T(4,128)}, u32[]{:S(2)}) copy-start(f32[4,256]{1,0:T(4,128)} %refs_19_.1) | copy-start | bytes 12292
  0.8 112.3 %copy-start.15 = (f32[4,256]{1,0:T(4,128)S(1)}, f32[4,256]{1,0:T(4,128)}, u32[]{:S(2)}) copy-start(f32[4,256]{1,0:T(4,128)} %refs_20_.1) | copy-start | bytes 12292
  0.8 112.3 %copy-start.16 = (f32[4,256]{1,0:T(4,128)S(1)}, f32[4,256]{1,0:T(4,128)}, u32[]{:S(2)}) copy-start(f32[4,256]{1,0:T(4,128)} %refs_21_.1) | copy-start | bytes 12292
  0.8 112.3 %copy-start.17 = (f32[2,512]{1,0:T(2,128)S(1)}, f32[2,512]{1,0:T(2,128)}, u32[]{:S(2)}) copy-start(f32[2,512]{1,0:T(2,128)} %refs_24_.1) | copy-start | bytes 12292
  0.9 112.3 %copy-start.18 = (f32[2,512]{1,0:T(2,128)S(1)}, f32[2,512]{1,0:T(2,128)}, u32[]{:S(2)}) copy-start(f32[2,512]{1,0:T(2,128)} %refs_25_.1) | copy-start | bytes 12292
  0.9 112.3 %copy-start.19 = (f32[2,512]{1,0:T(2,128)S(1)}, f32[2,512]{1,0:T(2,128)}, u32[]{:S(2)}) copy-start(f32[2,512]{1,0:T(2,128)} %refs_26_.1) | copy-start | bytes 12292
